TPU v7x, 32 devices: a whole 2x2x4 slice. The times are simulated.
32 devices in a mesh: dp: 4 (over y, x), mp: 8 (over z, core).
Axes of the slice: x: 2, y: 2, z: 4, core: 2. Of those that a mesh axis runs over, the one named last changes fastest.
Arguments:
- hidden_rows: bfloat16 [256, 16384], P('dp', 'mp'), may hold values from -60 to 60
- head_weight: bfloat16 [16384, 8, 4, 512], P('mp', None, 'dp'), may hold values from -0.046875 to 0.046875
- norm_gain: float32 [8, 4, 512], P('mp', 'dp'), may hold values from 0.1 to 1.9
- vocab_embed: bfloat16 [32768, 8, 4, 512], P('mp', None, 'dp'), may hold values from -6 to 6
- targets: int32 [256], replicated, may hold values from 0 to 32767
Outputs:
- weight_grad: bfloat16 [16384, 8, 4, 512], P('mp', None, 'dp')
- loss: float32 [], replicated
All inputs are finite; a program needn't handle non-finite values.
Results may differ from a plain program's by a relative error of at most 0.0046.
Values may be sent and summed in bfloat16 or wider, within the bound.
No kernel may reach another device: no remote copies, remote signals or barrier semaphores. Data moves between devices by JAX's collectives and lax.ppermute only.
A program may use at most 192 MiB of HBM per device.

v0:
```python
import jax
import jax.numpy as jnp
from jax import lax
from jax.sharding import PartitionSpec as P


def on_device(hidden_rows, head_weight, norm_gain, vocab_embed, targets):
    tok_dp, width_mp = hidden_rows.shape
    n_mp = lax.axis_size("mp")
    block = head_weight.shape[3]
    width = width_mp * n_mp
    vocab_mp = vocab_embed.shape[0]
    dp_index = lax.axis_index("dp")
    mp_index = lax.axis_index("mp")
    contract = (((0,), (1,)), ((), ()))
    gathered = lax.all_gather(hidden_rows, "dp", axis=0, tiled=True)
    tokens_all = gathered.shape[0]
    weight_flat = head_weight.reshape(width_mp, n_mp * block)
    columns = weight_flat
    pre = lax.psum_scatter(
        lax.dot_general(columns, gathered, contract, preferred_element_type=jnp.float32),
        "mp",
        scatter_dimension=0,
        tiled=True,
    )
    own_rows = lax.dynamic_slice_in_dim(gathered, dp_index * block, block, 1).astype(jnp.float32).T
    act = own_rows + jax.nn.silu(pre)
    squares = lax.psum(jnp.sum(act * act, axis=0), ("dp", "mp"))
    inv = lax.rsqrt(squares / width + 1e-05)
    gain = norm_gain.reshape(block, 1)
    normed = (act * inv[None, :] * gain).astype(jnp.bfloat16)
    full_normed = lax.all_gather(normed, "mp", axis=0, tiled=True)
    embed_flat = vocab_embed.reshape(vocab_mp, n_mp * block)
    columns = full_normed
    logits = lax.psum_scatter(
        lax.dot_general(columns, embed_flat, contract, preferred_element_type=jnp.float32),
        "dp",
        scatter_dimension=0,
        tiled=True,
    )
    row_targets = lax.dynamic_slice_in_dim(targets, dp_index * tok_dp, tok_dp, 0)
    local_ids = row_targets - mp_index * vocab_mp
    hit = lax.broadcasted_iota(jnp.int32, logits.shape, 1) == local_ids[:, None]
    picked_here = jnp.sum(jnp.where(hit, logits, 0.0), axis=1)
    local_max = jnp.max(logits, axis=1)
    top = lax.pmax(local_max, "mp")
    total, picked = lax.psum((jnp.sum(jnp.exp(logits - top[:, None]), axis=1), picked_here), "mp")
    lse = top + jnp.log(total)
    dlogits = ((jnp.exp(logits - lse[:, None]) - hit.astype(jnp.float32)) / tokens_all).astype(
        jnp.bfloat16
    )
    loss = lax.psum(jnp.sum(lse - picked), "dp") / tokens_all
    all_dlogits = lax.all_gather(dlogits, "dp", axis=0, tiled=True)
    columns = embed_flat
    dnormed = lax.psum_scatter(
        lax.dot_general(columns, all_dlogits, contract, preferred_element_type=jnp.float32),
        "mp",
        scatter_dimension=0,
        tiled=True,
    )
    scaled = gain * dnormed
    inner = lax.psum(jnp.sum(act * scaled, axis=0), ("dp", "mp")) / width
    dact = inv[None, :] * scaled - act * (inv * inv * inv * inner)[None, :]
    sigma = jax.nn.sigmoid(pre)
    dpre = (dact * sigma * (1.0 + pre * (1.0 - sigma))).astype(jnp.bfloat16)
    all_dpre = lax.all_gather(dpre, "mp", axis=0, tiled=True)
    grad = lax.dot_general(
        gathered, all_dpre, (((0,), (1,)), ((), ())), preferred_element_type=jnp.float32
    )
    return (grad.astype(jnp.bfloat16).reshape(head_weight.shape), loss)


def solution(mesh):
    return jax.shard_map(
        on_device,
        mesh=mesh,
        in_specs=(
            P("dp", "mp"),
            P("mp", None, "dp", None),
            P("mp", "dp", None),
            P("mp", None, "dp", None),
            P(),
        ),
        out_specs=(P("mp", None, "dp", None), P()),
        check_vma=False,
    )
```

profile of v0, /device:TPU:1, one launch (start us, length us, event | category | flops | bytes accessed | tf_op | source)
XLA Modules:
  0.0 494.3 jit_solution(8738022293041205566)
XLA Ops:
  7.2 0.7 all-gather.5.cloned.1.call-update
  7.9 16.8 %copy.15 = bf16[256,8,8,512]{3,1,2,0:T(8,128)(2,1)} copy(bf16[256,8,8,512]{3,2,1,0:T(8,128)(2,1)} %bitcast.36) | data formatting | bytes 33554432
  24.7 13.9 %all-gather.5.cloned.1.call-done = bf16[256,2048]{1,0:T(8,128)(2,1)} async-done(((bf16[64,2048]{1,0:T(8,128)(2,1)}), bf16[256,2048]{1,0:T(8,128)(2,1)}) %all-gather.5.cloned.1.call-update) | async-done | bytes 1048592 | tf_op jit(solution)/shard_map/all_gather | solution.py:16
  38.6 12.8 %fusion.1 = f32[4096,256]{1,0:T(8,128)} fusion(bf16[2048,4096]{1,0:T(8,128)(2,1)} %bitcast.37, bf16[256,2048]{1,0:T(8,128)(2,1)} %all-gather.5.cloned.1.call-done), kind=kOutput, calls=%fused_computation.19 | convolution fusion | flops 4294967296 | bytes 22020096 | tf_op jit(solution)/shard_map/dot_general | solution.py:21
  51.5 1.1 copy-done.1
  52.7 0.1 copy.14
  52.8 46.7 %reduce-scatter.4.cloned.1.call-done = f32[512,256]{1,0:T(8,128)} async-done(((f32[4096,256]{1,0:T(8,128)}), f32[512,256]{1,0:T(8,128)}) %reduce-scatter.4.cloned.1.call-update) | async-done | bytes 524304 | tf_op jit(solution)/shard_map/reduce_scatter | solution.py:20
  99.5 1.2 multiply_reduce_fusion.1
  100.7 39.1 %psum.35 = f32[256]{0:T(256)S(1)} all-reduce(f32[256]{0:T(256)S(1)} %multiply_reduce_fusion.1), channel_id=1, replica_groups=mesh['dp'=4,'mp'=8] {'dp','mp'}, use_global_device_ids=true, to_apply=%region_2.3 | all-reduce | flops 256 | bytes 2048 | tf_op jit(solution)/shard_map/psum | solution.py:28
  139.8 1.9 multiply_convert_fusion.2
  141.8 0.2 reduce-scatter.6.cloned.1.call-start
  142.0 22.8 %copy.16 = bf16[512,8,8,512]{3,1,2,0:T(8,128)(2,1)} copy(bf16[512,8,8,512]{3,2,1,0:T(8,128)(2,1)} %bitcast.33) | data formatting | bytes 67108864
  164.8 7.9 %all-gather.7.cloned.1.call-done = bf16[4096,256]{1,0:T(8,128)(2,1)} async-done(((bf16[512,256]{1,0:T(8,128)(2,1)}), bf16[4096,256]{1,0:T(8,128)(2,1)}) %all-gather.7.cloned.1.call-update) | async-done | bytes 2097168 | tf_op jit(solution)/shard_map/all_gather | solution.py:32
  172.7 17.4 %fusion.2 = f32[256,4096]{1,0:T(8,128)} fusion(bf16[4096,256]{1,0:T(8,128)(2,1)} %all-gather.7.cloned.1.call-done, bf16[4096,4096]{1,0:T(8,128)(2,1)} %bitcast.34), kind=kOutput, calls=%fused_computation.20 | convolution fusion | flops 8589934592 | bytes 39845888 | tf_op jit(solution)/shard_map/dot_general | solution.py:36
  190.2 0.6 copy-done.3
  190.9 51.2 %reduce-scatter.6.cloned.1.call-done = f32[64,4096]{1,0:T(8,128)} async-done(((f32[256,4096]{1,0:T(8,128)}), f32[64,4096]{1,0:T(8,128)}) %reduce-scatter.6.cloned.1.call-update) | async-done | bytes 1048592 | tf_op jit(solution)/shard_map/reduce_scatter | solution.py:35
  242.1 1.4 reduce_max.9
  243.5 13.6 %pmax.7 = f32[64]{0:T(128)S(1)} all-reduce(f32[64]{0:T(128)S(1)} %reduce_max.9), channel_id=1, replica_groups=mesh['dp'=4,'mp'=8] {'mp'}, use_global_device_ids=true, to_apply=%region_5.6 | all-reduce | flops 64 | bytes 512 | tf_op jit(solution)/shard_map/pmax | solution.py:46
  257.1 1.6 select_reduce_fusion
  258.8 16.4 %all-reduce = (f32[64]{0:T(128)S(1)}, f32[64]{0:T(128)S(1)}) all-reduce(f32[64]{0:T(128)S(1)} %get-tuple-element.7, f32[64]{0:T(128)S(1)} %get-tuple-element.6), channel_id=1, replica_groups=mesh['dp'=4,'mp'=8] {'mp'}, use_global_device_ids=true, to_apply=%region_7.8 | all-reduce | flops 128 | bytes 1024 | tf_op jit(solution)/shard_map/psum | solution.py:47
  275.1 0.6 subtract_reduce_fusion
  275.8 2.3 multiply_convert_fusion
  278.2 32.6 %all-gather.9.cloned.1.call-done = bf16[256,4096]{1,0:T(8,128)(2,1)} async-done(((bf16[64,4096]{1,0:T(8,128)(2,1)}), bf16[256,4096]{1,0:T(8,128)(2,1)}) %all-gather.9.cloned.1.call-update) | async-done | bytes 2097168 | tf_op jit(solution)/shard_map/all_gather | solution.py:53
  310.8 19.8 %convolution_bitcast_fusion = f32[4096,256]{1,0:T(8,128)} fusion(bf16[256,4096]{1,0:T(8,128)(2,1)} %all-gather.9.cloned.1.call-done, bf16[4096,4096]{1,0:T(8,128)(2,1)} %bitcast.35), kind=kOutput, calls=%fused_computation.1 | convolution fusion | flops 8589934592 | bytes 39845888 | tf_op jit(solution)/shard_map/dot_general | solution.py:56
  330.6 48.0 %reduce-scatter.8.cloned.1.call-done = f32[512,256]{1,0:T(8,128)} async-done(((f32[4096,256]{1,0:T(8,128)}), f32[512,256]{1,0:T(8,128)}) %reduce-scatter.8.cloned.1.call-update) | async-done | bytes 524304 | tf_op jit(solution)/shard_map/reduce_scatter | solution.py:55
  378.5 1.3 multiply_reduce_fusion
  379.8 39.2 %psum.37 = f32[256]{0:T(256)S(1)} all-reduce(f32[256]{0:T(256)S(1)} %multiply_reduce_fusion), channel_id=1, replica_groups=mesh['dp'=4,'mp'=8] {'dp','mp'}, use_global_device_ids=true, to_apply=%region_10.11 | all-reduce | flops 256 | bytes 2048 | tf_op jit(solution)/shard_map/psum | solution.py:62
  419.0 2.1 multiply_convert_fusion.1
  421.1 8.6 %psum.39 = f32[]{:T(128)} all-reduce(f32[]{:T(128)} %get-tuple-element.10), channel_id=1, replica_groups=mesh['dp'=4,'mp'=8] {'dp'}, use_global_device_ids=true, to_apply=%region_14.15 | all-reduce | flops 1 | bytes 8 | tf_op jit(solution)/shard_map/psum | solution.py:52
  430.3 21.6 %all-gather.11.cloned.1.call-done = bf16[4096,256]{1,0:T(8,128)(2,1)} async-done(((bf16[512,256]{1,0:T(8,128)(2,1)}), bf16[4096,256]{1,0:T(8,128)(2,1)}) %all-gather.11.cloned.1.call-update) | async-done | bytes 2097168 | tf_op jit(solution)/shard_map/all_gather | solution.py:66
  452.0 9.7 %convolution_convert_fusion = bf16[4096,2048]{1,0:T(8,128)(2,1)} fusion(bf16[4096,256]{1,0:T(8,128)(2,1)} %all-gather.11.cloned.1.call-done, bf16[256,2048]{1,0:T(8,128)(2,1)S(1)} %copy-done.1), kind=kOutput, calls=%fused_computation | convolution fusion | flops 4303355904 | bytes 19922944 | tf_op jit(solution)/shard_map/dot_general | solution.py:67
  461.7 24.7 %copy.12 = bf16[2048,8,1,512]{3,1,2,0:T(8,128)(2,1)} copy(bf16[2048,8,1,512]{0,3,1,2:T(8,128)(2,1)} %bitcast.32) | data formatting | bytes 33554432
  (22 shorter events, 0.5 us)
Async XLA Ops:
  7.2 31.4 %all-gather.5.cloned.1.call-start = ((), (), s32[]{:S(2)}) async-start(), calls=%async_computation.3 | async-start | bytes 1310720 | tf_op jit(solution)/shard_map/all_gather | solution.py:16
  7.9 91.6 %reduce-scatter.4.cloned.1.call-start = ((), (), s32[]{:S(2)}) async-start(), calls=%async_computation.4 | async-start | bytes 4718592 | tf_op jit(solution)/shard_map/reduce_scatter | solution.py:20
  51.4 1.2 copy-start.1
  51.4 88.4 %copy-start.2 = (f32[1,1,512]{2,1,0:T(1,128)S(1)}, f32[1,1,512]{2,1,0:T(1,128)}, u32[]{:S(2)}) copy-start(f32[1,1,512]{2,1,0:T(1,128)} %param.7) | copy-start | bytes 6148
  51.4 121.3 %all-gather.7.cloned.1.call-start = ((), (), s32[]{:S(2)}) async-start(), calls=%async_computation.5 | async-start | bytes 2359296 | tf_op jit(solution)/shard_map/all_gather | solution.py:32
  141.8 100.3 %reduce-scatter.6.cloned.1.call-start = ((), (), s32[]{:S(2)}) async-start(), calls=%async_computation.6 | async-start | bytes 5242880 | tf_op jit(solution)/shard_map/reduce_scatter | solution.py:35
  190.1 0.7 copy-start.3
  190.2 120.6 %all-gather.9.cloned.1.call-start = ((), (), s32[]{:S(2)}) async-start(), calls=%async_computation.7 | async-start | bytes 2621440 | tf_op jit(solution)/shard_map/all_gather | solution.py:53
  278.1 100.4 %reduce-scatter.8.cloned.1.call-start = ((), (), s32[]{:S(2)}) async-start(), calls=%async_computation.8 | async-start | bytes 4718592 | tf_op jit(solution)/shard_map/reduce_scatter | solution.py:55
  330.5 48.0 %copy-start = (f32[512,256]{1,0:T(8,128)S(1)}, f32[512,256]{1,0:T(8,128)}, u32[]{:S(2)}) copy-start(f32[512,256]{1,0:T(8,128)} %reduce-scatter.4.cloned.1.call-done) | copy-start | bytes 1572868
  330.5 121.4 %all-gather.11.cloned.1.call-start = ((), (), s32[]{:S(2)}) async-start(), calls=%async_computation.9 | async-start | bytes 2359296 | tf_op jit(solution)/shard_map/all_gather | solution.py:66
Sparse Core Ops, SparseCore 0:
  9.8 28.6 all-gather.4
  51.6 47.8 reduce-scatter.3
  141.9 30.7 all-gather.6
  190.3 51.8 reduce-scatter.5
  278.2 32.4 all-gather.8
  330.7 47.8 reduce-scatter.7
  421.2 30.7 all-gather.10
where the time goes:
time: 496 us; the launch traced here: 494 us
  waiting for transfers between devices  223 us (45%)
  blocking collectives  117 us (24%)
  local copies, waits for them, and re-layouts  66.1 us (13%)
  matrix products  59.7 us (12%)
  between operations  16 us (3%)
  other arithmetic  12.5 us (3%)
    unnamed x12, local copies, waits for them, and re-layouts  66.1 us
    reduce_scatter x1, waiting for transfers between devices, on_device(): lax.psum_scatter(lax.dot_general(columns, embed_flat, contract, preferred...  51.2 us
    reduce_scatter x1, waiting for transfers between devices, on_device(): lax.psum_scatter(lax.dot_general(columns, all_dlogits, contract, preferre...  48 us
    reduce_scatter x1, waiting for transfers between devices, on_device(): lax.psum_scatter(lax.dot_general(columns, gathered, contract, preferred_e...  46.7 us
    psum x1, blocking collectives, on_device(): inner = lax.psum(jnp.sum(act * scaled, axis=0), ('dp', 'mp')) / width  39.2 us
    psum x1, blocking collectives, on_device(): squares = lax.psum(jnp.sum(act * act, axis=0), ('dp', 'mp'))  39.1 us
    all_gather x1, waiting for transfers between devices, on_device(): all_dlogits = lax.all_gather(dlogits, 'dp', axis=0, tiled=True)  32.6 us
    all_gather x1, waiting for transfers between devices, on_device(): all_dpre = lax.all_gather(dpre, 'mp', axis=0, tiled=True)  21.6 us
  transfers between devices with their start and end apart: 7, of which 7 were waited for; matrix products, arithmetic and copies ran while one was open for 8% of the time, Pallas kernels for 0%

commit v1 on v0

v1 whole, which is shorter than its diff:
```python
import functools

import jax
import jax.numpy as jnp
from jax import lax
from jax.experimental import pallas as pl
from jax.experimental.pallas import tpu as pltpu
from jax.sharding import PartitionSpec as P

F32 = jnp.float32
BF16 = jnp.bfloat16
LANES = 128


def params(mib):
    return pltpu.CompilerParams(vmem_limit_bytes=mib * 2**20)


def bits_of(n):
    bits = [1 << i for i in range(n.bit_length() - 1)]
    assert 1 << len(bits) == n
    return bits


def swap(value, axis, bit):
    n = lax.axis_size(axis)
    return lax.ppermute(value, axis, [(i, i ^ bit) for i in range(n)])


def gather_xor(value, axis, bits):
    held = {0: value}
    for bit in bits:
        for s in list(held):
            held[s | bit] = swap(held[s], axis, bit)
    return held


def scatter_xor(terms, axis, bits, dtype):
    done = 0
    for bit in bits:
        for s in sorted(terms, reverse=True):
            if s & bit and not s & done:
                total = functools.reduce(jnp.add, terms[s])
                terms[s ^ bit].append(swap(total.astype(dtype), axis, bit))
        done |= bit
    return terms[0]


def whole(shape):
    return pl.BlockSpec(shape, lambda *_: (0,) * len(shape))


def project_kernel(ks, lhs, w, out):
    out[0] = jnp.dot(lhs[...], w[0], preferred_element_type=F32).astype(out.dtype)


def project(lhs, w, ks, dtype):
    _, depth, block = w.shape
    rows = lhs.shape[0]
    count = ks.shape[0]
    return pl.pallas_call(
        project_kernel,
        out_shape=jax.ShapeDtypeStruct((count, rows, block), dtype),
        grid_spec=pltpu.PrefetchScalarGridSpec(
            num_scalar_prefetch=1,
            grid=(count,),
            in_specs=[whole(lhs.shape), pl.BlockSpec((1, depth, block), lambda i, ks: (ks[i], 0, 0))],
            out_specs=pl.BlockSpec((1, rows, block), lambda i, ks: (i, 0, 0)),
        ),
        compiler_params=params(32),
        cost_estimate=pl.CostEstimate(
            flops=2 * count * rows * depth * block, bytes_accessed=2 * count * depth * block, transcendentals=0
        ),
    )(ks, lhs, w)


def act_kernel(n, *refs):
    parts, (h, gain, pre, x, squares) = refs[:n], refs[n:]
    total = parts[0][...]
    for part in parts[1:]:
        total = total + part[...].astype(F32)
    pre[...] = total
    act = h[...].astype(F32) + total / (1.0 + jnp.exp(-total))
    x[...] = (act * gain[...]).astype(BF16)
    squares[...] = jnp.sum(act * act, axis=1, keepdims=True) + jnp.zeros(squares.shape, F32)


def activate(parts, h, gain):
    rows, block = h.shape
    return pl.pallas_call(
        functools.partial(act_kernel, len(parts)),
        out_shape=[
            jax.ShapeDtypeStruct((rows, block), F32),
            jax.ShapeDtypeStruct((rows, block), BF16),
            jax.ShapeDtypeStruct((rows, LANES), F32),
        ],
        compiler_params=params(32),
    )(*parts, h, gain)


def logits_kernel(order, n_out, me, *refs):
    xs, e, outs = refs[: len(order)], refs[len(order)], refs[len(order) + 1 :]
    total = 0.0
    for s, x in zip(order, xs):
        total = total + lax.dot_general(
            x[...], e[me[0] ^ s], (((1,), (1,)), ((), ())), preferred_element_type=F32
        )
    rows = total.shape[0] // n_out
    for i, out in enumerate(outs):
        out[...] = total[i * rows : (i + 1) * rows]


def project_vocab(xs, embed, me, n_out, start, size):
    n, _, block = embed.shape
    order = sorted(xs)
    rows = xs[0].shape[0]
    step = min(512, size)
    return pl.pallas_call(
        functools.partial(logits_kernel, order, n_out),
        out_shape=[jax.ShapeDtypeStruct((rows // n_out, size), F32)] * n_out,
        grid_spec=pltpu.PrefetchScalarGridSpec(
            num_scalar_prefetch=1,
            grid=(size // step,),
            in_specs=[whole((rows, block))] * n
            + [pl.BlockSpec((n, step, block), lambda i, me: (0, start // step + i, 0))],
            out_specs=[pl.BlockSpec((rows // n_out, step), lambda i, me: (0, i))] * n_out,
        ),
        compiler_params=params(40),
        cost_estimate=pl.CostEstimate(
            flops=2 * rows * size * n * block, bytes_accessed=2 * size * n * block, transcendentals=0
        ),
    )(me, *[xs[s] for s in order], embed)


def softmax_kernel(counts, width, *refs):
    parts, refs = refs[: sum(counts)], refs[sum(counts) :]
    squares, targets, refs = refs[0], refs[1], refs[2:]
    qs, stats = refs[:-1], refs[-1]
    inv = lax.rsqrt(squares[:, 0:1] / width + 1e-05)
    target = targets[:, 0:1]
    pieces, hits, at, first = [], [], 0, 0
    for count in counts:
        total = parts[at][...]
        for part in parts[at + 1 : at + count]:
            total = total + part[...]
        at += count
        total = total * inv
        ids = lax.broadcasted_iota(jnp.int32, total.shape, 1) + first
        first += total.shape[1]
        pieces.append(total)
        hits.append(ids == target)
    top = functools.reduce(jnp.maximum, [jnp.max(p, axis=1, keepdims=True) for p in pieces])
    mass, moment, picked = 0.0, 0.0, 0.0
    for piece, hit, q in zip(pieces, hits, qs):
        shifted = piece - top
        e = jnp.exp(shifted)
        mass = mass + jnp.sum(e, axis=1, keepdims=True)
        moment = moment + jnp.sum(e * shifted, axis=1, keepdims=True)
        picked = picked + jnp.sum(jnp.where(hit, piece, 0.0), axis=1, keepdims=True)
        q[...] = e.astype(BF16)
    lane = lax.broadcasted_iota(jnp.int32, stats.shape, 1)
    out = jnp.zeros(stats.shape, F32)
    for i, value in enumerate([top, mass, moment, picked]):
        out = jnp.where(lane == i, value, out)
    stats[...] = out


def softmax(pieces, squares, targets, width):
    counts = [len(p) for p in pieces]
    flat = [part for p in pieces for part in p]
    rows = flat[0].shape[0]
    return pl.pallas_call(
        functools.partial(softmax_kernel, counts, width),
        out_shape=[jax.ShapeDtypeStruct(p[0].shape, BF16) for p in pieces]
        + [jax.ShapeDtypeStruct((rows, LANES), F32)],
        compiler_params=params(32),
    )(*flat, squares, targets)


def tree(op, values):
    while len(values) > 1:
        half = len(values) // 2
        values = [op(a, b) for a, b in zip(values[:half], values[half:])]
    return values[0]


def merge_kernel(n, tokens, width, *refs):
    stats, (squares, targets, out) = refs[:n], refs[n:]
    tops = [st[:, 0:1] for st in stats]
    top = tree(jnp.maximum, tops)
    weights = [jnp.exp(t - top) for t in tops]
    mass = tree(jnp.add, [w * st[:, 1:2] for w, st in zip(weights, stats)])
    moment = tree(
        jnp.add, [w * (st[:, 2:3] + st[:, 1:2] * (t - top)) for w, t, st in zip(weights, tops, stats)]
    )
    picked = tree(jnp.add, [st[:, 3:4] for st in stats])
    lse = top + jnp.log(mass)
    inv = lax.rsqrt(squares[:, 0:1] / width + 1e-05)
    scale = jnp.exp(tops[0] - lse) / tokens
    at_target = (jnp.exp(picked - lse) - 1.0) / tokens
    pull = (moment / mass + (top - picked)) * (inv * inv) / (tokens * width)
    lane = lax.broadcasted_iota(jnp.int32, out.shape, 1)
    packed = jnp.zeros(out.shape, F32)
    values = [scale, at_target, targets[:, 0:1].astype(F32), inv, pull, lse - picked]
    for i, value in enumerate(values):
        packed = jnp.where(lane == i, value, packed)
    out[...] = packed


def merge(stats, squares, targets, tokens, width):
    return pl.pallas_call(
        functools.partial(merge_kernel, len(stats), tokens, width),
        out_shape=jax.ShapeDtypeStruct(stats[0].shape, F32),
        compiler_params=params(32),
    )(*stats, squares, targets)


def dnormed_kernel(n_blocks, n_pieces, ks, *refs):
    qs, refs = refs[: n_blocks * n_pieces], refs[n_blocks * n_pieces :]
    packs, (w, out, dlogits) = refs[:n_blocks], refs[n_blocks:]

    @pl.when(pl.program_id(0) == 0)
    def _():
        for b in range(n_blocks):
            scale, at_target = packs[b][:, 0:1], packs[b][:, 1:2]
            target = packs[b][:, 2:3].astype(jnp.int32)
            rows = scale.shape[0]
            first = 0
            for p in range(n_pieces):
                q = qs[b * n_pieces + p][...].astype(F32) * scale
                ids = lax.broadcasted_iota(jnp.int32, q.shape, 1) + first
                values = jnp.where(ids == target, at_target, q)
                dlogits[b * rows : (b + 1) * rows, first : first + q.shape[1]] = values.astype(BF16)
                first += q.shape[1]

    out[0] = jnp.dot(dlogits[...], w[0], preferred_element_type=F32).astype(out.dtype)


def project_back(qs, packs, w, ks, dtype):
    _, depth, block = w.shape
    n_blocks, n_pieces = len(qs), len(qs[0])
    flat = [q for row in qs for q in row]
    rows = n_blocks * packs[0].shape[0]
    count = ks.shape[0]
    return pl.pallas_call(
        functools.partial(dnormed_kernel, n_blocks, n_pieces),
        out_shape=jax.ShapeDtypeStruct((count, rows, block), dtype),
        grid_spec=pltpu.PrefetchScalarGridSpec(
            num_scalar_prefetch=1,
            grid=(count,),
            in_specs=[whole(q.shape) for q in flat]
            + [whole(p.shape) for p in packs]
            + [pl.BlockSpec((1, depth, block), lambda i, ks: (ks[i], 0, 0))],
            out_specs=pl.BlockSpec((1, rows, block), lambda i, ks: (i, 0, 0)),
            scratch_shapes=[pltpu.VMEM((rows, depth), BF16)],
        ),
        compiler_params=params(40),
        cost_estimate=pl.CostEstimate(
            flops=2 * count * rows * depth * block, bytes_accessed=2 * count * depth * block, transcendentals=0
        ),
    )(ks, *flat, *packs, w)


def dpre_kernel(n, n_blocks, *refs):
    parts, refs = refs[:n], refs[n:]
    packs, (pre, h, gain, out) = refs[:n_blocks], refs[n_blocks:]
    rows = packs[0].shape[0]
    for b in range(n_blocks):
        at = slice(b * rows, (b + 1) * rows)
        dnormed = parts[0][at, :]
        for part in parts[1:]:
            dnormed = dnormed + part[at, :].astype(F32)
        inv, pull = packs[b][:, 3:4], packs[b][:, 4:5]
        v = pre[at, :]
        sigma = 1.0 / (1.0 + jnp.exp(-v))
        act = h[at, :].astype(F32) + v * sigma
        dact = inv * gain[...] * dnormed - act * pull
        out[at, :] = (dact * sigma * (1.0 + v * (1.0 - sigma))).astype(BF16)


def grad_pre(parts, packs, pre, h, gain):
    return pl.pallas_call(
        functools.partial(dpre_kernel, len(parts), len(packs)),
        out_shape=jax.ShapeDtypeStruct(pre.shape, BF16),
        compiler_params=params(32),
    )(*parts, *packs, pre, h, gain)


def grad_kernel(order, me, h, *refs):
    n = len(order)
    ds, out, placed, mixed = refs[:n], refs[n], refs[n + 1], refs[n + 2]

    @pl.when(pl.program_id(0) == 0)
    def _():
        for s, d in zip(order, ds):
            placed[me[0] ^ s] = d[...]

    step = h.shape[1]
    for k in range(n):
        product = lax.dot_general(
            h[...], placed[k], (((0,), (0,)), ((), ())), preferred_element_type=F32
        )
        for j in range(mixed.shape[0]):
            mixed[j, pl.ds(k, step, stride=n), :] = product[:, j * LANES : (j + 1) * LANES]
    for j in range(mixed.shape[0]):
        out[:, j * LANES : (j + 1) * LANES] = mixed[j].astype(BF16)


def weight_grad(h, ds, me):
    rows, width = h.shape
    n = len(ds)
    block = ds[0].shape[1]
    order = sorted(ds)
    step = min(128, width)
    return pl.pallas_call(
        functools.partial(grad_kernel, order),
        out_shape=jax.ShapeDtypeStruct((width * n, block), BF16),
        grid_spec=pltpu.PrefetchScalarGridSpec(
            num_scalar_prefetch=1,
            grid=(width // step,),
            in_specs=[pl.BlockSpec((rows, step), lambda i, me: (0, i))] + [whole((rows, block))] * n,
            out_specs=pl.BlockSpec((step * n, block), lambda i, me: (i, 0)),
            scratch_shapes=[pltpu.VMEM((n, rows, block), BF16), pltpu.VMEM((block // LANES, step * n, LANES), F32)],
        ),
        compiler_params=params(40),
        cost_estimate=pl.CostEstimate(
            flops=2 * rows * width * n * block, bytes_accessed=2 * width * n * block, transcendentals=0
        ),
    )(me, h, *[ds[s] for s in order])


def column(values):
    return jnp.broadcast_to(values[:, None], (values.shape[0], LANES))


def on_device(hidden_rows, head_weight, norm_gain, vocab_embed, targets):
    n_dp, n_mp = lax.axis_size("dp"), lax.axis_size("mp")
    tok_dp, width_mp = hidden_rows.shape
    block = head_weight.shape[3]
    width = width_mp * n_mp
    tokens = tok_dp * n_dp
    vocab_mp = vocab_embed.shape[0]
    dp_bits, mp_bits = bits_of(n_dp), bits_of(n_mp)
    dp_index = lax.axis_index("dp")
    mp_index = lax.axis_index("mp")
    me = mp_index.astype(jnp.int32).reshape(1)
    odd = [s for s in range(n_mp - 1, -1, -1) if s & 1]
    even = [s - 1 for s in odd]
    ks_odd = mp_index.astype(jnp.int32) ^ jnp.array(odd, jnp.int32)
    ks_even = mp_index.astype(jnp.int32) ^ jnp.array(even, jnp.int32)
    orders = [dp_bits, dp_bits[::-1]]

    weight = head_weight.reshape(width_mp, n_mp, block).transpose(1, 0, 2)
    embed = vocab_embed.reshape(vocab_mp, n_mp, block).transpose(1, 0, 2)
    gain = norm_gain.reshape(1, block)

    half = width_mp // 2
    left, right = (
        gather_xor(hidden_rows[:, i * half : (i + 1) * half], "dp", orders[i]) for i in range(2)
    )
    h = jnp.concatenate(
        [jnp.concatenate([left[s], right[s]], axis=1) for s in range(n_dp)], axis=0
    )
    own_h = lax.dynamic_slice_in_dim(h, dp_index * block, block, 1)

    def reduce_blocks(sent, kept):
        arrived = swap(sent, "mp", 1)
        terms = {s: [kept[i], arrived[i]] for i, s in enumerate(even)}
        return scatter_xor(terms, "mp", mp_bits[1:], BF16)

    parts = reduce_blocks(project(h, weight, ks_odd, BF16), project(h, weight, ks_even, F32))
    pre, x, squares = activate(parts, own_h, gain)

    squares = squares[:, 0].reshape(n_dp, tok_dp)
    for bit in mp_bits:
        squares = squares + swap(squares, "mp", bit)
    for bit in dp_bits:
        arrived = swap(squares, "dp", bit)
        squares = squares + jnp.stack([arrived[s ^ bit] for s in range(n_dp)])
    squares = column(squares[0])

    xs = gather_xor(x, "mp", mp_bits[::-1])
    half = vocab_mp // 2
    pieces = []
    for i in range(2):
        partial = project_vocab(xs, embed, me, n_dp, i * half, half)
        pieces.append(scatter_xor({s: [p] for s, p in enumerate(partial)}, "dp", orders[i], F32))
    local = lax.dynamic_slice_in_dim(targets, dp_index * tok_dp, tok_dp, 0) - mp_index * vocab_mp
    local = column(local)
    *own_q, stats = softmax(pieces, squares, local, width)
    q = [gather_xor(own_q[i], "dp", orders[i]) for i in range(2)]
    all_stats = gather_xor(stats, "mp", mp_bits)
    packed = merge([all_stats[s] for s in range(n_mp)], squares, local, tokens, width)
    packs = gather_xor(packed, "dp", dp_bits)
    packs = [packs[s] for s in range(n_dp)]
    loss = tree(jnp.add, [jnp.sum(p[:, 5]) for p in packs]) / tokens

    rows = [[q[0][s], q[1][s]] for s in range(n_dp)]
    parts = reduce_blocks(
        project_back(rows, packs, embed, ks_odd, BF16), project_back(rows, packs, embed, ks_even, F32)
    )
    dpre = grad_pre(parts, packs, pre, own_h, gain)
    grad = weight_grad(h, gather_xor(dpre, "mp", mp_bits[::-1]), me)
    return (grad.reshape(head_weight.shape), loss)


def solution(mesh):
    return jax.shard_map(
        on_device,
        mesh=mesh,
        in_specs=(
            P("dp", "mp"),
            P("mp", None, "dp", None),
            P("mp", "dp", None),
            P("mp", None, "dp", None),
            P(),
        ),
        out_specs=(P("mp", None, "dp", None), P()),
        check_vma=False,
    )
```

time: 496 us -> 298 us (0.60)
  blocking collectives: 117 us -> 0 us
  waiting for transfers between devices: 223 us -> 115 us
  starting transfers between devices: 0.47 us -> 64.7 us
  Pallas kernels: 0 us -> 62.8 us
  matrix products: 59.7 us -> 0 us
  local copies, waits for them, and re-layouts: 66.1 us -> 44.8 us
  between operations: 16 us -> 4.72 us
  other arithmetic: 12.5 us -> 5.67 us
    reduce_scatter x3 -> x0, waiting for transfers between devices: 146 us -> none  [the longest x1 51.2 us: on_device(): lax.psum_scatter(lax.dot_general(columns, embed_flat, contract, preferred...]
    ppermute x0 -> x55, waiting for transfers between devices: none -> 115 us  [swap(): return lax.ppermute(value, axis, [(i, i ^ bit) for i in range(n)])]
    psum x4 -> x0, blocking collectives: 103 us -> none  [the longest x1 39.2 us: on_device(): inner = lax.psum(jnp.sum(act * scaled, axis=0), ('dp', 'mp')) / width]
    all_gather x4 -> x0, waiting for transfers between devices: 76 us -> none  [the longest x1 32.6 us: on_device(): all_dlogits = lax.all_gather(dlogits, 'dp', axis=0, tiled=True)]
    ppermute x0 -> x55, starting transfers between devices: none -> 64.7 us  [swap(): return lax.ppermute(value, axis, [(i, i ^ bit) for i in range(n)])]
    pallas_call x0 -> x11, Pallas kernels: none -> 62.8 us  [the longest x2 19.9 us: project_back(): pl.pallas_call(functools.partial(dnormed_kernel, n_blocks, n_pieces), out...]
    dot_general x4 -> x0, matrix products: 59.7 us -> none  [the longest x1 19.8 us: on_device(): lax.dot_general(columns, all_dlogits, contract, preferred_element_type=jn...]
    unnamed x12 -> x24, local copies, waits for them, and re-layouts: 66.1 us -> 42.4 us
  transfers between devices with their start and end apart: 7 -> 55, of which waited for: 7 -> 26; matrix products, arithmetic and copies ran while one was open for 8% -> 14% of each run, Pallas kernels for 0% -> 11%
where the time goes in v1:
time: 298 us
  waiting for transfers between devices  115 us (39%)
  starting transfers between devices  64.7 us (22%)
  Pallas kernels  62.8 us (21%)
  local copies, waits for them, and re-layouts  44.8 us (15%)
  other arithmetic  5.67 us (2%)
  between operations  4.72 us (2%)
    ppermute x55, waiting for transfers between devices, swap(): return lax.ppermute(value, axis, [(i, i ^ bit) for i in range(n)])  115 us
    ppermute x55, starting transfers between devices, swap(): return lax.ppermute(value, axis, [(i, i ^ bit) for i in range(n)])  64.7 us
    unnamed x24, local copies, waits for them, and re-layouts  42.4 us
    pallas_call x2, Pallas kernels, project_back(): pl.pallas_call(functools.partial(dnormed_kernel, n_blocks, n_pieces), out...  19.9 us
    pallas_call x2, Pallas kernels, project_vocab(): pl.pallas_call(functools.partial(logits_kernel, order, n_out), out_shape=...  17.2 us
    pallas_call x1, Pallas kernels, weight_grad(): pl.pallas_call(functools.partial(grad_kernel, order), out_shape=jax.Shape...  16.1 us
    pallas_call x2, Pallas kernels, project(): pl.pallas_call(project_kernel, out_shape=jax.ShapeDtypeStruct((count, row...  6.81 us
  transfers between devices with their start and end apart: 55, of which 26 were waited for; matrix products, arithmetic and copies ran while one was open for 14% of the time, Pallas kernels for 11%

profile of v1, /device:TPU:1, one launch (start us, length us, event | category | flops | bytes accessed | tf_op | source)
XLA Modules:
  0.0 297.5 jit_solution(15788810890214889386)
XLA Ops:
  5.3 12.2 %copy.18 = bf16[2048,8,1,512]{3,0,1,2:T(8,128)(2,1)S(1)} copy(bf16[2048,8,1,512]{3,1,2,0:T(8,128)(2,1)} %param.8) | data formatting | bytes 33554432 | tf_op args[1]
  23.2 3.4 %shard_map.87 = bf16[4,256,512]{2,1,0:T(8,128)(2,1)S(1)} custom-call(s32[4]{0:T(128)S(1)} %broadcast_xor_fusion.ks, bf16[256,2048]{1,0:T(8,128)(2,1)S(1)} %maximum_maximum_fusion.lhs.h, bf16[8,2048,512]{2,1,0:T(8,128)(2,1)S(1)} %bitcast.45), custom_call_target="tpu_custom_call" | custom-call | flops 2147483648 | bytes 8388608 | tf_op jit(solution)/shard_map/pallas_call | solution.py:61
  26.6 3.0 %collective-permute-start.6 = (bf16[4,256,512]{2,1,0:T(8,128)(2,1)S(1)}, bf16[4,256,512]{2,1,0:T(8,128)(2,1)S(1)}, u32[]{:S(2)}, u32[]{:S(2)}) collective-permute-start(bf16[4,256,512]{2,1,0:T(8,128)(2,1)S(1)} %shard_map.87), channel_id=1, source_target_pairs={{0,1},{1,0},{2,3},{3,2},{4,5},{5,4},{6,7},{7,6},{8,9},{9,8},{10,11... | collective-permute-start | bytes 3145736 | tf_op jit(solution)/shard_map/ppermute | solution.py:27
  29.6 5.8 %copy-done.1 = bf16[2048,8,1,512]{3,0,1,2:T(8,128)(2,1)S(1)} copy-done((bf16[2048,8,1,512]{3,0,1,2:T(8,128)(2,1)S(1)}, bf16[2048,8,1,512]{3,0,1,2:T(8,128)(2,1)}, u32[]{:S(2)}) %copy-start.1) | copy-done | bytes 16777240
  35.4 3.4 %shard_map.86 = f32[4,256,512]{2,1,0:T(8,128)S(1)} custom-call(s32[4]{0:T(128)S(1)} %broadcast_xor_fusion.1.ks, bf16[256,2048]{1,0:T(8,128)(2,1)S(1)} %maximum_maximum_fusion.lhs.h, bf16[8,2048,512]{2,1,0:T(8,128)(2,1)S(1)} %bitcast.46), custom_call_target="tpu_custom_call" | custom-call | flops 2147483648 | bytes 8388608 | tf_op jit(solution)/shard_map/pallas_call | solution.py:61
  42.4 6.8 %collective-permute-done.8 = bf16[256,512]{1,0:T(8,128)(2,1)} collective-permute-done((bf16[256,512]{1,0:T(8,128)(2,1)}, bf16[256,512]{1,0:T(8,128)(2,1)}, u32[]{:S(2)}, u32[]{:S(2)}) %collective-permute-start.8) | collective-permute-done | bytes 262176 | tf_op jit(solution)/shard_map/ppermute | solution.py:27
  53.7 4.2 %collective-permute-done.7.refs_2_ = bf16[256,512]{1,0:T(8,128)(2,1)S(1)} collective-permute-done((bf16[256,512]{1,0:T(8,128)(2,1)S(1)}, bf16[256,512]{1,0:T(8,128)(2,1)S(1)}, u32[]{:S(2)}, u32[]{:S(2)}) %collective-permute-start.7) | collective-permute-done | bytes 262176 | tf_op jit(solution)/shard_map/ppermute | solution.py:27
  57.9 5.7 %collective-permute-done.9.refs_3_ = bf16[256,512]{1,0:T(8,128)(2,1)S(1)} collective-permute-done((bf16[256,512]{1,0:T(8,128)(2,1)S(1)}, bf16[256,512]{1,0:T(8,128)(2,1)S(1)}, u32[]{:S(2)}, u32[]{:S(2)}) %collective-permute-start.9) | collective-permute-done | bytes 262176 | tf_op jit(solution)/shard_map/ppermute | solution.py:27
  64.7 4.2 %collective-permute-start.11 = (bf16[256,512]{1,0:T(8,128)(2,1)S(1)}, bf16[256,512]{1,0:T(8,128)(2,1)S(1)}, u32[]{:S(2)}, u32[]{:S(2)}) collective-permute-start(bf16[256,512]{1,0:T(8,128)(2,1)S(1)} %get-tuple-element.16.refs_0_), channel_id=1, source_target_pairs={{0,2},{1,3},{2,0},{3,1},{4,6},{5,7},{6,4},{7,5},{8,10},{9,11},{10,... | collective-permute-start | bytes 786440 | tf_op jit(solution)/shard_map/ppermute | solution.py:27
  69.0 8.9 %collective-permute-done.13.refs_4_ = bf16[256,512]{1,0:T(8,128)(2,1)S(1)} collective-permute-done((bf16[256,512]{1,0:T(8,128)(2,1)S(1)}, bf16[256,512]{1,0:T(8,128)(2,1)S(1)}, u32[]{:S(2)}, u32[]{:S(2)}) %collective-permute-start.13) | collective-permute-done | bytes 262176 | tf_op jit(solution)/shard_map/ppermute | solution.py:27
  80.6 2.8 collective-permute-done.15.refs_6_
  83.4 3.2 %collective-permute-start.16 = (bf16[256,512]{1,0:T(8,128)(2,1)S(1)}, bf16[256,512]{1,0:T(8,128)(2,1)S(1)}, u32[]{:S(2)}, u32[]{:S(2)}) collective-permute-start(bf16[256,512]{1,0:T(8,128)(2,1)S(1)} %collective-permute-done.15.refs_6_), channel_id=1, source_target_pairs={{0,1},{1,0},{2,3},{3,2},{4,5},{5,4},{6,7},{7,6},{8,9},{9,8},{10,11... | collective-permute-start | bytes 786440 | tf_op jit(solution)/shard_map/ppermute | solution.py:27
  91.5 22.7 %copy.17 = bf16[4096,8,1,512]{3,0,1,2:T(8,128)(2,1)} copy(bf16[4096,8,1,512]{3,1,2,0:T(8,128)(2,1)} %param.10) | data formatting | bytes 67108864 | tf_op args[3]
  115.5 8.6 %shard_map.90 = (f32[64,2048]{1,0:T(8,128)S(1)}, f32[64,2048]{1,0:T(8,128)S(1)}, f32[64,2048]{1,0:T(8,128)S(1)}, f32[64,2048]{1,0:T(8,128)S(1)}) custom-call(s32[1]{0:T(128)} %bitcast.me, bf16[256,512]{1,0:T(8,128)(2,1)S(1)} %get-tuple-element.16.refs_0_, bf16[256,512]{1,0:T(8,128)(2,1)S(1)} %collective-permute-done.10.refs_1_, ...), custom_call_target="tpu_custom_call" | custom-call | flops 4294967296 | bytes 16777216 | tf_op jit(solution)/shard_map/pallas_call | solution.py:118
  124.5 8.6 %shard_map.89 = (f32[64,2048]{1,0:T(8,128)S(1)}, f32[64,2048]{1,0:T(8,128)S(1)}, f32[64,2048]{1,0:T(8,128)S(1)}, f32[64,2048]{1,0:T(8,128)S(1)}) custom-call(s32[1]{0:T(128)} %bitcast.me, bf16[256,512]{1,0:T(8,128)(2,1)S(1)} %get-tuple-element.16.refs_0_, bf16[256,512]{1,0:T(8,128)(2,1)S(1)} %collective-permute-done.10.refs_1_, ...), custom_call_target="tpu_custom_call" | custom-call | flops 4294967296 | bytes 16777216 | tf_op jit(solution)/shard_map/pallas_call | solution.py:118
  137.0 7.4 %collective-permute-done.18 = f32[64,2048]{1,0:T(8,128)S(1)} collective-permute-done((f32[64,2048]{1,0:T(8,128)S(1)}, f32[64,2048]{1,0:T(8,128)S(1)}, u32[]{:S(2)}, u32[]{:S(2)}) %collective-permute-start.18) | collective-permute-done | bytes 524320 | tf_op jit(solution)/shard_map/ppermute | solution.py:27
  146.9 8.7 %collective-permute-done.17.refs_1_ = f32[64,2048]{1,0:T(8,128)S(1)} collective-permute-done((f32[64,2048]{1,0:T(8,128)S(1)}, f32[64,2048]{1,0:T(8,128)S(1)}, u32[]{:S(2)}, u32[]{:S(2)}) %collective-permute-start.17) | collective-permute-done | bytes 524320 | tf_op jit(solution)/shard_map/ppermute | solution.py:27
  155.6 11.2 %collective-permute-done.22.refs_5_ = f32[64,2048]{1,0:T(8,128)S(1)} collective-permute-done((f32[64,2048]{1,0:T(8,128)S(1)}, f32[64,2048]{1,0:T(8,128)S(1)}, u32[]{:S(2)}, u32[]{:S(2)}) %collective-permute-start.22) | collective-permute-done | bytes 524320 | tf_op jit(solution)/shard_map/ppermute | solution.py:27
  169.3 3.7 %collective-permute-start.34 = (f32[64,128]{1,0:T(8,128)S(1)}, f32[64,128]{1,0:T(8,128)S(1)}, u32[]{:S(2)}, u32[]{:S(2)}) collective-permute-start(f32[64,128]{1,0:T(8,128)S(1)} %get-tuple-element.28.refs_0_), channel_id=1, source_target_pairs={{0,1},{1,0},{2,3},{3,2},{4,5},{5,4},{6,7},{7,6},{8,9},{9,8},{10,11... | collective-permute-start | bytes 98312 | tf_op jit(solution)/shard_map/ppermute | solution.py:27
  182.9 2.5 collective-permute-done.38.refs_5_
  190.2 2.5 collective-permute-done.40.refs_7_
  197.1 2.5 collective-permute-done.42.refs_10_.refs_6_
  199.8 2.5 collective-permute-done.43.refs_11_.refs_7_
  202.4 10.1 %shard_map.94 = bf16[4,256,512]{2,1,0:T(8,128)(2,1)S(1)} custom-call(s32[4]{0:T(128)S(1)} %broadcast_xor_fusion.ks, bf16[64,2048]{1,0:T(8,128)(2,1)S(1)} %get-tuple-element.26.refs_0_, bf16[64,2048]{1,0:T(8,128)(2,1)S(1)} %get-tuple-element.27.refs_1_, bf16[64,2048]{1,0:T(8,128)(2,1)S(1)} %collective-permute-done.28.refs_2_, ...), custom_call_target="tpu_custom_call" | custom-call | flops 4294967296 | bytes 16777216 | tf_op jit(solution)/shard_map/pallas_call | solution.py:245
  212.4 9.5 %collective-permute-start.44 = (bf16[4,256,512]{2,1,0:T(8,128)(2,1)S(1)}, bf16[4,256,512]{2,1,0:T(8,128)(2,1)S(1)}, u32[]{:S(2)}, u32[]{:S(2)}) collective-permute-start(bf16[4,256,512]{2,1,0:T(8,128)(2,1)S(1)} %shard_map.94), channel_id=1, source_target_pairs={{0,1},{1,0},{2,3},{3,2},{4,5},{5,4},{6,7},{7,6},{8,9},{9,8},{10,11... | collective-permute-start | bytes 3145736 | tf_op jit(solution)/shard_map/ppermute | solution.py:27
  222.0 9.9 %shard_map.93 = f32[4,256,512]{2,1,0:T(8,128)S(1)} custom-call(s32[4]{0:T(128)S(1)} %broadcast_xor_fusion.1.ks, bf16[64,2048]{1,0:T(8,128)(2,1)S(1)} %get-tuple-element.26.refs_0_, bf16[64,2048]{1,0:T(8,128)(2,1)S(1)} %get-tuple-element.27.refs_1_, bf16[64,2048]{1,0:T(8,128)(2,1)S(1)} %collective-permute-done.28.refs_2_, ...), custom_call_target="tpu_custom_call" | custom-call | flops 4294967296 | bytes 16777216 | tf_op jit(solution)/shard_map/pallas_call | solution.py:245
  233.9 6.6 %collective-permute-done.46 = bf16[256,512]{1,0:T(8,128)(2,1)S(1)} collective-permute-done((bf16[256,512]{1,0:T(8,128)(2,1)S(1)}, bf16[256,512]{1,0:T(8,128)(2,1)S(1)}, u32[]{:S(2)}, u32[]{:S(2)}) %collective-permute-start.46) | collective-permute-done | bytes 262176 | tf_op jit(solution)/shard_map/ppermute | solution.py:27
  241.6 7.4 %collective-permute-done.45.refs_2_ = bf16[256,512]{1,0:T(8,128)(2,1)S(1)} collective-permute-done((bf16[256,512]{1,0:T(8,128)(2,1)S(1)}, bf16[256,512]{1,0:T(8,128)(2,1)S(1)}, u32[]{:S(2)}, u32[]{:S(2)}) %collective-permute-start.45) | collective-permute-done | bytes 262176 | tf_op jit(solution)/shard_map/ppermute | solution.py:27
  249.0 5.2 %collective-permute-done.47.refs_3_ = bf16[256,512]{1,0:T(8,128)(2,1)S(1)} collective-permute-done((bf16[256,512]{1,0:T(8,128)(2,1)S(1)}, bf16[256,512]{1,0:T(8,128)(2,1)S(1)}, u32[]{:S(2)}, u32[]{:S(2)}) %collective-permute-start.47) | collective-permute-done | bytes 262176 | tf_op jit(solution)/shard_map/ppermute | solution.py:27
  254.8 12.1 %collective-permute-done.51.refs_4_ = bf16[256,512]{1,0:T(8,128)(2,1)S(1)} collective-permute-done((bf16[256,512]{1,0:T(8,128)(2,1)S(1)}, bf16[256,512]{1,0:T(8,128)(2,1)S(1)}, u32[]{:S(2)}, u32[]{:S(2)}) %collective-permute-start.51) | collective-permute-done | bytes 262176 | tf_op jit(solution)/shard_map/ppermute | solution.py:27
  269.4 4.1 %collective-permute-done.53.refs_6_ = bf16[256,512]{1,0:T(8,128)(2,1)S(1)} collective-permute-done((bf16[256,512]{1,0:T(8,128)(2,1)S(1)}, bf16[256,512]{1,0:T(8,128)(2,1)S(1)}, u32[]{:S(2)}, u32[]{:S(2)}) %collective-permute-start.53) | collective-permute-done | bytes 262176 | tf_op jit(solution)/shard_map/ppermute | solution.py:27
  280.3 16.1 %shard_map.96 = bf16[16384,512]{1,0:T(8,128)(2,1)} custom-call(s32[1]{0:T(128)} %bitcast.me, bf16[256,2048]{1,0:T(8,128)(2,1)S(1)} %maximum_maximum_fusion.lhs.h, bf16[256,512]{1,0:T(8,128)(2,1)S(1)} %shard_map.95.refs_0_, bf16[256,512]{1,0:T(8,128)(2,1)S(1)} %collective-permute-done.48.refs_1_, bf16[256,512]{1,0:T(8,128)(2,1)S(1)} %collective-permute-done.49.refs_2_, ...), custom_call_target="tpu_custom_call" | custom-call | flops 4294967296 | bytes 16777216 | tf_op jit(solution)/shard_map/pallas_call | solution.py:315
  (143 shorter events, 67.6 us)
Async XLA Ops:
  1.6 15.9 %collective-permute-start = (bf16[64,1024]{1,0:T(8,128)(2,1)S(1)}, bf16[64,1024]{1,0:T(8,128)(2,1)S(1)}, u32[]{:S(2)}, u32[]{:S(2)}) collective-permute-start(bf16[64,1024]{1,0:T(8,128)(2,1)S(1)} %get-tuple-element.40), channel_id=1, source_target_pairs={{0,8},{8,0},{16,24},{24,16},{1,9},{9,1},{17,25},{25,17},{2,10},{10... | collective-permute-start | bytes 393224 | tf_op jit(solution)/shard_map/ppermute | solution.py:27
  3.7 15.2 %collective-permute-start.3 = (bf16[64,1024]{1,0:T(8,128)(2,1)S(1)}, bf16[64,1024]{1,0:T(8,128)(2,1)S(1)}, u32[]{:S(2)}, u32[]{:S(2)}) collective-permute-start(bf16[64,1024]{1,0:T(8,128)(2,1)S(1)} %get-tuple-element.41), channel_id=1, source_target_pairs={{0,16},{8,24},{16,0},{24,8},{1,17},{9,25},{17,1},{25,9},{2,18},{10... | collective-permute-start | bytes 393224 | tf_op jit(solution)/shard_map/ppermute | solution.py:27
  5.0 15.2 %collective-permute-start.1 = (bf16[64,1024]{1,0:T(8,128)(2,1)S(1)}, bf16[64,1024]{1,0:T(8,128)(2,1)S(1)}, u32[]{:S(2)}, u32[]{:S(2)}) collective-permute-start(bf16[64,1024]{1,0:T(8,128)(2,1)S(1)} %get-tuple-element.41), channel_id=1, source_target_pairs={{0,8},{8,0},{16,24},{24,16},{1,9},{9,1},{17,25},{25,17},{2,10},{10... | collective-permute-start | bytes 393224 | tf_op jit(solution)/shard_map/ppermute | solution.py:27
  5.2 15.0 %collective-permute-start.2 = (bf16[64,1024]{1,0:T(8,128)(2,1)S(1)}, bf16[64,1024]{1,0:T(8,128)(2,1)S(1)}, u32[]{:S(2)}, u32[]{:S(2)}) collective-permute-start(bf16[64,1024]{1,0:T(8,128)(2,1)S(1)} %get-tuple-element.40), channel_id=1, source_target_pairs={{0,16},{8,24},{16,0},{24,8},{1,17},{9,25},{17,1},{25,9},{2,18},{10... | collective-permute-start | bytes 393224 | tf_op jit(solution)/shard_map/ppermute | solution.py:27
  26.6 12.2 %collective-permute-start.6 = (bf16[4,256,512]{2,1,0:T(8,128)(2,1)S(1)}, bf16[4,256,512]{2,1,0:T(8,128)(2,1)S(1)}, u32[]{:S(2)}, u32[]{:S(2)}) collective-permute-start(bf16[4,256,512]{2,1,0:T(8,128)(2,1)S(1)} %shard_map.87), channel_id=1, source_target_pairs={{0,1},{1,0},{2,3},{3,2},{4,5},{5,4},{6,7},{7,6},{8,9},{9,8},{10,11... | collective-permute-start | bytes 3145736 | tf_op jit(solution)/shard_map/ppermute | solution.py:27
  42.2 15.6 %collective-permute-start.7 = (bf16[256,512]{1,0:T(8,128)(2,1)S(1)}, bf16[256,512]{1,0:T(8,128)(2,1)S(1)}, u32[]{:S(2)}, u32[]{:S(2)}) collective-permute-start(bf16[256,512]{1,0:T(8,128)(2,1)S(1)} %get-tuple-element.37), channel_id=1, source_target_pairs={{0,2},{1,3},{2,0},{3,1},{4,6},{5,7},{6,4},{7,5},{8,10},{9,11},{10,... | collective-permute-start | bytes 786440 | tf_op jit(solution)/shard_map/ppermute | solution.py:27
  50.3 13.2 %collective-permute-start.9 = (bf16[256,512]{1,0:T(8,128)(2,1)S(1)}, bf16[256,512]{1,0:T(8,128)(2,1)S(1)}, u32[]{:S(2)}, u32[]{:S(2)}) collective-permute-start(bf16[256,512]{1,0:T(8,128)(2,1)S(1)} %fusion.8), channel_id=1, source_target_pairs={{0,4},{1,5},{2,6},{3,7},{4,0},{5,1},{6,2},{7,3},{8,12},{9,13},{10,... | collective-permute-start | bytes 786440 | tf_op jit(solution)/shard_map/ppermute | solution.py:27
  64.7 13.1 %collective-permute-start.13 = (bf16[256,512]{1,0:T(8,128)(2,1)S(1)}, bf16[256,512]{1,0:T(8,128)(2,1)S(1)}, u32[]{:S(2)}, u32[]{:S(2)}) collective-permute-start(bf16[256,512]{1,0:T(8,128)(2,1)S(1)} %get-tuple-element.16.refs_0_), channel_id=1, source_target_pairs={{0,4},{1,5},{2,6},{3,7},{4,0},{5,1},{6,2},{7,3},{8,12},{9,13},{10,... | collective-permute-start | bytes 786440 | tf_op jit(solution)/shard_map/ppermute | solution.py:27
  64.7 15.4 %collective-permute-start.11 = (bf16[256,512]{1,0:T(8,128)(2,1)S(1)}, bf16[256,512]{1,0:T(8,128)(2,1)S(1)}, u32[]{:S(2)}, u32[]{:S(2)}) collective-permute-start(bf16[256,512]{1,0:T(8,128)(2,1)S(1)} %get-tuple-element.16.refs_0_), channel_id=1, source_target_pairs={{0,2},{1,3},{2,0},{3,1},{4,6},{5,7},{6,4},{7,5},{8,10},{9,11},{10,... | collective-permute-start | bytes 786440 | tf_op jit(solution)/shard_map/ppermute | solution.py:27
  77.8 37.7 %collective-permute-start.10 = (bf16[256,512]{1,0:T(8,128)(2,1)S(1)}, bf16[256,512]{1,0:T(8,128)(2,1)S(1)}, u32[]{:S(2)}, u32[]{:S(2)}) collective-permute-start(bf16[256,512]{1,0:T(8,128)(2,1)S(1)} %get-tuple-element.16.refs_0_), channel_id=1, source_target_pairs={{0,1},{1,0},{2,3},{3,2},{4,5},{5,4},{6,7},{7,6},{8,9},{9,8},{10,11... | collective-permute-start | bytes 786440 | tf_op jit(solution)/shard_map/ppermute | solution.py:27
  80.1 35.4 %collective-permute-start.14 = (bf16[256,512]{1,0:T(8,128)(2,1)S(1)}, bf16[256,512]{1,0:T(8,128)(2,1)S(1)}, u32[]{:S(2)}, u32[]{:S(2)}) collective-permute-start(bf16[256,512]{1,0:T(8,128)(2,1)S(1)} %collective-permute-done.13.refs_4_), channel_id=1, source_target_pairs={{0,1},{1,0},{2,3},{3,2},{4,5},{5,4},{6,7},{7,6},{8,9},{9,8},{10,11... | collective-permute-start | bytes 786440 | tf_op jit(solution)/shard_map/ppermute | solution.py:27
  80.1 35.4 %collective-permute-start.12 = (bf16[256,512]{1,0:T(8,128)(2,1)S(1)}, bf16[256,512]{1,0:T(8,128)(2,1)S(1)}, u32[]{:S(2)}, u32[]{:S(2)}) collective-permute-start(bf16[256,512]{1,0:T(8,128)(2,1)S(1)} %collective-permute-done.11.refs_2_), channel_id=1, source_target_pairs={{0,1},{1,0},{2,3},{3,2},{4,5},{5,4},{6,7},{7,6},{8,9},{9,8},{10,11... | collective-permute-start | bytes 786440 | tf_op jit(solution)/shard_map/ppermute | solution.py:27
  83.4 32.2 %collective-permute-start.16 = (bf16[256,512]{1,0:T(8,128)(2,1)S(1)}, bf16[256,512]{1,0:T(8,128)(2,1)S(1)}, u32[]{:S(2)}, u32[]{:S(2)}) collective-permute-start(bf16[256,512]{1,0:T(8,128)(2,1)S(1)} %collective-permute-done.15.refs_6_), channel_id=1, source_target_pairs={{0,1},{1,0},{2,3},{3,2},{4,5},{5,4},{6,7},{7,6},{8,9},{9,8},{10,11... | collective-permute-start | bytes 786440 | tf_op jit(solution)/shard_map/ppermute | solution.py:27
  90.3 23.9 %collective-permute-start.25 = (f32[4,64]{1,0:T(4,128)S(1)}, f32[4,64]{1,0:T(4,128)S(1)}, u32[]{:S(2)}, u32[]{:S(2)}) collective-permute-start(f32[4,64]{1,0:T(4,128)S(1)} %add.79), channel_id=1, source_target_pairs={{0,4},{1,5},{2,6},{3,7},{4,0},{5,1},{6,2},{7,3},{8,12},{9,13},{10,... | collective-permute-start | bytes 3080 | tf_op jit(solution)/shard_map/ppermute | solution.py:27
  114.2 19.5 %collective-permute-start.26 = (f32[4,64]{1,0:T(4,128)S(1)}, f32[4,64]{1,0:T(4,128)S(1)}, u32[]{:S(2)}, u32[]{:S(2)}) collective-permute-start(f32[4,64]{1,0:T(4,128)S(1)} %add.80), channel_id=1, source_target_pairs={{0,8},{8,0},{16,24},{24,16},{1,9},{9,1},{17,25},{25,17},{2,10},{10... | collective-permute-start | bytes 3080 | tf_op jit(solution)/shard_map/ppermute | solution.py:27
  124.2 12.1 %collective-permute-start.21 = (f32[64,2048]{1,0:T(8,128)S(1)}, f32[64,2048]{1,0:T(8,128)S(1)}, u32[]{:S(2)}, u32[]{:S(2)}) collective-permute-start(f32[64,2048]{1,0:T(8,128)S(1)} %get-tuple-element.24), channel_id=1, source_target_pairs={{0,16},{8,24},{16,0},{24,8},{1,17},{9,25},{17,1},{25,9},{2,18},{10... | collective-permute-start | bytes 1572872 | tf_op jit(solution)/shard_map/ppermute | solution.py:27
  133.8 12.0 %collective-permute-start.27 = (f32[4,64]{1,0:T(4,128)S(1)}, f32[4,64]{1,0:T(4,128)S(1)}, u32[]{:S(2)}, u32[]{:S(2)}) collective-permute-start(f32[4,64]{1,0:T(4,128)S(1)} %maximum_add_fusion), channel_id=1, source_target_pairs={{0,16},{8,24},{16,0},{24,8},{1,17},{9,25},{17,1},{25,9},{2,18},{10... | collective-permute-start | bytes 3080 | tf_op jit(solution)/shard_map/ppermute | solution.py:27
  134.8 12.1 %collective-permute-start.20 = (f32[64,2048]{1,0:T(8,128)S(1)}, f32[64,2048]{1,0:T(8,128)S(1)}, u32[]{:S(2)}, u32[]{:S(2)}) collective-permute-start(f32[64,2048]{1,0:T(8,128)S(1)} %get-tuple-element.22), channel_id=1, source_target_pairs={{0,16},{8,24},{16,0},{24,8},{1,17},{9,25},{17,1},{25,9},{2,18},{10... | collective-permute-start | bytes 1572872 | tf_op jit(solution)/shard_map/ppermute | solution.py:27
  135.4 20.2 %collective-permute-start.17 = (f32[64,2048]{1,0:T(8,128)S(1)}, f32[64,2048]{1,0:T(8,128)S(1)}, u32[]{:S(2)}, u32[]{:S(2)}) collective-permute-start(f32[64,2048]{1,0:T(8,128)S(1)} %get-tuple-element.18), channel_id=1, source_target_pairs={{0,8},{8,0},{16,24},{24,16},{1,9},{9,1},{17,25},{25,17},{2,10},{10... | collective-permute-start | bytes 1572872 | tf_op jit(solution)/shard_map/ppermute | solution.py:27
  136.3 30.5 %collective-permute-start.22 = (f32[64,2048]{1,0:T(8,128)S(1)}, f32[64,2048]{1,0:T(8,128)S(1)}, u32[]{:S(2)}, u32[]{:S(2)}) collective-permute-start(f32[64,2048]{1,0:T(8,128)S(1)} %add.77), channel_id=1, source_target_pairs={{0,8},{8,0},{16,24},{24,16},{1,9},{9,1},{17,25},{25,17},{2,10},{10... | collective-permute-start | bytes 1572872 | tf_op jit(solution)/shard_map/ppermute | solution.py:27
  144.5 22.4 %collective-permute-start.19 = (f32[64,2048]{1,0:T(8,128)S(1)}, f32[64,2048]{1,0:T(8,128)S(1)}, u32[]{:S(2)}, u32[]{:S(2)}) collective-permute-start(f32[64,2048]{1,0:T(8,128)S(1)} %add.76), channel_id=1, source_target_pairs={{0,16},{8,24},{16,0},{24,8},{1,17},{9,25},{17,1},{25,9},{2,18},{10... | collective-permute-start | bytes 1572872 | tf_op jit(solution)/shard_map/ppermute | solution.py:27
  174.4 28.0 %collective-permute-start.29 = (bf16[64,2048]{1,0:T(8,128)(2,1)S(1)}, bf16[64,2048]{1,0:T(8,128)(2,1)S(1)}, u32[]{:S(2)}, u32[]{:S(2)}) collective-permute-start(bf16[64,2048]{1,0:T(8,128)(2,1)S(1)} %get-tuple-element.27.refs_1_), channel_id=1, source_target_pairs={{0,8},{8,0},{16,24},{24,16},{1,9},{9,1},{17,25},{25,17},{2,10},{10... | collective-permute-start | bytes 786440 | tf_op jit(solution)/shard_map/ppermute | solution.py:27
  176.0 26.4 %collective-permute-start.30 = (bf16[64,2048]{1,0:T(8,128)(2,1)S(1)}, bf16[64,2048]{1,0:T(8,128)(2,1)S(1)}, u32[]{:S(2)}, u32[]{:S(2)}) collective-permute-start(bf16[64,2048]{1,0:T(8,128)(2,1)S(1)} %get-tuple-element.26.refs_0_), channel_id=1, source_target_pairs={{0,16},{8,24},{16,0},{24,8},{1,17},{9,25},{17,1},{25,9},{2,18},{10... | collective-permute-start | bytes 786440 | tf_op jit(solution)/shard_map/ppermute | solution.py:27
  176.6 25.8 %collective-permute-start.32 = (bf16[64,2048]{1,0:T(8,128)(2,1)S(1)}, bf16[64,2048]{1,0:T(8,128)(2,1)S(1)}, u32[]{:S(2)}, u32[]{:S(2)}) collective-permute-start(bf16[64,2048]{1,0:T(8,128)(2,1)S(1)} %collective-permute-done.28.refs_2_), channel_id=1, source_target_pairs={{0,16},{8,24},{16,0},{24,8},{1,17},{9,25},{17,1},{25,9},{2,18},{10... | collective-permute-start | bytes 786440 | tf_op jit(solution)/shard_map/ppermute | solution.py:27
  177.4 24.9 %collective-permute-start.33 = (bf16[64,2048]{1,0:T(8,128)(2,1)S(1)}, bf16[64,2048]{1,0:T(8,128)(2,1)S(1)}, u32[]{:S(2)}, u32[]{:S(2)}) collective-permute-start(bf16[64,2048]{1,0:T(8,128)(2,1)S(1)} %collective-permute-done.31.refs_5_), channel_id=1, source_target_pairs={{0,8},{8,0},{16,24},{24,16},{1,9},{9,1},{17,25},{25,17},{2,10},{10... | collective-permute-start | bytes 786440 | tf_op jit(solution)/shard_map/ppermute | solution.py:27
  212.4 19.4 %collective-permute-start.44 = (bf16[4,256,512]{2,1,0:T(8,128)(2,1)S(1)}, bf16[4,256,512]{2,1,0:T(8,128)(2,1)S(1)}, u32[]{:S(2)}, u32[]{:S(2)}) collective-permute-start(bf16[4,256,512]{2,1,0:T(8,128)(2,1)S(1)} %shard_map.94), channel_id=1, source_target_pairs={{0,1},{1,0},{2,3},{3,2},{4,5},{5,4},{6,7},{7,6},{8,9},{9,8},{10,11... | collective-permute-start | bytes 3145736 | tf_op jit(solution)/shard_map/ppermute | solution.py:27
  233.9 15.1 %collective-permute-start.45 = (bf16[256,512]{1,0:T(8,128)(2,1)S(1)}, bf16[256,512]{1,0:T(8,128)(2,1)S(1)}, u32[]{:S(2)}, u32[]{:S(2)}) collective-permute-start(bf16[256,512]{1,0:T(8,128)(2,1)S(1)} %get-tuple-element.35), channel_id=1, source_target_pairs={{0,2},{1,3},{2,0},{3,1},{4,6},{5,7},{6,4},{7,5},{8,10},{9,11},{10,... | collective-permute-start | bytes 786440 | tf_op jit(solution)/shard_map/ppermute | solution.py:27
  240.6 13.6 %collective-permute-start.47 = (bf16[256,512]{1,0:T(8,128)(2,1)S(1)}, bf16[256,512]{1,0:T(8,128)(2,1)S(1)}, u32[]{:S(2)}, u32[]{:S(2)}) collective-permute-start(bf16[256,512]{1,0:T(8,128)(2,1)S(1)} %fusion.3), channel_id=1, source_target_pairs={{0,4},{1,5},{2,6},{3,7},{4,0},{5,1},{6,2},{7,3},{8,12},{9,13},{10,... | collective-permute-start | bytes 786440 | tf_op jit(solution)/shard_map/ppermute | solution.py:27
  254.7 12.2 %collective-permute-start.51 = (bf16[256,512]{1,0:T(8,128)(2,1)S(1)}, bf16[256,512]{1,0:T(8,128)(2,1)S(1)}, u32[]{:S(2)}, u32[]{:S(2)}) collective-permute-start(bf16[256,512]{1,0:T(8,128)(2,1)S(1)} %shard_map.95.refs_0_), channel_id=1, source_target_pairs={{0,4},{1,5},{2,6},{3,7},{4,0},{5,1},{6,2},{7,3},{8,12},{9,13},{10,... | collective-permute-start | bytes 786440 | tf_op jit(solution)/shard_map/ppermute | solution.py:27
  254.7 14.1 %collective-permute-start.49 = (bf16[256,512]{1,0:T(8,128)(2,1)S(1)}, bf16[256,512]{1,0:T(8,128)(2,1)S(1)}, u32[]{:S(2)}, u32[]{:S(2)}) collective-permute-start(bf16[256,512]{1,0:T(8,128)(2,1)S(1)} %shard_map.95.refs_0_), channel_id=1, source_target_pairs={{0,2},{1,3},{2,0},{3,1},{4,6},{5,7},{6,4},{7,5},{8,10},{9,11},{10,... | collective-permute-start | bytes 786440 | tf_op jit(solution)/shard_map/ppermute | solution.py:27
  267.6 12.7 %collective-permute-start.48 = (bf16[256,512]{1,0:T(8,128)(2,1)S(1)}, bf16[256,512]{1,0:T(8,128)(2,1)S(1)}, u32[]{:S(2)}, u32[]{:S(2)}) collective-permute-start(bf16[256,512]{1,0:T(8,128)(2,1)S(1)} %shard_map.95.refs_0_), channel_id=1, source_target_pairs={{0,1},{1,0},{2,3},{3,2},{4,5},{5,4},{6,7},{7,6},{8,9},{9,8},{10,11... | collective-permute-start | bytes 786440 | tf_op jit(solution)/shard_map/ppermute | solution.py:27
  268.8 11.4 %collective-permute-start.52 = (bf16[256,512]{1,0:T(8,128)(2,1)S(1)}, bf16[256,512]{1,0:T(8,128)(2,1)S(1)}, u32[]{:S(2)}, u32[]{:S(2)}) collective-permute-start(bf16[256,512]{1,0:T(8,128)(2,1)S(1)} %collective-permute-done.51.refs_4_), channel_id=1, source_target_pairs={{0,1},{1,0},{2,3},{3,2},{4,5},{5,4},{6,7},{7,6},{8,9},{9,8},{10,11... | collective-permute-start | bytes 786440 | tf_op jit(solution)/shard_map/ppermute | solution.py:27
  (34 other events, 257.6 us)

commit v2 on v1

v2 whole, which is shorter than its diff:
```python
import functools

import jax
import jax.numpy as jnp
from jax import lax
from jax.experimental import pallas as pl
from jax.experimental.pallas import tpu as pltpu
from jax.sharding import PartitionSpec as P

F32 = jnp.float32
BF16 = jnp.bfloat16
LANES = 128


def params(mib):
    return pltpu.CompilerParams(vmem_limit_bytes=mib * 2**20)


def bits_of(n):
    bits = [1 << i for i in range(n.bit_length() - 1)]
    assert 1 << len(bits) == n
    return bits


def swap(value, axis, bit):
    n = lax.axis_size(axis)
    return lax.ppermute(value, axis, [(i, i ^ bit) for i in range(n)])


def gather_xor(value, axis, bits):
    held = {0: value}
    for bit in bits:
        for s in list(held):
            held[s | bit] = swap(held[s], axis, bit)
    return held


def gather_direct(value, axis):
    return [value] + [swap(value, axis, s) for s in range(1, lax.axis_size(axis))]


def scatter_xor(terms, axis, bits):
    done = 0
    for bit in bits:
        for s in sorted(terms, reverse=True):
            if s & bit and not s & done:
                total = functools.reduce(jnp.add, terms[s])
                terms[s ^ bit].append(swap(total, axis, bit))
        done |= bit
    return terms[0]


def whole(shape):
    return pl.BlockSpec(shape, lambda *_: (0,) * len(shape))


def after(deps):
    return [pl.BlockSpec(memory_space=pl.ANY)] * len(deps)


def relayout_kernel(n, n_skip, x, *refs):
    out, mixed = refs[n_skip:]
    rows = out.shape[1]
    for j in range(mixed.shape[0]):
        mixed[j] = x[:, j * LANES : (j + 1) * LANES].astype(F32)
    for k in range(n):
        for j in range(mixed.shape[0]):
            out[k, :, j * LANES : (j + 1) * LANES] = mixed[j, pl.ds(k, rows, stride=n), :].astype(BF16)


def relayout(flat, n, start, rows, into, deps):
    total, block = flat.shape[0] // n, flat.shape[1]
    step = min(128, rows)
    skipped = list(deps) if into is None else [into, *deps]
    return pl.pallas_call(
        functools.partial(relayout_kernel, n, len(skipped)),
        out_shape=jax.ShapeDtypeStruct((n, total, block), BF16),
        grid=(rows // step,),
        in_specs=[pl.BlockSpec((step * n, block), lambda i: (start // step + i, 0))] + after(skipped),
        out_specs=pl.BlockSpec((n, step, block), lambda i: (0, start // step + i, 0)),
        scratch_shapes=[pltpu.VMEM((block // LANES, step * n, LANES), F32)],
        input_output_aliases={} if into is None else {1: 0},
        compiler_params=params(40),
        cost_estimate=pl.CostEstimate(flops=0, bytes_accessed=4 * rows * n * block, transcendentals=0),
    )(flat, *skipped)


def project_kernel(n_skip, ks, lhs, w, *refs):
    odd, even, total = refs[n_skip:]
    i, c = pl.program_id(0), pl.program_id(1)
    depth = w.shape[1]
    part = jnp.dot(lhs[:, pl.ds(pl.multiple_of(c * depth, depth), depth)], w[0], preferred_element_type=F32)

    @pl.when(c == 0)
    def _():
        total[...] = part

    @pl.when(c > 0)
    def _():
        total[...] += part

    last = c == pl.num_programs(1) - 1

    @pl.when(jnp.logical_and(last, i % 2 == 0))
    def _():
        odd[0] = total[...].astype(odd.dtype)

    @pl.when(jnp.logical_and(last, i % 2 == 1))
    def _():
        even[0] = total[...]


def project(lhs, w, me, pairs, deps=()):
    _, depth, block = w.shape
    rows = lhs.shape[0]
    count = len(pairs)
    step = min(2048, depth)
    ks = me ^ jnp.array([s for pair in pairs for s in (pair + 1, pair)], jnp.int32)
    return pl.pallas_call(
        functools.partial(project_kernel, len(deps)),
        out_shape=[
            jax.ShapeDtypeStruct((count, rows, block), BF16),
            jax.ShapeDtypeStruct((count, rows, block), F32),
        ],
        grid_spec=pltpu.PrefetchScalarGridSpec(
            num_scalar_prefetch=1,
            grid=(2 * count, depth // step),
            in_specs=[whole(lhs.shape), pl.BlockSpec((1, step, block), lambda i, c, ks: (ks[i], c, 0))]
            + after(deps),
            out_specs=[pl.BlockSpec((1, rows, block), lambda i, c, ks: (i // 2, 0, 0))] * 2,
            scratch_shapes=[pltpu.VMEM((rows, block), F32)],
        ),
        compiler_params=params(40),
        cost_estimate=pl.CostEstimate(
            flops=4 * count * rows * depth * block, bytes_accessed=4 * count * depth * block, transcendentals=0
        ),
    )(ks, lhs, w, *deps)


def pick(term, rows, block):
    array, place = term
    return pl.BlockSpec((1, rows, block), lambda *_: (place, 0, 0))


def add_kernel(n, *refs):
    out = refs[-1]
    total = refs[0][0].astype(F32)
    for ref in refs[1:n]:
        total = total + ref[0].astype(F32)
    out[0] = total.astype(out.dtype)


def add_round(terms, deps=()):
    _, rows, block = terms[0][0].shape
    return pl.pallas_call(
        functools.partial(add_kernel, len(terms)),
        out_shape=jax.ShapeDtypeStruct((1, rows, block), BF16),
        grid=(1,),
        in_specs=[pick(t, rows, block) for t in terms] + after(deps),
        out_specs=whole((1, rows, block)),
        compiler_params=params(40),
    )(*[t[0] for t in terms], *deps)


def act_kernel(n, *refs):
    parts, (h, gain, pre, x, squares) = refs[:n], refs[-5:]
    total = parts[0][0]
    for part in parts[1:]:
        total = total + part[0].astype(F32)
    pre[...] = total
    act = h[...].astype(F32) + total / (1.0 + jnp.exp(-total))
    x[...] = (act * gain[...]).astype(BF16)
    sums = jnp.broadcast_to(jnp.sum(act * act, axis=1, keepdims=True), (act.shape[0], LANES))
    squares[...] = jnp.transpose(sums)[: squares.shape[0]]


def activate(parts, h, gain, deps=()):
    rows, block = h.shape
    return pl.pallas_call(
        functools.partial(act_kernel, len(parts)),
        out_shape=[
            jax.ShapeDtypeStruct((rows, block), F32),
            jax.ShapeDtypeStruct((rows, block), BF16),
            jax.ShapeDtypeStruct((8, rows), F32),
        ],
        grid=(1,),
        in_specs=[pick(t, rows, block) for t in parts] + after(deps) + [whole(h.shape), whole(gain.shape)],
        out_specs=[whole((rows, block)), whole((rows, block)), whole((8, rows))],
        compiler_params=params(40),
    )(*[t[0] for t in parts], *deps, h, gain)


def logits_kernel(n, n_out, me, *refs):
    xs, es, before, outs = refs[:n], refs[n : 2 * n], refs[2 * n : -n_out], refs[-n_out:]
    total = before[0][...] if before else 0.0
    for x, e in zip(xs, es):
        total = total + lax.dot_general(
            x[...], e[0], (((1,), (1,)), ((), ())), preferred_element_type=F32
        )
    rows = total.shape[0] // n_out
    for i, out in enumerate(outs):
        out[...] = total[i * rows : (i + 1) * rows]


def project_vocab(xs, embed, me, before, n_out, start, size):
    block = embed.shape[2]
    order = sorted(xs)
    n = len(order)
    rows = xs[order[0]].shape[0]
    step = min(512, size)
    first = start // step
    sources = [] if before is None else [before]

    def place(s):
        return pl.BlockSpec((1, step, block), lambda i, me: (me[0] ^ s, first + i, 0))

    return pl.pallas_call(
        functools.partial(logits_kernel, n, n_out),
        out_shape=[jax.ShapeDtypeStruct((rows // n_out, size), F32)] * n_out,
        grid_spec=pltpu.PrefetchScalarGridSpec(
            num_scalar_prefetch=1,
            grid=(size // step,),
            in_specs=[whole((rows, block))] * n
            + [place(s) for s in order]
            + [pl.BlockSpec((rows, step), lambda i, me: (0, first + i))] * len(sources),
            out_specs=[pl.BlockSpec((rows // n_out, step), lambda i, me: (0, i))] * n_out,
        ),
        compiler_params=params(40),
        cost_estimate=pl.CostEstimate(
            flops=2 * rows * size * n * block,
            bytes_accessed=2 * size * n * block + 8 * rows * size,
            transcendentals=0,
        ),
    )(me, *[xs[s] for s in order], *[embed] * n, *sources)


def softmax_kernel(counts, width, *refs):
    parts, refs = refs[: sum(counts)], refs[sum(counts) :]
    squares, targets, refs = refs[0], refs[1], refs[2:]
    qs, stats = refs[:-1], refs[-1]
    inv = lax.rsqrt(squares[:, 0:1] / width + 1e-05)
    target = targets[:, 0:1]
    pieces, hits, at, first = [], [], 0, 0
    for count in counts:
        total = parts[at][...]
        for part in parts[at + 1 : at + count]:
            total = total + part[...]
        at += count
        total = total * inv
        ids = lax.broadcasted_iota(jnp.int32, total.shape, 1) + first
        first += total.shape[1]
        pieces.append(total)
        hits.append(ids == target)
    top = functools.reduce(jnp.maximum, [jnp.max(p, axis=1, keepdims=True) for p in pieces])
    mass, moment, picked = 0.0, 0.0, 0.0
    for piece, hit, q in zip(pieces, hits, qs):
        shifted = piece - top
        e = jnp.exp(shifted)
        mass = mass + jnp.sum(e, axis=1, keepdims=True)
        moment = moment + jnp.sum(e * shifted, axis=1, keepdims=True)
        picked = picked + jnp.sum(jnp.where(hit, piece, 0.0), axis=1, keepdims=True)
        q[...] = e.astype(BF16)
    lane = lax.broadcasted_iota(jnp.int32, stats.shape, 1)
    out = jnp.zeros(stats.shape, F32)
    for i, value in enumerate([top, mass, moment, picked]):
        out = jnp.where(lane == i, value, out)
    stats[...] = out


def softmax(pieces, squares, targets, width):
    counts = [len(p) for p in pieces]
    flat = [part for p in pieces for part in p]
    rows = flat[0].shape[0]
    return pl.pallas_call(
        functools.partial(softmax_kernel, counts, width),
        out_shape=[jax.ShapeDtypeStruct(p[0].shape, BF16) for p in pieces]
        + [jax.ShapeDtypeStruct((rows, LANES), F32)],
        compiler_params=params(32),
    )(*flat, squares, targets)


def tree(op, values):
    while len(values) > 1:
        half = len(values) // 2
        values = [op(a, b) for a, b in zip(values[:half], values[half:])]
    return values[0]


def hold_kernel(value, *refs):
    refs[-1][...] = value[...]


def hold(value, deps):
    return pl.pallas_call(
        hold_kernel,
        out_shape=jax.ShapeDtypeStruct(value.shape, value.dtype),
        in_specs=[pl.BlockSpec(memory_space=pltpu.VMEM)] + after(deps),
        compiler_params=params(40),
    )(value, *deps)


def merge_kernel(n, tokens, width, *refs):
    stats, (squares, targets, out) = refs[:n], refs[n:]
    tops = [st[:, 0:1] for st in stats]
    top = tree(jnp.maximum, tops)
    weights = [jnp.exp(t - top) for t in tops]
    mass = tree(jnp.add, [w * st[:, 1:2] for w, st in zip(weights, stats)])
    moment = tree(
        jnp.add, [w * (st[:, 2:3] + st[:, 1:2] * (t - top)) for w, t, st in zip(weights, tops, stats)]
    )
    picked = tree(jnp.add, [st[:, 3:4] for st in stats])
    lse = top + jnp.log(mass)
    inv = lax.rsqrt(squares[:, 0:1] / width + 1e-05)
    scale = jnp.exp(tops[0] - lse) / tokens
    at_target = (jnp.exp(picked - lse) - 1.0) / tokens
    pull = (moment / mass + (top - picked)) * (inv * inv) / (tokens * width)
    lane = lax.broadcasted_iota(jnp.int32, out.shape, 1)
    packed = jnp.zeros(out.shape, F32)
    values = [scale, at_target, targets[:, 0:1].astype(F32), inv, pull, lse - picked]
    for i, value in enumerate(values):
        packed = jnp.where(lane == i, value, packed)
    out[...] = packed


def merge(stats, squares, targets, tokens, width):
    return pl.pallas_call(
        functools.partial(merge_kernel, len(stats), tokens, width),
        out_shape=jax.ShapeDtypeStruct(stats[0].shape, F32),
        compiler_params=params(40),
    )(*stats, squares, targets)


def dlogits_kernel(n_blocks, n_pieces, *refs):
    qs, (packs, dlogits) = refs[: n_blocks * n_pieces], refs[-2:]
    rows = qs[0].shape[0]
    for b in range(n_blocks):
        at = slice(b * rows, (b + 1) * rows)
        scale, at_target, target = packs[at, 0:1], packs[at, 1:2], packs[at, 2:3].astype(jnp.int32)
        first = 0
        for p in range(n_pieces):
            q = qs[b * n_pieces + p][...].astype(F32) * scale
            ids = lax.broadcasted_iota(jnp.int32, q.shape, 1) + first
            dlogits[at, first : first + q.shape[1]] = jnp.where(ids == target, at_target, q).astype(BF16)
            first += q.shape[1]


def scale_rows(qs, packs):
    flat = [q for row in qs for q in row]
    shape = (packs.shape[0], sum(q.shape[1] for q in qs[0]))
    return pl.pallas_call(
        functools.partial(dlogits_kernel, len(qs), len(qs[0])),
        out_shape=jax.ShapeDtypeStruct(shape, BF16),
        compiler_params=params(40),
    )(*flat, packs)


def dpre_kernel(n, *refs):
    parts, (packs, pre, h, gain, out) = refs[:n], refs[n:]
    dnormed = parts[0][0]
    for part in parts[1:]:
        dnormed = dnormed + part[0].astype(F32)
    inv, pull = packs[:, 3:4], packs[:, 4:5]
    v = pre[...]
    sigma = 1.0 / (1.0 + jnp.exp(-v))
    act = h[...].astype(F32) + v * sigma
    dact = inv * gain[...] * dnormed - act * pull
    out[...] = (dact * sigma * (1.0 + v * (1.0 - sigma))).astype(BF16)


def grad_pre(parts, packs, pre, h, gain):
    rows, block = pre.shape
    rest = [packs, pre, h, gain]
    return pl.pallas_call(
        functools.partial(dpre_kernel, len(parts)),
        out_shape=jax.ShapeDtypeStruct(pre.shape, BF16),
        grid=(1,),
        in_specs=[pick(t, rows, block) for t in parts] + [whole(r.shape) for r in rest],
        out_specs=whole(pre.shape),
        compiler_params=params(40),
    )(*[t[0] for t in parts], *rest)


def grad_kernel(order, me, h, *refs):
    n = len(order)
    ds, out, placed, mixed = refs[:n], refs[n], refs[n + 1], refs[n + 2]

    @pl.when(pl.program_id(0) == 0)
    def _():
        for s, d in zip(order, ds):
            placed[me[0] ^ s] = d[...]

    step = h.shape[0]
    for k in range(n):
        product = jnp.dot(h[...], placed[k], preferred_element_type=F32)
        for j in range(mixed.shape[0]):
            mixed[j, pl.ds(k, step, stride=n), :] = product[:, j * LANES : (j + 1) * LANES]
    for j in range(mixed.shape[0]):
        out[:, j * LANES : (j + 1) * LANES] = mixed[j].astype(BF16)


def weight_grad(h, ds, me):
    width, rows = h.shape
    n = len(ds)
    block = ds[0].shape[1]
    order = sorted(ds)
    step = min(256, width)
    return pl.pallas_call(
        functools.partial(grad_kernel, order),
        out_shape=jax.ShapeDtypeStruct((width * n, block), BF16),
        grid_spec=pltpu.PrefetchScalarGridSpec(
            num_scalar_prefetch=1,
            grid=(width // step,),
            in_specs=[pl.BlockSpec((step, rows), lambda i, me: (i, 0))] + [whole((rows, block))] * n,
            out_specs=pl.BlockSpec((step * n, block), lambda i, me: (i, 0)),
            scratch_shapes=[pltpu.VMEM((n, rows, block), BF16), pltpu.VMEM((block // LANES, step * n, LANES), F32)],
        ),
        compiler_params=params(40),
        cost_estimate=pl.CostEstimate(
            flops=2 * rows * width * n * block, bytes_accessed=2 * width * n * block, transcendentals=0
        ),
    )(me, h, *[ds[s] for s in order])


def column(values):
    return jnp.broadcast_to(values[:, None], (values.shape[0], LANES))


def on_device(hidden_rows, head_weight, norm_gain, vocab_embed, targets):
    n_dp, n_mp = lax.axis_size("dp"), lax.axis_size("mp")
    tok_dp, width_mp = hidden_rows.shape
    block = head_weight.shape[3]
    width = width_mp * n_mp
    tokens = tok_dp * n_dp
    vocab_mp = vocab_embed.shape[0]
    dp_bits, mp_bits = bits_of(n_dp), bits_of(n_mp)
    dp_index = lax.axis_index("dp")
    mp_index = lax.axis_index("mp")
    me = mp_index.astype(jnp.int32).reshape(1)
    pairs = list(range(n_mp - 2, -1, -2))
    orders = [dp_bits, dp_bits[::-1]]

    weight_rows = head_weight.reshape(width_mp * n_mp, block)
    embed_rows = vocab_embed.reshape(vocab_mp * n_mp, block)
    gain = norm_gain.reshape(1, block)
    quarter = vocab_mp // 4

    h = jnp.concatenate(gather_direct(hidden_rows, "dp"), axis=0)
    weight = relayout(weight_rows, n_mp, 0, width_mp, None, [])
    own_h = lax.dynamic_slice_in_dim(h, dp_index * block, block, 1)

    def reduce_blocks(products, fillers):
        terms = {}
        for group, (odd, even) in products:
            arrived = swap(odd, "mp", 1)
            for i, s in enumerate(group):
                terms[s] = [(even, i), (arrived, i)]
        done, filled = 1, []
        for bit in mp_bits[1:]:
            senders = [s for s in sorted(terms, reverse=True) if s & bit and not s & done]
            totals = [add_round(terms[s], filled) for s in senders]
            for s, total in zip(senders, totals):
                terms[s ^ bit].append((swap(total, "mp", bit), 0))
            if fillers:
                filled = [fillers.pop(0)(totals)]
            done |= bit
        return terms[0], filled

    cut = n_mp // 4
    early = project(h, weight, me, pairs[:cut])
    late = project(h, weight, me, pairs[cut:], [early[1]])
    made = []

    def fill(first, count):
        def run(deps):
            into = made[-1] if made else None
            made.append(relayout(embed_rows, n_mp, first * quarter, count * quarter, into, deps))
            return made[-1]

        return run

    parts, filled = reduce_blocks([(pairs[:cut], early), (pairs[cut:], late)], [fill(0, 1), fill(1, 2)])
    pre, x, squares = activate(parts, own_h, gain, filled)

    xs = gather_xor(x, "mp", mp_bits[::-1])
    for bit in mp_bits:
        squares = squares + swap(squares, "mp", bit)
    embed = fill(3, 1)([x])

    partial = None
    for blocks in ([0, 1], list(range(2, n_mp - 2))):
        [partial] = project_vocab({s: xs[s] for s in blocks}, embed, me, partial, 1, 0, vocab_mp)
    half = vocab_mp // 2
    pieces = []
    for i in range(2):
        last = project_vocab(
            {s: xs[s] for s in (n_mp - 2, n_mp - 1)}, embed, me, partial, n_dp, i * half, half
        )
        pieces.append(scatter_xor({s: [p] for s, p in enumerate(last)}, "dp", orders[i]))

    squares = squares[0].reshape(n_dp, tok_dp)
    for bit in dp_bits:
        arrived = swap(squares, "dp", bit)
        squares = squares + jnp.stack([arrived[s ^ bit] for s in range(n_dp)])
    squares = column(squares[0])
    local = lax.dynamic_slice_in_dim(targets, dp_index * tok_dp, tok_dp, 0) - mp_index * vocab_mp
    local = column(local)
    *own_q, stats = softmax(pieces, squares, local, width)
    q = [gather_xor(own_q[i], "dp", orders[i]) for i in range(2)]
    stats = hold(stats, [q[0][orders[0][0]]])
    packed = merge(gather_direct(stats, "mp"), squares, local, tokens, width)
    packs = jnp.concatenate(gather_direct(packed, "dp"), axis=0)
    sums = [jnp.sum(packs[s * tok_dp : (s + 1) * tok_dp, 5]) for s in range(n_dp)]
    loss = tree(jnp.add, sums) / tokens

    dlogits = scale_rows([[q[0][s], q[1][s]] for s in range(n_dp)], packs)
    products, deps = [], []
    for pair in pairs:
        product = project(dlogits, embed, me, [pair], deps)
        deps = [product[1]]
        products.append(([pair], product))
    parts, _ = reduce_blocks(products, [])
    dpre = grad_pre(parts, packs, pre, own_h, gain)
    grad = weight_grad(h.T, gather_xor(dpre, "mp", mp_bits[::-1]), me)
    return (grad.reshape(head_weight.shape), loss)


def solution(mesh):
    return jax.shard_map(
        on_device,
        mesh=mesh,
        in_specs=(
            P("dp", "mp"),
            P("mp", None, "dp", None),
            P("mp", "dp", None),
            P("mp", None, "dp", None),
            P(),
        ),
        out_specs=(P("mp", None, "dp", None), P()),
        check_vma=False,
    )
```

time: 298 us -> 302 us (1.013)
  Pallas kernels: 62.8 us -> 143 us
  local copies, waits for them, and re-layouts: 44.8 us -> 4.12 us
  waiting for transfers between devices: 115 us -> 90.7 us
  starting transfers between devices: 64.7 us -> 50.9 us
    pallas_call x7 -> x23, Pallas kernels: 44.4 us -> 126 us  [the longest x4 60.3 us: relayout(): pl.pallas_call(functools.partial(relayout_kernel, n, len(skipped)), out_s...]
    unnamed x24 -> x33, local copies, waits for them, and re-layouts: 42.4 us -> 2.13 us
    ppermute x55 -> x56, waiting for transfers between devices: 115 us -> 90.7 us  [swap(): return lax.ppermute(value, axis, [(i, i ^ bit) for i in range(n)])]
    ppermute x55 -> x56, starting transfers between devices: 64.7 us -> 50.9 us  [swap(): return lax.ppermute(value, axis, [(i, i ^ bit) for i in range(n)])]
  transfers between devices with their start and end apart: 55 -> 56, of which waited for: 26 -> 17; matrix products, arithmetic and copies ran while one was open for 14% -> 2% of each run, Pallas kernels for 11% -> 38%
where the time goes in v2:
time: 302 us; the launch traced here: 300 us
  Pallas kernels  143 us (47%)
  waiting for transfers between devices  90.7 us (30%)
  starting transfers between devices  50.9 us (17%)
  other arithmetic  6.43 us (2%)
  between operations  4.84 us (2%)
  local copies, waits for them, and re-layouts  4.12 us (1%)
    ppermute x56, waiting for transfers between devices, swap(): return lax.ppermute(value, axis, [(i, i ^ bit) for i in range(n)])  90.7 us
    pallas_call x4, Pallas kernels, relayout(): pl.pallas_call(functools.partial(relayout_kernel, n, len(skipped)), out_s...  60.3 us
    ppermute x56, starting transfers between devices, swap(): return lax.ppermute(value, axis, [(i, i ^ bit) for i in range(n)])  50.9 us
    pallas_call x6, Pallas kernels, project(): pl.pallas_call(functools.partial(project_kernel, len(deps)), out_shape=[j...  37.6 us
    pallas_call x4, Pallas kernels, project_vocab(): pl.pallas_call(functools.partial(logits_kernel, n, n_out), out_shape=[jax...  26.7 us
    pallas_call x1, Pallas kernels, weight_grad(): pl.pallas_call(functools.partial(grad_kernel, order), out_shape=jax.Shape...  14.3 us
  transfers between devices with their start and end apart: 56, of which 17 were waited for; matrix products, arithmetic and copies ran while one was open for 2% of the time, Pallas kernels for 38%

profile of v2, /device:TPU:1, one launch (start us, length us, event | category | flops | bytes accessed | tf_op | source)
XLA Modules:
  0.0 299.9 jit_solution(15777458170981299923)
XLA Ops:
  1.9 3.1 %collective-permute-start.2 = (bf16[64,2048]{0,1:T(8,128)(2,1)S(1)}, bf16[64,2048]{0,1:T(8,128)(2,1)S(1)}, u32[]{:S(2)}, u32[]{:S(2)}) collective-permute-start(bf16[64,2048]{0,1:T(8,128)(2,1)S(1)} %copy.18), channel_id=1, source_target_pairs={{0,24},{8,16},{16,8},{24,0},{1,25},{9,17},{17,9},{25,1},{2,26},{10... | collective-permute-start | bytes 786440 | tf_op jit(solution)/shard_map/ppermute | solution.py:27
  5.3 19.7 %shard_map.122.w = bf16[8,2048,512]{2,1,0:T(8,128)(2,1)} custom-call(bf16[16384,512]{1,0:T(8,128)(2,1)} %bitcast.16), custom_call_target="tpu_custom_call" | custom-call | bytes 33554432 | tf_op jit(solution)/shard_map/pallas_call | solution.py:75
  25.1 3.6 %collective-permute-done.1 = bf16[64,2048]{0,1:T(8,128)(2,1)S(1)} collective-permute-done((bf16[64,2048]{0,1:T(8,128)(2,1)S(1)}, bf16[64,2048]{0,1:T(8,128)(2,1)S(1)}, u32[]{:S(2)}, u32[]{:S(2)}) %collective-permute-start.1) | collective-permute-done | bytes 262176 | tf_op jit(solution)/shard_map/ppermute | solution.py:27
  31.9 6.1 %shard_map.123 = (bf16[2,256,512]{2,1,0:T(8,128)(2,1)S(1)}, f32[2,256,512]{2,1,0:T(8,128)S(1)}) custom-call(s32[4]{0:T(128)S(1)} %get-tuple-element.62.ks, bf16[256,2048]{1,0:T(8,128)(2,1)S(1)} %copy.20.lhs, bf16[8,2048,512]{2,1,0:T(8,128)(2,1)} %shard_map.122.w), custom_call_target="tpu_custom_call" | custom-call | flops 2147483648 | bytes 8388608 | tf_op jit(solution)/shard_map/pallas_call | solution.py:119
  38.5 6.1 %shard_map.124 = (bf16[2,256,512]{2,1,0:T(8,128)(2,1)S(1)}, f32[2,256,512]{2,1,0:T(8,128)S(1)}) custom-call(s32[4]{0:T(128)S(1)} %get-tuple-element.63.ks, bf16[256,2048]{1,0:T(8,128)(2,1)S(1)} %copy.20.lhs, bf16[8,2048,512]{2,1,0:T(8,128)(2,1)} %shard_map.122.w, f32[2,256,512]{2,1,0:T(8,128)S(1)} %get-tuple-element.28.refs_0_), custom_call_target="tpu_custom_call" | custom-call | flops 2147483648 | bytes 8388608 | tf_op jit(solution)/shard_map/pallas_call | solution.py:119
  48.2 10.4 %shard_map.127.refs_3_.refs_0_ = bf16[8,4096,512]{2,1,0:T(8,128)(2,1)} custom-call(bf16[32768,512]{1,0:T(8,128)(2,1)} %bitcast.13, bf16[1,256,512]{2,1,0:T(8,128)(2,1)S(1)} %shard_map.126.refs_0_, bf16[1,256,512]{2,1,0:T(8,128)(2,1)S(1)} %shard_map.125.refs_1_), custom_call_target="tpu_custom_call" | custom-call | bytes 16777216 | tf_op jit(solution)/shard_map/pallas_call | solution.py:75
  62.2 19.7 %shard_map.129.refs_4_.refs_0_ = bf16[8,4096,512]{2,1,0:T(8,128)(2,1)} custom-call(bf16[32768,512]{1,0:T(8,128)(2,1)} %bitcast.14, bf16[8,4096,512]{2,1,0:T(8,128)(2,1)} %shard_map.127.refs_3_.refs_0_, bf16[1,256,512]{2,1,0:T(8,128)(2,1)S(1)} %shard_map.128.refs_1_), custom_call_target="tpu_custom_call", output_to_operand_aliasing={{}: (1, {})} | custom-call | bytes 33554432 | tf_op jit(solution)/shard_map/pallas_call | solution.py:75
  86.4 6.9 %collective-permute-done.22 = f32[8,256]{1,0:T(8,128)S(1)} collective-permute-done((f32[8,256]{1,0:T(8,128)S(1)}, f32[8,256]{1,0:T(8,128)S(1)}, u32[]{:S(2)}, u32[]{:S(2)}) %collective-permute-start.22) | collective-permute-done | bytes 8224 | tf_op jit(solution)/shard_map/ppermute | solution.py:27
  93.3 3.0 collective-permute-start.23
  96.2 10.5 %shard_map.131.refs_2_.refs_3_.refs_4_.refs_5_.refs_6_.refs_7_.w = bf16[8,4096,512]{2,1,0:T(8,128)(2,1)} custom-call(bf16[32768,512]{1,0:T(8,128)(2,1)} %bitcast.15, bf16[8,4096,512]{2,1,0:T(8,128)(2,1)} %shard_map.129.refs_4_.refs_0_, bf16[256,512]{1,0:T(8,128)(2,1)S(1)} %get-tuple-element.32.refs_1_.refs_0_), custom_call_target="tpu_custom_call", output_to_operand_aliasing={{}: (1, {})} | custom-call | bytes 16777216 | tf_op jit(solution)/shard_map/pallas_call | solution.py:75
  110.7 7.6 %shard_map.132.refs_8_ = f32[256,4096]{1,0:T(8,128)S(1)} custom-call(s32[1]{0:T(128)} %bitcast.me, bf16[256,512]{1,0:T(8,128)(2,1)S(1)} %get-tuple-element.32.refs_1_.refs_0_, bf16[256,512]{1,0:T(8,128)(2,1)S(1)} %collective-permute-done.14.refs_1_, bf16[8,4096,512]{2,1,0:T(8,128)(2,1)} %shard_map.131.refs_2_.refs_3_.refs_4_.refs_5_.refs_6_.refs_7_.w, ...), custom_call_target="tpu_custom_call" | custom-call | flops 2147483648 | bytes 16777216 | tf_op jit(solution)/shard_map/pallas_call | solution.py:217
  118.9 10.6 %shard_map.133.refs_4_ = f32[256,4096]{1,0:T(8,128)S(1)} custom-call(s32[1]{0:T(128)} %bitcast.me, bf16[256,512]{1,0:T(8,128)(2,1)S(1)} %collective-permute-done.11.refs_0_, bf16[256,512]{1,0:T(8,128)(2,1)S(1)} %collective-permute-done.12.refs_1_, bf16[256,512]{1,0:T(8,128)(2,1)S(1)} %collective-permute-done.8.refs_2_, ...), custom_call_target="tpu_custom_call" | custom-call | flops 4294967296 | bytes 25165824 | tf_op jit(solution)/shard_map/pallas_call | solution.py:217
  129.5 4.2 %shard_map.135 = (f32[64,2048]{1,0:T(8,128)S(1)}, f32[64,2048]{1,0:T(8,128)S(1)}, f32[64,2048]{1,0:T(8,128)S(1)}, f32[64,2048]{1,0:T(8,128)S(1)}) custom-call(s32[1]{0:T(128)} %bitcast.me, bf16[256,512]{1,0:T(8,128)(2,1)S(1)} %collective-permute-done.9.refs_0_, bf16[256,512]{1,0:T(8,128)(2,1)S(1)} %collective-permute-done.10.refs_1_, ...), custom_call_target="tpu_custom_call" | custom-call | flops 1073741824 | bytes 8388608 | tf_op jit(solution)/shard_map/pallas_call | solution.py:217
  134.3 4.3 %shard_map.134 = (f32[64,2048]{1,0:T(8,128)S(1)}, f32[64,2048]{1,0:T(8,128)S(1)}, f32[64,2048]{1,0:T(8,128)S(1)}, f32[64,2048]{1,0:T(8,128)S(1)}) custom-call(s32[1]{0:T(128)} %bitcast.me, bf16[256,512]{1,0:T(8,128)(2,1)S(1)} %collective-permute-done.9.refs_0_, bf16[256,512]{1,0:T(8,128)(2,1)S(1)} %collective-permute-done.10.refs_1_, ...), custom_call_target="tpu_custom_call" | custom-call | flops 1073741824 | bytes 8388608 | tf_op jit(solution)/shard_map/pallas_call | solution.py:217
  141.7 5.5 %collective-permute-done.19 = f32[64,2048]{1,0:T(8,128)S(1)} collective-permute-done((f32[64,2048]{1,0:T(8,128)S(1)}, f32[64,2048]{1,0:T(8,128)S(1)}, u32[]{:S(2)}, u32[]{:S(2)}) %collective-permute-start.19) | collective-permute-done | bytes 524320 | tf_op jit(solution)/shard_map/ppermute | solution.py:27
  147.6 4.2 %collective-permute-done.16 = f32[64,2048]{1,0:T(8,128)S(1)} collective-permute-done((f32[64,2048]{1,0:T(8,128)S(1)}, f32[64,2048]{1,0:T(8,128)S(1)}, u32[]{:S(2)}, u32[]{:S(2)}) %collective-permute-start.16) | collective-permute-done | bytes 524320 | tf_op jit(solution)/shard_map/ppermute | solution.py:27
  153.0 5.5 %collective-permute-done.18.refs_4_ = f32[64,2048]{1,0:T(8,128)S(1)} collective-permute-done((f32[64,2048]{1,0:T(8,128)S(1)}, f32[64,2048]{1,0:T(8,128)S(1)}, u32[]{:S(2)}, u32[]{:S(2)}) %collective-permute-start.18) | collective-permute-done | bytes 524320 | tf_op jit(solution)/shard_map/ppermute | solution.py:27
  158.5 4.5 %collective-permute-done.15.refs_1_ = f32[64,2048]{1,0:T(8,128)S(1)} collective-permute-done((f32[64,2048]{1,0:T(8,128)S(1)}, f32[64,2048]{1,0:T(8,128)S(1)}, u32[]{:S(2)}, u32[]{:S(2)}) %collective-permute-start.15) | collective-permute-done | bytes 524320 | tf_op jit(solution)/shard_map/ppermute | solution.py:27
  163.0 11.2 %collective-permute-done.20.refs_5_ = f32[64,2048]{1,0:T(8,128)S(1)} collective-permute-done((f32[64,2048]{1,0:T(8,128)S(1)}, f32[64,2048]{1,0:T(8,128)S(1)}, u32[]{:S(2)}, u32[]{:S(2)}) %collective-permute-start.20) | collective-permute-done | bytes 524320 | tf_op jit(solution)/shard_map/ppermute | solution.py:27
  176.2 5.6 %collective-permute-done.26.refs_0_.refs_2_ = bf16[64,2048]{1,0:T(8,128)(2,1)S(1)} collective-permute-done((bf16[64,2048]{1,0:T(8,128)(2,1)S(1)}, bf16[64,2048]{1,0:T(8,128)(2,1)S(1)}, u32[]{:S(2)}, u32[]{:S(2)}) %collective-permute-start.26) | collective-permute-done | bytes 262176 | tf_op jit(solution)/shard_map/ppermute | solution.py:27
  181.8 2.8 collective-permute-start.38
  201.8 9.7 %collective-permute-done.39 = f32[64,128]{1,0:T(8,128)S(1)} collective-permute-done((f32[64,128]{1,0:T(8,128)S(1)}, f32[64,128]{1,0:T(8,128)S(1)}, u32[]{:S(2)}, u32[]{:S(2)}) %collective-permute-start.39) | collective-permute-done | bytes 32800 | tf_op jit(solution)/shard_map/ppermute | solution.py:27
  212.5 6.3 %shard_map.140 = (bf16[1,256,512]{2,1,0:T(8,128)(2,1)S(1)}, f32[1,256,512]{2,1,0:T(8,128)S(1)}) custom-call(s32[2]{0:T(128)S(1)} %get-tuple-element.64.ks, bf16[256,4096]{1,0:T(8,128)(2,1)S(1)} %shard_map.139.lhs, bf16[8,4096,512]{2,1,0:T(8,128)(2,1)} %shard_map.131.refs_2_.refs_3_.refs_4_.refs_5_.refs_6_.refs_7_.w), custom_call_target="tpu_custom_call" | custom-call | flops 2147483648 | bytes 8388608 | tf_op jit(solution)/shard_map/pallas_call | solution.py:119
  218.8 2.5 collective-permute-start.46
  221.3 6.3 %shard_map.141 = (bf16[1,256,512]{2,1,0:T(8,128)(2,1)S(1)}, f32[1,256,512]{2,1,0:T(8,128)S(1)}) custom-call(s32[2]{0:T(128)S(1)} %get-tuple-element.65.ks, bf16[256,4096]{1,0:T(8,128)(2,1)S(1)} %shard_map.139.lhs, bf16[8,4096,512]{2,1,0:T(8,128)(2,1)} %shard_map.131.refs_2_.refs_3_.refs_4_.refs_5_.refs_6_.refs_7_.w, f32[1,256,512]{2,1,0:T(8,128)S(1)} %get-tuple-element.45.refs_0_), custom_call_target="tpu_custom_call" | custom-call | flops 2147483648 | bytes 8388608 | tf_op jit(solution)/shard_map/pallas_call | solution.py:119
  227.6 6.3 %shard_map.142 = (bf16[1,256,512]{2,1,0:T(8,128)(2,1)S(1)}, f32[1,256,512]{2,1,0:T(8,128)S(1)}) custom-call(s32[2]{0:T(128)S(1)} %get-tuple-element.66.ks, bf16[256,4096]{1,0:T(8,128)(2,1)S(1)} %shard_map.139.lhs, bf16[8,4096,512]{2,1,0:T(8,128)(2,1)} %shard_map.131.refs_2_.refs_3_.refs_4_.refs_5_.refs_6_.refs_7_.w, f32[1,256,512]{2,1,0:T(8,128)S(1)} %get-tuple-element.46.refs_0_), custom_call_target="tpu_custom_call" | custom-call | flops 2147483648 | bytes 8388608 | tf_op jit(solution)/shard_map/pallas_call | solution.py:119
  235.6 6.3 %shard_map.143 = (bf16[1,256,512]{2,1,0:T(8,128)(2,1)S(1)}, f32[1,256,512]{2,1,0:T(8,128)S(1)}) custom-call(s32[2]{0:T(128)S(1)} %get-tuple-element.67.ks, bf16[256,4096]{1,0:T(8,128)(2,1)S(1)} %shard_map.139.lhs, bf16[8,4096,512]{2,1,0:T(8,128)(2,1)} %shard_map.131.refs_2_.refs_3_.refs_4_.refs_5_.refs_6_.refs_7_.w, f32[1,256,512]{2,1,0:T(8,128)S(1)} %get-tuple-element.47.refs_0_), custom_call_target="tpu_custom_call" | custom-call | flops 2147483648 | bytes 8388608 | tf_op jit(solution)/shard_map/pallas_call | solution.py:119
  243.9 10.3 %collective-permute-done.44.refs_2_ = bf16[1,256,512]{2,1,0:T(8,128)(2,1)S(1)} collective-permute-done((bf16[1,256,512]{2,1,0:T(8,128)(2,1)S(1)}, bf16[1,256,512]{2,1,0:T(8,128)(2,1)S(1)}, u32[]{:S(2)}, u32[]{:S(2)}) %collective-permute-start.44) | collective-permute-done | bytes 262176 | tf_op jit(solution)/shard_map/ppermute | solution.py:27
  254.2 3.0 %collective-permute-done.48.refs_3_ = bf16[1,256,512]{2,1,0:T(8,128)(2,1)S(1)} collective-permute-done((bf16[1,256,512]{2,1,0:T(8,128)(2,1)S(1)}, bf16[1,256,512]{2,1,0:T(8,128)(2,1)S(1)}, u32[]{:S(2)}, u32[]{:S(2)}) %collective-permute-start.48) | collective-permute-done | bytes 262176 | tf_op jit(solution)/shard_map/ppermute | solution.py:27
  257.8 13.2 %collective-permute-done.52.refs_4_ = bf16[256,512]{1,0:T(8,128)(2,1)S(1)} collective-permute-done((bf16[256,512]{1,0:T(8,128)(2,1)S(1)}, bf16[256,512]{1,0:T(8,128)(2,1)S(1)}, u32[]{:S(2)}, u32[]{:S(2)}) %collective-permute-start.52) | collective-permute-done | bytes 262176 | tf_op jit(solution)/shard_map/ppermute | solution.py:27
  274.6 3.8 %collective-permute-done.54.refs_6_ = bf16[256,512]{1,0:T(8,128)(2,1)S(1)} collective-permute-done((bf16[256,512]{1,0:T(8,128)(2,1)S(1)}, bf16[256,512]{1,0:T(8,128)(2,1)S(1)}, u32[]{:S(2)}, u32[]{:S(2)}) %collective-permute-start.54) | collective-permute-done | bytes 262176 | tf_op jit(solution)/shard_map/ppermute | solution.py:27
  284.5 14.3 %shard_map.148 = bf16[16384,512]{1,0:T(8,128)(2,1)} custom-call(s32[1]{0:T(128)} %bitcast.me, bf16[2048,256]{1,0:T(8,128)(2,1)S(1)} %fusion.3.h, bf16[256,512]{1,0:T(8,128)(2,1)S(1)} %shard_map.147.refs_0_, bf16[256,512]{1,0:T(8,128)(2,1)S(1)} %collective-permute-done.49.refs_1_, bf16[256,512]{1,0:T(8,128)(2,1)S(1)} %collective-permute-done.50.refs_2_, ...), custom_call_target="tpu_custom_call" | custom-call | flops 4294967296 | bytes 16777216 | tf_op jit(solution)/shard_map/pallas_call | solution.py:407
  (167 shorter events, 57.7 us)
Async XLA Ops:
  1.9 23.2 %collective-permute-start.2 = (bf16[64,2048]{0,1:T(8,128)(2,1)S(1)}, bf16[64,2048]{0,1:T(8,128)(2,1)S(1)}, u32[]{:S(2)}, u32[]{:S(2)}) collective-permute-start(bf16[64,2048]{0,1:T(8,128)(2,1)S(1)} %copy.18), channel_id=1, source_target_pairs={{0,24},{8,16},{16,8},{24,0},{1,25},{9,17},{17,9},{25,1},{2,26},{10... | collective-permute-start | bytes 786440 | tf_op jit(solution)/shard_map/ppermute | solution.py:27
  4.9 23.7 %collective-permute-start.1 = (bf16[64,2048]{0,1:T(8,128)(2,1)S(1)}, bf16[64,2048]{0,1:T(8,128)(2,1)S(1)}, u32[]{:S(2)}, u32[]{:S(2)}) collective-permute-start(bf16[64,2048]{0,1:T(8,128)(2,1)S(1)} %copy.18), channel_id=1, source_target_pairs={{0,16},{8,24},{16,0},{24,8},{1,17},{9,25},{17,1},{25,9},{2,18},{10... | collective-permute-start | bytes 786440 | tf_op jit(solution)/shard_map/ppermute | solution.py:27
  5.2 23.5 %collective-permute-start = (bf16[64,2048]{0,1:T(8,128)(2,1)S(1)}, bf16[64,2048]{0,1:T(8,128)(2,1)}, u32[]{:S(2)}, u32[]{:S(2)}) collective-permute-start(bf16[64,2048]{0,1:T(8,128)(2,1)S(1)} %copy.18), channel_id=1, source_target_pairs={{0,8},{8,0},{16,24},{24,16},{1,9},{9,1},{17,25},{25,17},{2,10},{10... | collective-permute-start | bytes 786440 | tf_op jit(solution)/shard_map/ppermute | solution.py:27
  44.9 13.8 %collective-permute-start.6 = (bf16[1,256,512]{2,1,0:T(8,128)(2,1)S(1)}, bf16[1,256,512]{2,1,0:T(8,128)(2,1)S(1)}, u32[]{:S(2)}, u32[]{:S(2)}) collective-permute-start(bf16[1,256,512]{2,1,0:T(8,128)(2,1)S(1)} %shard_map.126.refs_0_), channel_id=1, source_target_pairs={{0,2},{1,3},{2,0},{3,1},{4,6},{5,7},{6,4},{7,5},{8,10},{9,11},{10,... | collective-permute-start | bytes 786440 | tf_op jit(solution)/shard_map/ppermute | solution.py:27
  46.7 35.3 %collective-permute-start.4 = (bf16[1,256,512]{2,1,0:T(8,128)(2,1)S(1)}, bf16[1,256,512]{2,1,0:T(8,128)(2,1)S(1)}, u32[]{:S(2)}, u32[]{:S(2)}) collective-permute-start(bf16[1,256,512]{2,1,0:T(8,128)(2,1)S(1)} %shard_map.125.refs_1_), channel_id=1, source_target_pairs={{0,2},{1,3},{2,0},{3,1},{4,6},{5,7},{6,4},{7,5},{8,10},{9,11},{10,... | collective-permute-start | bytes 786440 | tf_op jit(solution)/shard_map/ppermute | solution.py:27
  58.8 23.2 %collective-permute-start.7 = (bf16[1,256,512]{2,1,0:T(8,128)(2,1)S(1)}, bf16[1,256,512]{2,1,0:T(8,128)(2,1)S(1)}, u32[]{:S(2)}, u32[]{:S(2)}) collective-permute-start(bf16[1,256,512]{2,1,0:T(8,128)(2,1)S(1)} %shard_map.128.refs_1_), channel_id=1, source_target_pairs={{0,4},{1,5},{2,6},{3,7},{4,0},{5,1},{6,2},{7,3},{8,12},{9,13},{10,... | collective-permute-start | bytes 786440 | tf_op jit(solution)/shard_map/ppermute | solution.py:27
  82.4 24.4 %collective-permute-start.8 = (bf16[256,512]{1,0:T(8,128)(2,1)S(1)}, bf16[256,512]{1,0:T(8,128)(2,1)S(1)}, u32[]{:S(2)}, u32[]{:S(2)}) collective-permute-start(bf16[256,512]{1,0:T(8,128)(2,1)S(1)} %get-tuple-element.32.refs_1_.refs_0_), channel_id=1, source_target_pairs={{0,4},{1,5},{2,6},{3,7},{4,0},{5,1},{6,2},{7,3},{8,12},{9,13},{10,... | collective-permute-start | bytes 786440 | tf_op jit(solution)/shard_map/ppermute | solution.py:27
  82.4 26.6 %collective-permute-start.11 = (bf16[256,512]{1,0:T(8,128)(2,1)S(1)}, bf16[256,512]{1,0:T(8,128)(2,1)S(1)}, u32[]{:S(2)}, u32[]{:S(2)}) collective-permute-start(bf16[256,512]{1,0:T(8,128)(2,1)S(1)} %get-tuple-element.32.refs_1_.refs_0_), channel_id=1, source_target_pairs={{0,2},{1,3},{2,0},{3,1},{4,6},{5,7},{6,4},{7,5},{8,10},{9,11},{10,... | collective-permute-start | bytes 786440 | tf_op jit(solution)/shard_map/ppermute | solution.py:27
  82.6 28.1 %collective-permute-start.14 = (bf16[256,512]{1,0:T(8,128)(2,1)S(1)}, bf16[256,512]{1,0:T(8,128)(2,1)S(1)}, u32[]{:S(2)}, u32[]{:S(2)}) collective-permute-start(bf16[256,512]{1,0:T(8,128)(2,1)S(1)} %get-tuple-element.32.refs_1_.refs_0_), channel_id=1, source_target_pairs={{0,1},{1,0},{2,3},{3,2},{4,5},{5,4},{6,7},{7,6},{8,9},{9,8},{10,11... | collective-permute-start | bytes 786440 | tf_op jit(solution)/shard_map/ppermute | solution.py:27
  93.3 16.1 %collective-permute-start.23 = (f32[8,256]{1,0:T(8,128)S(1)}, f32[8,256]{1,0:T(8,128)S(1)}, u32[]{:S(2)}, u32[]{:S(2)}) collective-permute-start(f32[8,256]{1,0:T(8,128)S(1)} %add.40), channel_id=1, source_target_pairs={{0,4},{1,5},{2,6},{3,7},{4,0},{5,1},{6,2},{7,3},{8,12},{9,13},{10,... | collective-permute-start | bytes 24584 | tf_op jit(solution)/shard_map/ppermute | solution.py:27
  106.7 12.2 %collective-permute-start.13 = (bf16[256,512]{1,0:T(8,128)(2,1)S(1)}, bf16[256,512]{1,0:T(8,128)(2,1)S(1)}, u32[]{:S(2)}, u32[]{:S(2)}) collective-permute-start(bf16[256,512]{1,0:T(8,128)(2,1)S(1)} %collective-permute-done.8.refs_2_), channel_id=1, source_target_pairs={{0,1},{1,0},{2,3},{3,2},{4,5},{5,4},{6,7},{7,6},{8,9},{9,8},{10,11... | collective-permute-start | bytes 786440 | tf_op jit(solution)/shard_map/ppermute | solution.py:27
  109.5 30.1 %collective-permute-start.24 = (f32[4,64]{1,0:T(4,128)S(1)}, f32[4,64]{1,0:T(4,128)S(1)}, u32[]{:S(2)}, u32[]{:S(2)}) collective-permute-start(f32[4,64]{1,0:T(4,128)S(1)} %reshape_squeeze.3), channel_id=1, source_target_pairs={{0,8},{8,0},{16,24},{24,16},{1,9},{9,1},{17,25},{25,17},{2,10},{10... | collective-permute-start | bytes 3080 | tf_op jit(solution)/shard_map/ppermute | solution.py:27
  118.4 11.1 %collective-permute-start.10 = (bf16[256,512]{1,0:T(8,128)(2,1)S(1)}, bf16[256,512]{1,0:T(8,128)(2,1)S(1)}, u32[]{:S(2)}, u32[]{:S(2)}) collective-permute-start(bf16[256,512]{1,0:T(8,128)(2,1)S(1)} %collective-permute-done.9.refs_0_), channel_id=1, source_target_pairs={{0,1},{1,0},{2,3},{3,2},{4,5},{5,4},{6,7},{7,6},{8,9},{9,8},{10,11... | collective-permute-start | bytes 786440 | tf_op jit(solution)/shard_map/ppermute | solution.py:27
  133.7 13.5 %collective-permute-start.19 = (f32[64,2048]{1,0:T(8,128)S(1)}, f32[64,2048]{1,0:T(8,128)S(1)}, u32[]{:S(2)}, u32[]{:S(2)}) collective-permute-start(f32[64,2048]{1,0:T(8,128)S(1)} %get-tuple-element.40), channel_id=1, source_target_pairs={{0,16},{8,24},{16,0},{24,8},{1,17},{9,25},{17,1},{25,9},{2,18},{10... | collective-permute-start | bytes 1572872 | tf_op jit(solution)/shard_map/ppermute | solution.py:27
  138.6 13.2 %collective-permute-start.16 = (f32[64,2048]{1,0:T(8,128)S(1)}, f32[64,2048]{1,0:T(8,128)S(1)}, u32[]{:S(2)}, u32[]{:S(2)}) collective-permute-start(f32[64,2048]{1,0:T(8,128)S(1)} %get-tuple-element.36), channel_id=1, source_target_pairs={{0,8},{8,0},{16,24},{24,16},{1,9},{9,1},{17,25},{25,17},{2,10},{10... | collective-permute-start | bytes 1572872 | tf_op jit(solution)/shard_map/ppermute | solution.py:27
  139.7 13.3 %collective-permute-start.25 = (f32[4,64]{1,0:T(4,128)S(1)}, f32[4,64]{1,0:T(4,128)S(1)}, u32[]{:S(2)}, u32[]{:S(2)}) collective-permute-start(f32[4,64]{1,0:T(4,128)S(1)} %maximum_add_fusion), channel_id=1, source_target_pairs={{0,16},{8,24},{16,0},{24,8},{1,17},{9,25},{17,1},{25,9},{2,18},{10... | collective-permute-start | bytes 3080 | tf_op jit(solution)/shard_map/ppermute | solution.py:27
  140.0 18.5 %collective-permute-start.18 = (f32[64,2048]{1,0:T(8,128)S(1)}, f32[64,2048]{1,0:T(8,128)S(1)}, u32[]{:S(2)}, u32[]{:S(2)}) collective-permute-start(f32[64,2048]{1,0:T(8,128)S(1)} %get-tuple-element.38), channel_id=1, source_target_pairs={{0,16},{8,24},{16,0},{24,8},{1,17},{9,25},{17,1},{25,9},{2,18},{10... | collective-permute-start | bytes 1572872 | tf_op jit(solution)/shard_map/ppermute | solution.py:27
  141.3 21.8 %collective-permute-start.15 = (f32[64,2048]{1,0:T(8,128)S(1)}, f32[64,2048]{1,0:T(8,128)S(1)}, u32[]{:S(2)}, u32[]{:S(2)}) collective-permute-start(f32[64,2048]{1,0:T(8,128)S(1)} %get-tuple-element.34), channel_id=1, source_target_pairs={{0,8},{8,0},{16,24},{24,16},{1,9},{9,1},{17,25},{25,17},{2,10},{10... | collective-permute-start | bytes 1572872 | tf_op jit(solution)/shard_map/ppermute | solution.py:27
  147.3 27.0 %collective-permute-start.20 = (f32[64,2048]{1,0:T(8,128)S(1)}, f32[64,2048]{1,0:T(8,128)S(1)}, u32[]{:S(2)}, u32[]{:S(2)}) collective-permute-start(f32[64,2048]{1,0:T(8,128)S(1)} %add.38), channel_id=1, source_target_pairs={{0,8},{8,0},{16,24},{24,16},{1,9},{9,1},{17,25},{25,17},{2,10},{10... | collective-permute-start | bytes 1572872 | tf_op jit(solution)/shard_map/ppermute | solution.py:27
  151.9 22.4 %collective-permute-start.17 = (f32[64,2048]{1,0:T(8,128)S(1)}, f32[64,2048]{1,0:T(8,128)S(1)}, u32[]{:S(2)}, u32[]{:S(2)}) collective-permute-start(f32[64,2048]{1,0:T(8,128)S(1)} %add.37), channel_id=1, source_target_pairs={{0,16},{8,24},{16,0},{24,8},{1,17},{9,25},{17,1},{25,9},{2,18},{10... | collective-permute-start | bytes 1572872 | tf_op jit(solution)/shard_map/ppermute | solution.py:27
  187.1 12.3 %collective-permute-start.29 = (bf16[64,2048]{1,0:T(8,128)(2,1)S(1)}, bf16[64,2048]{1,0:T(8,128)(2,1)S(1)}, u32[]{:S(2)}, u32[]{:S(2)}) collective-permute-start(bf16[64,2048]{1,0:T(8,128)(2,1)S(1)} %get-tuple-element.43.refs_1_), channel_id=1, source_target_pairs={{0,16},{8,24},{16,0},{24,8},{1,17},{9,25},{17,1},{25,9},{2,18},{10... | collective-permute-start | bytes 786440 | tf_op jit(solution)/shard_map/ppermute | solution.py:27
  197.5 14.0 %collective-permute-start.28 = (bf16[64,2048]{1,0:T(8,128)(2,1)S(1)}, bf16[64,2048]{1,0:T(8,128)(2,1)S(1)}, u32[]{:S(2)}, u32[]{:S(2)}) collective-permute-start(bf16[64,2048]{1,0:T(8,128)(2,1)S(1)} %get-tuple-element.42.refs_0_), channel_id=1, source_target_pairs={{0,16},{8,24},{16,0},{24,8},{1,17},{9,25},{17,1},{25,9},{2,18},{10... | collective-permute-start | bytes 786440 | tf_op jit(solution)/shard_map/ppermute | solution.py:27
  198.9 12.7 %collective-permute-start.27 = (bf16[64,2048]{1,0:T(8,128)(2,1)S(1)}, bf16[64,2048]{1,0:T(8,128)(2,1)S(1)}, u32[]{:S(2)}, u32[]{:S(2)}) collective-permute-start(bf16[64,2048]{1,0:T(8,128)(2,1)S(1)} %get-tuple-element.43.refs_1_), channel_id=1, source_target_pairs={{0,8},{8,0},{16,24},{24,16},{1,9},{9,1},{17,25},{25,17},{2,10},{10... | collective-permute-start | bytes 786440 | tf_op jit(solution)/shard_map/ppermute | solution.py:27
  199.3 12.2 %collective-permute-start.30 = (bf16[64,2048]{1,0:T(8,128)(2,1)S(1)}, bf16[64,2048]{1,0:T(8,128)(2,1)S(1)}, u32[]{:S(2)}, u32[]{:S(2)}) collective-permute-start(bf16[64,2048]{1,0:T(8,128)(2,1)S(1)} %collective-permute-done.26.refs_0_.refs_2_), channel_id=1, source_target_pairs={{0,16},{8,24},{16,0},{24,8},{1,17},{9,25},{17,1},{25,9},{2,18},{10... | collective-permute-start | bytes 786440 | tf_op jit(solution)/shard_map/ppermute | solution.py:27
  200.3 11.3 %collective-permute-start.31 = (bf16[64,2048]{1,0:T(8,128)(2,1)S(1)}, bf16[64,2048]{1,0:T(8,128)(2,1)S(1)}, u32[]{:S(2)}, u32[]{:S(2)}) collective-permute-start(bf16[64,2048]{1,0:T(8,128)(2,1)S(1)} %collective-permute-done.29.refs_5_), channel_id=1, source_target_pairs={{0,8},{8,0},{16,24},{24,16},{1,9},{9,1},{17,25},{25,17},{2,10},{10... | collective-permute-start | bytes 786440 | tf_op jit(solution)/shard_map/ppermute | solution.py:27
  200.5 11.0 %collective-permute-start.39 = (f32[64,128]{1,0:T(8,128)S(1)}, f32[64,128]{1,0:T(8,128)S(1)}, u32[]{:S(2)}, u32[]{:S(2)}) collective-permute-start(f32[64,128]{1,0:T(8,128)S(1)} %shard_map.138), channel_id=1, source_target_pairs={{0,8},{8,0},{16,24},{24,16},{1,9},{9,1},{17,25},{25,17},{2,10},{10... | collective-permute-start | bytes 98312 | tf_op jit(solution)/shard_map/ppermute | solution.py:27
  218.8 15.7 %collective-permute-start.46 = (bf16[1,256,512]{2,1,0:T(8,128)(2,1)S(1)}, bf16[1,256,512]{2,1,0:T(8,128)(2,1)S(1)}, u32[]{:S(2)}, u32[]{:S(2)}) collective-permute-start(bf16[1,256,512]{2,1,0:T(8,128)(2,1)S(1)} %get-tuple-element.52), channel_id=1, source_target_pairs={{0,1},{1,0},{2,3},{3,2},{4,5},{5,4},{6,7},{7,6},{8,9},{9,8},{10,11... | collective-permute-start | bytes 786440 | tf_op jit(solution)/shard_map/ppermute | solution.py:27
  242.4 11.8 %collective-permute-start.44 = (bf16[1,256,512]{2,1,0:T(8,128)(2,1)S(1)}, bf16[1,256,512]{2,1,0:T(8,128)(2,1)S(1)}, u32[]{:S(2)}, u32[]{:S(2)}) collective-permute-start(bf16[1,256,512]{2,1,0:T(8,128)(2,1)S(1)} %shard_map.144), channel_id=1, source_target_pairs={{0,2},{1,3},{2,0},{3,1},{4,6},{5,7},{6,4},{7,5},{8,10},{9,11},{10,... | collective-permute-start | bytes 786440 | tf_op jit(solution)/shard_map/ppermute | solution.py:27
  243.1 14.1 %collective-permute-start.48 = (bf16[1,256,512]{2,1,0:T(8,128)(2,1)S(1)}, bf16[1,256,512]{2,1,0:T(8,128)(2,1)S(1)}, u32[]{:S(2)}, u32[]{:S(2)}) collective-permute-start(bf16[1,256,512]{2,1,0:T(8,128)(2,1)S(1)} %shard_map.146), channel_id=1, source_target_pairs={{0,4},{1,5},{2,6},{3,7},{4,0},{5,1},{6,2},{7,3},{8,12},{9,13},{10,... | collective-permute-start | bytes 786440 | tf_op jit(solution)/shard_map/ppermute | solution.py:27
  257.6 13.4 %collective-permute-start.52 = (bf16[256,512]{1,0:T(8,128)(2,1)S(1)}, bf16[256,512]{1,0:T(8,128)(2,1)S(1)}, u32[]{:S(2)}, u32[]{:S(2)}) collective-permute-start(bf16[256,512]{1,0:T(8,128)(2,1)S(1)} %shard_map.147.refs_0_), channel_id=1, source_target_pairs={{0,4},{1,5},{2,6},{3,7},{4,0},{5,1},{6,2},{7,3},{8,12},{9,13},{10,... | collective-permute-start | bytes 786440 | tf_op jit(solution)/shard_map/ppermute | solution.py:27
  257.8 16.2 %collective-permute-start.50 = (bf16[256,512]{1,0:T(8,128)(2,1)S(1)}, bf16[256,512]{1,0:T(8,128)(2,1)S(1)}, u32[]{:S(2)}, u32[]{:S(2)}) collective-permute-start(bf16[256,512]{1,0:T(8,128)(2,1)S(1)} %shard_map.147.refs_0_), channel_id=1, source_target_pairs={{0,2},{1,3},{2,0},{3,1},{4,6},{5,7},{6,4},{7,5},{8,10},{9,11},{10,... | collective-permute-start | bytes 786440 | tf_op jit(solution)/shard_map/ppermute | solution.py:27
  273.5 10.9 %collective-permute-start.49 = (bf16[256,512]{1,0:T(8,128)(2,1)S(1)}, bf16[256,512]{1,0:T(8,128)(2,1)S(1)}, u32[]{:S(2)}, u32[]{:S(2)}) collective-permute-start(bf16[256,512]{1,0:T(8,128)(2,1)S(1)} %shard_map.147.refs_0_), channel_id=1, source_target_pairs={{0,1},{1,0},{2,3},{3,2},{4,5},{5,4},{6,7},{7,6},{8,9},{9,8},{10,11... | collective-permute-start | bytes 786440 | tf_op jit(solution)/shard_map/ppermute | solution.py:27
  (40 other events, 542.9 us)

commit v3 on v2

v3 whole, which is shorter than its diff:
```python
import functools

import jax
import jax.numpy as jnp
from jax import lax
from jax.experimental import pallas as pl
from jax.experimental.pallas import tpu as pltpu
from jax.sharding import PartitionSpec as P

F32 = jnp.float32
BF16 = jnp.bfloat16
LANES = 128


def params(mib):
    return pltpu.CompilerParams(vmem_limit_bytes=mib * 2**20)


def bits_of(n):
    bits = [1 << i for i in range(n.bit_length() - 1)]
    assert 1 << len(bits) == n
    return bits


def swap(value, axis, bit):
    n = lax.axis_size(axis)
    return lax.ppermute(value, axis, [(i, i ^ bit) for i in range(n)])


def gather_xor(value, axis, bits):
    held = {0: value}
    for bit in bits:
        for s in list(held):
            held[s | bit] = swap(held[s], axis, bit)
    return held


def gather_rows(value, axis, bits):
    first, places = None, [0]
    for bit in bits:
        arrived = swap(value, axis, bit)
        first = arrived if first is None else first
        value = jnp.concatenate([value, arrived], axis=0)
        places = places + [s ^ bit for s in places]
    return (value, places), first


def gather_direct(value, axis):
    return [value] + [swap(value, axis, s) for s in range(1, lax.axis_size(axis))]


def scatter_xor(terms, axis, bits):
    done = 0
    for bit in bits:
        for s in sorted(terms, reverse=True):
            if s & bit and not s & done:
                total = functools.reduce(jnp.add, terms[s])
                terms[s ^ bit].append(swap(total, axis, bit))
        done |= bit
    return terms[0]


def whole(shape):
    return pl.BlockSpec(shape, lambda *_: (0,) * len(shape))


def after(deps):
    return [pl.BlockSpec(memory_space=pl.ANY)] * len(deps)


def each_tile(n, rows, run):
    group = max(1, 16 // n)

    def body(i, carry):
        run(i * group, group)
        return carry

    lax.fori_loop(0, rows // group, body, 0, unroll=8)


def relayout_kernel(n, n_skip, x, *refs):
    out, mixed = refs[n_skip:]
    rows = out.shape[1]
    lanes = range(0, x.shape[1], LANES)

    def spread(first, group):
        at = pl.multiple_of(first * n, 16)
        values = x[pl.ds(at, group * n), :].astype(F32)
        for g in range(group):
            for p in range(0, n, 8):
                part = values[g * n + p : g * n + p + 8]
                for j, lane in enumerate(lanes):
                    mixed[j, pl.ds((first + g) * (n + 1) + p, 8), :] = part[:, lane : lane + LANES]

    each_tile(n, rows, spread)
    for k in range(n):
        for j, lane in enumerate(lanes):
            out[k, :, lane : lane + LANES] = mixed[j, pl.ds(k, rows, stride=n + 1), :].astype(BF16)


def relayout(flat, n, start, rows, into, deps):
    total, block = flat.shape[0] // n, flat.shape[1]
    step = min(128, rows)
    skipped = list(deps) if into is None else [into, *deps]
    return pl.pallas_call(
        functools.partial(relayout_kernel, n, len(skipped)),
        out_shape=jax.ShapeDtypeStruct((n, total, block), BF16),
        grid=(rows // step,),
        in_specs=[pl.BlockSpec((step * n, block), lambda i: (start // step + i, 0))] + after(skipped),
        out_specs=pl.BlockSpec((n, step, block), lambda i: (0, start // step + i, 0)),
        scratch_shapes=[pltpu.VMEM((block // LANES, step * (n + 1), LANES), F32)],
        input_output_aliases={} if into is None else {1: 0},
        compiler_params=params(48),
        cost_estimate=pl.CostEstimate(flops=0, bytes_accessed=4 * rows * n * block, transcendentals=0),
    )(flat, *skipped)


def project_kernel(n, n_skip, ks, lhs, *refs):
    ws, (odd, even) = refs[:n], refs[n + n_skip :]
    total, first = 0.0, 0
    for w in ws:
        depth = w.shape[1]
        total = total + jnp.dot(lhs[:, first : first + depth], w[0], preferred_element_type=F32)
        first += depth
    is_odd = pl.program_id(0) % 2 == 0

    @pl.when(is_odd)
    def _():
        odd[0] = total.astype(odd.dtype)

    @pl.when(jnp.logical_not(is_odd))
    def _():
        even[0] = total


def project(lhs, ws, me, pairs, deps=()):
    block = ws[0].shape[2]
    rows, depth = lhs.shape
    count = len(pairs)
    ks = me ^ jnp.array([s for pair in pairs for s in (pair + 1, pair)], jnp.int32)
    return pl.pallas_call(
        functools.partial(project_kernel, len(ws), len(deps)),
        out_shape=[
            jax.ShapeDtypeStruct((count, rows, block), BF16),
            jax.ShapeDtypeStruct((count, rows, block), F32),
        ],
        grid_spec=pltpu.PrefetchScalarGridSpec(
            num_scalar_prefetch=1,
            grid=(2 * count,),
            in_specs=[whole(lhs.shape)]
            + [pl.BlockSpec((1, w.shape[1], block), lambda i, ks: (ks[i], 0, 0)) for w in ws]
            + after(deps),
            out_specs=[pl.BlockSpec((1, rows, block), lambda i, ks: (i // 2, 0, 0))] * 2,
        ),
        compiler_params=params(48),
        cost_estimate=pl.CostEstimate(
            flops=4 * count * rows * depth * block, bytes_accessed=4 * count * depth * block, transcendentals=0
        ),
    )(ks, lhs, *ws, *deps)


def pick(term, rows, block):
    array, place = term
    return pl.BlockSpec((1, rows, block), lambda *_: (place, 0, 0))


def add_kernel(n, *refs):
    out = refs[-1]
    total = refs[0][0].astype(F32)
    for ref in refs[1:n]:
        total = total + ref[0].astype(F32)
    out[0] = total.astype(out.dtype)


def add_round(terms, deps=()):
    _, rows, block = terms[0][0].shape
    return pl.pallas_call(
        functools.partial(add_kernel, len(terms)),
        out_shape=jax.ShapeDtypeStruct((1, rows, block), BF16),
        grid=(1,),
        in_specs=[pick(t, rows, block) for t in terms] + after(deps),
        out_specs=whole((1, rows, block)),
        compiler_params=params(48),
    )(*[t[0] for t in terms], *deps)


def act_kernel(n, *refs):
    parts, (h, gain, pre, x, squares) = refs[:n], refs[-5:]
    total = parts[0][0]
    for part in parts[1:]:
        total = total + part[0].astype(F32)
    pre[...] = total
    act = h[...].astype(F32) + total / (1.0 + jnp.exp(-total))
    x[...] = (act * gain[...]).astype(BF16)
    sums = jnp.broadcast_to(jnp.sum(act * act, axis=1, keepdims=True), (act.shape[0], LANES))
    squares[...] = jnp.transpose(sums)[: squares.shape[0]]


def activate(parts, h, gain, deps=()):
    rows, block = h.shape
    return pl.pallas_call(
        functools.partial(act_kernel, len(parts)),
        out_shape=[
            jax.ShapeDtypeStruct((rows, block), F32),
            jax.ShapeDtypeStruct((rows, block), BF16),
            jax.ShapeDtypeStruct((8, rows), F32),
        ],
        grid=(1,),
        in_specs=[pick(t, rows, block) for t in parts] + after(deps) + [whole(h.shape), whole(gain.shape)],
        out_specs=[whole((rows, block)), whole((rows, block)), whole((8, rows))],
        compiler_params=params(48),
    )(*[t[0] for t in parts], *deps, h, gain)


def logits_kernel(order, n_out, me, *refs):
    xs, e, outs = refs[: len(order)], refs[len(order)], refs[len(order) + 1 :]
    total = 0.0
    for s, x in zip(order, xs):
        total = total + lax.dot_general(
            x[...], e[me[0] ^ s], (((1,), (1,)), ((), ())), preferred_element_type=F32
        )
    rows = total.shape[0] // n_out
    for i, out in enumerate(outs):
        out[...] = total[i * rows : (i + 1) * rows]


def project_vocab(xs, embed, me, n_out, start, size):
    n, _, block = embed.shape
    order = sorted(xs)
    rows = xs[0].shape[0]
    step = min(512, size)
    return pl.pallas_call(
        functools.partial(logits_kernel, order, n_out),
        out_shape=[jax.ShapeDtypeStruct((rows // n_out, size), F32)] * n_out,
        grid_spec=pltpu.PrefetchScalarGridSpec(
            num_scalar_prefetch=1,
            grid=(size // step,),
            in_specs=[whole((rows, block))] * n
            + [pl.BlockSpec((n, step, block), lambda i, me: (0, start // step + i, 0))],
            out_specs=[pl.BlockSpec((rows // n_out, step), lambda i, me: (0, i))] * n_out,
        ),
        compiler_params=params(48),
        cost_estimate=pl.CostEstimate(
            flops=2 * rows * size * n * block, bytes_accessed=2 * size * n * block, transcendentals=0
        ),
    )(me, *[xs[s] for s in order], embed)


def softmax_kernel(counts, width, *refs):
    parts, refs = refs[: sum(counts)], refs[sum(counts) :]
    squares, targets, refs = refs[0], refs[1], refs[2:]
    qs, stats = refs[:-1], refs[-1]
    inv = lax.rsqrt(squares[:, 0:1] / width + 1e-05)
    target = targets[:, 0:1]
    pieces, hits, at, first = [], [], 0, 0
    for count in counts:
        total = parts[at][...]
        for part in parts[at + 1 : at + count]:
            total = total + part[...]
        at += count
        total = total * inv
        ids = lax.broadcasted_iota(jnp.int32, total.shape, 1) + first
        first += total.shape[1]
        pieces.append(total)
        hits.append(ids == target)
    top = functools.reduce(jnp.maximum, [jnp.max(p, axis=1, keepdims=True) for p in pieces])
    mass, moment, picked = 0.0, 0.0, 0.0
    for i, (piece, hit) in enumerate(zip(pieces, hits)):
        shifted = piece - top
        e = jnp.exp(shifted)
        mass = mass + jnp.sum(e, axis=1, keepdims=True)
        moment = moment + jnp.sum(e * shifted, axis=1, keepdims=True)
        picked = picked + jnp.sum(jnp.where(hit, piece, 0.0), axis=1, keepdims=True)
        size = piece.shape[1]
        first = i // len(qs) * size
        qs[i % len(qs)][:, first : first + size] = e.astype(BF16)
    lane = lax.broadcasted_iota(jnp.int32, stats.shape, 1)
    out = jnp.zeros(stats.shape, F32)
    for i, value in enumerate([top, mass, moment, picked]):
        out = jnp.where(lane == i, value, out)
    stats[...] = out


def softmax(pieces, squares, targets, width):
    counts = [len(p) for p in pieces]
    flat = [part for p in pieces for part in p]
    rows = flat[0].shape[0]
    return pl.pallas_call(
        functools.partial(softmax_kernel, counts, width),
        out_shape=[jax.ShapeDtypeStruct((rows, len(pieces) // 2 * flat[0].shape[1]), BF16)] * 2
        + [jax.ShapeDtypeStruct((rows, LANES), F32)],
        compiler_params=params(48),
    )(*flat, squares, targets)


def tree(op, values):
    while len(values) > 1:
        half = len(values) // 2
        values = [op(a, b) for a, b in zip(values[:half], values[half:])]
    return values[0]


def merge_kernel(n, tokens, width, *refs):
    stats, (squares, targets), out = refs[:n], refs[n : n + 2], refs[-1]
    tops = [st[:, 0:1] for st in stats]
    top = tree(jnp.maximum, tops)
    weights = [jnp.exp(t - top) for t in tops]
    mass = tree(jnp.add, [w * st[:, 1:2] for w, st in zip(weights, stats)])
    moment = tree(
        jnp.add, [w * (st[:, 2:3] + st[:, 1:2] * (t - top)) for w, t, st in zip(weights, tops, stats)]
    )
    picked = tree(jnp.add, [st[:, 3:4] for st in stats])
    lse = top + jnp.log(mass)
    inv = lax.rsqrt(squares[:, 0:1] / width + 1e-05)
    scale = jnp.exp(tops[0] - lse) / tokens
    at_target = (jnp.exp(picked - lse) - 1.0) / tokens
    pull = (moment / mass + (top - picked)) * (inv * inv) / (tokens * width)
    lane = lax.broadcasted_iota(jnp.int32, out.shape, 1)
    packed = jnp.zeros(out.shape, F32)
    values = [scale, at_target, targets[:, 0:1].astype(F32), inv, pull, lse - picked]
    for i, value in enumerate(values):
        packed = jnp.where(lane == i, value, packed)
    out[...] = packed


def merge(stats, squares, targets, tokens, width, deps):
    n = len(stats)
    return pl.pallas_call(
        functools.partial(merge_kernel, n, tokens, width),
        out_shape=jax.ShapeDtypeStruct(stats[0].shape, F32),
        in_specs=[pl.BlockSpec(memory_space=pltpu.VMEM)] * (n + 2) + after(deps),
        compiler_params=params(48),
    )(*stats, squares, targets, *deps)


def dlogits_kernel(places, quarter, *refs):
    qs, (packs, dlogits) = refs[:-2], refs[-2:]
    n = len(places[0])
    rows = packs.shape[0] // n
    for s in range(n):
        at = slice(s * rows, (s + 1) * rows)
        scale, at_target, target = packs[at, 0:1], packs[at, 1:2], packs[at, 2:3].astype(jnp.int32)
        for i, q in enumerate(qs):
            here = places[i].index(s) * rows
            for j in range(q.shape[1] // quarter):
                first = (j * len(qs) + i) * quarter
                values = q[here : here + rows, j * quarter : (j + 1) * quarter].astype(F32) * scale
                ids = lax.broadcasted_iota(jnp.int32, values.shape, 1) + first
                dlogits[at, first : first + quarter] = jnp.where(ids == target, at_target, values).astype(BF16)


def scale_rows(q, packs, quarter):
    values, places = zip(*q)
    shape = (packs.shape[0], sum(v.shape[1] for v in values))
    return pl.pallas_call(
        functools.partial(dlogits_kernel, places, quarter),
        out_shape=jax.ShapeDtypeStruct(shape, BF16),
        compiler_params=params(48),
    )(*values, packs)


def dpre_kernel(n, *refs):
    parts, (packs, pre, h, gain, out) = refs[:n], refs[n:]
    dnormed = parts[0][0]
    for part in parts[1:]:
        dnormed = dnormed + part[0].astype(F32)
    inv, pull = packs[:, 3:4], packs[:, 4:5]
    v = pre[...]
    sigma = 1.0 / (1.0 + jnp.exp(-v))
    act = h[...].astype(F32) + v * sigma
    dact = inv * gain[...] * dnormed - act * pull
    out[...] = (dact * sigma * (1.0 + v * (1.0 - sigma))).astype(BF16)


def grad_pre(parts, packs, pre, h, gain):
    rows, block = pre.shape
    rest = [packs, pre, h, gain]
    return pl.pallas_call(
        functools.partial(dpre_kernel, len(parts)),
        out_shape=jax.ShapeDtypeStruct(pre.shape, BF16),
        grid=(1,),
        in_specs=[pick(t, rows, block) for t in parts] + [whole(r.shape) for r in rest],
        out_specs=whole(pre.shape),
        compiler_params=params(48),
    )(*[t[0] for t in parts], *rest)


def grad_kernel(order, me, h, *refs):
    n = len(order)
    ds, out, placed, mixed = refs[:n], refs[n], refs[n + 1], refs[n + 2]

    @pl.when(pl.program_id(0) == 0)
    def _():
        for s, d in zip(order, ds):
            placed[me[0] ^ s] = d[...]

    step = h.shape[0]
    lanes = range(0, out.shape[1], LANES)
    for k in range(n):
        product = jnp.dot(h[...], placed[k], preferred_element_type=F32)
        for j, lane in enumerate(lanes):
            mixed[j, pl.ds(k, step, stride=n + 1), :] = product[:, lane : lane + LANES]

    def collect(first, group):
        at = pl.multiple_of(first * n, 16)
        for j, lane in enumerate(lanes):
            parts = [
                mixed[j, pl.ds((first + g) * (n + 1) + p, 8), :] for g in range(group) for p in range(0, n, 8)
            ]
            out[pl.ds(at, group * n), lane : lane + LANES] = jnp.concatenate(parts, axis=0).astype(BF16)

    each_tile(n, step, collect)


def weight_grad(h, ds, me):
    width, rows = h.shape
    n = len(ds)
    block = ds[0].shape[1]
    order = sorted(ds)
    step = min(256, width)
    return pl.pallas_call(
        functools.partial(grad_kernel, order),
        out_shape=jax.ShapeDtypeStruct((width * n, block), BF16),
        grid_spec=pltpu.PrefetchScalarGridSpec(
            num_scalar_prefetch=1,
            grid=(width // step,),
            in_specs=[pl.BlockSpec((step, rows), lambda i, me: (i, 0))] + [whole((rows, block))] * n,
            out_specs=pl.BlockSpec((step * n, block), lambda i, me: (i, 0)),
            scratch_shapes=[pltpu.VMEM((n, rows, block), BF16), pltpu.VMEM((block // LANES, step * (n + 1), LANES), F32)],
        ),
        compiler_params=params(48),
        cost_estimate=pl.CostEstimate(
            flops=2 * rows * width * n * block, bytes_accessed=2 * width * n * block, transcendentals=0
        ),
    )(me, h, *[ds[s] for s in order])


def column(values):
    return jnp.broadcast_to(values[:, None], (values.shape[0], LANES))


def on_device(hidden_rows, head_weight, norm_gain, vocab_embed, targets):
    n_dp, n_mp = lax.axis_size("dp"), lax.axis_size("mp")
    tok_dp, width_mp = hidden_rows.shape
    block = head_weight.shape[3]
    width = width_mp * n_mp
    tokens = tok_dp * n_dp
    vocab_mp = vocab_embed.shape[0]
    dp_bits, mp_bits = bits_of(n_dp), bits_of(n_mp)
    dp_index = lax.axis_index("dp")
    mp_index = lax.axis_index("mp")
    me = mp_index.astype(jnp.int32).reshape(1)
    pairs = list(range(n_mp - 2, -1, -2))
    orders = [dp_bits, dp_bits[::-1]]

    embed_rows = vocab_embed.reshape(vocab_mp * n_mp, block)
    gain = norm_gain.reshape(1, block)
    quarter = vocab_mp // 4

    h = jnp.concatenate(gather_direct(hidden_rows, "dp"), axis=0)
    weight = relayout(head_weight.reshape(width_mp * n_mp, block), n_mp, 0, width_mp, None, [])
    own_h = lax.dynamic_slice_in_dim(h, dp_index * block, block, 1)

    def reduce_blocks(products, fillers):
        terms = {}
        for group, (odd, even) in products:
            arrived = swap(odd, "mp", 1)
            for i, s in enumerate(group):
                terms[s] = [(even, i), (arrived, i)]
        done, made = 1, None
        for bit in mp_bits[1:]:
            senders = [s for s in sorted(terms, reverse=True) if s & bit and not s & done]
            totals = [add_round(terms[s], [] if made is None else [made]) for s in senders]
            for s, total in zip(senders, totals):
                terms[s ^ bit].append((swap(total, "mp", bit), 0))
            if fillers:
                made = fillers.pop(0)(made, totals)
            done |= bit
        return terms[0], made

    def fill(first, count):
        def run(into, deps):
            return relayout(embed_rows, n_mp, first * quarter, count * quarter, into, deps)

        return run

    cut = n_mp // 4
    early = project(h, [weight], me, pairs[:cut])
    late = project(h, [weight], me, pairs[cut:], [early[1]])
    parts, embed = reduce_blocks([(pairs[:cut], early), (pairs[cut:], late)], [fill(0, 1), fill(1, 2)])
    pre, x, squares = activate(parts, own_h, gain, [embed])

    xs = gather_xor(x, "mp", mp_bits[::-1])
    for bit in mp_bits:
        squares = squares + swap(squares, "mp", bit)
    embed = fill(3, 1)(embed, [x])
    pieces = []
    for i in range(4):
        partial = project_vocab(xs, embed, me, n_dp, i * quarter, quarter)
        pieces.append(scatter_xor({s: [p] for s, p in enumerate(partial)}, "dp", orders[i % 2]))

    squares = squares[0].reshape(n_dp, tok_dp)
    for bit in dp_bits:
        arrived = swap(squares, "dp", bit)
        squares = squares + jnp.stack([arrived[s ^ bit] for s in range(n_dp)])
    squares = column(squares[0])
    local = lax.dynamic_slice_in_dim(targets, dp_index * tok_dp, tok_dp, 0) - mp_index * vocab_mp
    local = column(local)
    *own_q, stats = softmax(pieces, squares, local, width)
    q, first_hops = zip(*[gather_rows(own_q[i], "dp", orders[i]) for i in range(2)])
    packed = merge(gather_direct(stats, "mp"), squares, local, tokens, width, first_hops)
    packs = jnp.concatenate(gather_direct(packed, "dp"), axis=0)
    sums = [jnp.sum(packs[s * tok_dp : (s + 1) * tok_dp, 5]) for s in range(n_dp)]
    loss = tree(jnp.add, sums) / tokens

    dlogits = scale_rows(q, packs, quarter)
    early = project(dlogits, [embed], me, pairs[:cut])
    late = project(dlogits, [embed], me, pairs[cut:], [early[1]])
    parts, _ = reduce_blocks([(pairs[:cut], early), (pairs[cut:], late)], [])
    dpre = grad_pre(parts, packs, pre, own_h, gain)
    grad = weight_grad(h.T, gather_xor(dpre, "mp", mp_bits[::-1]), me)
    return (grad.reshape(head_weight.shape), loss)


def solution(mesh):
    return jax.shard_map(
        on_device,
        mesh=mesh,
        in_specs=(
            P("dp", "mp"),
            P("mp", None, "dp", None),
            P("mp", "dp", None),
            P("mp", None, "dp", None),
            P(),
        ),
        out_specs=(P("mp", None, "dp", None), P()),
        check_vma=False,
    )
```

time: 302 us -> 287 us (0.950)
  Pallas kernels: 143 us -> 124 us
  starting transfers between devices: 50.9 us -> 58 us
    pallas_call x13 -> x10, Pallas kernels: 66.4 us -> 52.1 us  [the longest x4 30.3 us: project(): pl.pallas_call(functools.partial(project_kernel, len(ws), len(deps)), out...]
    ppermute x56 -> x58, starting transfers between devices: 50.9 us -> 58 us  [swap(): return lax.ppermute(value, axis, [(i, i ^ bit) for i in range(n)])]
    pallas_call x1, Pallas kernels: 14.3 us -> 11.1 us  [weight_grad(): pl.pallas_call(functools.partial(grad_kernel, order), out_shape=jax.Shape...]
    ppermute x56 -> x58, waiting for transfers between devices: 90.7 us -> 88.9 us  [swap(): return lax.ppermute(value, axis, [(i, i ^ bit) for i in range(n)])]
  transfers between devices with their start and end apart: 56 -> 58, of which waited for: 17 -> 25; matrix products, arithmetic and copies ran while one was open for 2% -> 2% of each run, Pallas kernels for 38% -> 33%
where the time goes in v3:
time: 287 us; the launch traced here: 285 us
  Pallas kernels  124 us (43%)
  waiting for transfers between devices  88.9 us (31%)
  starting transfers between devices  58 us (20%)
  local copies, waits for them, and re-layouts  4.86 us (2%)
  between operations  4.85 us (2%)
  other arithmetic  4.74 us (2%)
    ppermute x58, waiting for transfers between devices, swap(): return lax.ppermute(value, axis, [(i, i ^ bit) for i in range(n)])  88.9 us
    pallas_call x4, Pallas kernels, relayout(): pl.pallas_call(functools.partial(relayout_kernel, n, len(skipped)), out_s...  58.6 us
    ppermute x58, starting transfers between devices, swap(): return lax.ppermute(value, axis, [(i, i ^ bit) for i in range(n)])  58 us
    pallas_call x4, Pallas kernels, project(): pl.pallas_call(functools.partial(project_kernel, len(ws), len(deps)), out...  30.3 us
    pallas_call x4, Pallas kernels, project_vocab(): pl.pallas_call(functools.partial(logits_kernel, order, n_out), out_shape=...  19.7 us
    pallas_call x1, Pallas kernels, weight_grad(): pl.pallas_call(functools.partial(grad_kernel, order), out_shape=jax.Shape...  11.1 us
  transfers between devices with their start and end apart: 58, of which 25 were waited for; matrix products, arithmetic and copies ran while one was open for 2% of the time, Pallas kernels for 33%

profile of v3, /device:TPU:1, one launch (start us, length us, event | category | flops | bytes accessed | tf_op | source)
XLA Modules:
  0.0 285.1 jit_solution(2621608741545020893)
XLA Ops:
  1.9 3.1 %collective-permute-start.2 = (bf16[64,2048]{0,1:T(8,128)(2,1)S(1)}, bf16[64,2048]{0,1:T(8,128)(2,1)S(1)}, u32[]{:S(2)}, u32[]{:S(2)}) collective-permute-start(bf16[64,2048]{0,1:T(8,128)(2,1)S(1)} %copy.16), channel_id=1, source_target_pairs={{0,24},{8,16},{16,8},{24,0},{1,25},{9,17},{17,9},{25,1},{2,26},{10... | collective-permute-start | bytes 786440 | tf_op jit(solution)/shard_map/ppermute | solution.py:27
  5.3 19.3 %shard_map.104.refs_0_ = bf16[8,2048,512]{2,1,0:T(8,128)(2,1)} custom-call(bf16[16384,512]{1,0:T(8,128)(2,1)} %bitcast.16), custom_call_target="tpu_custom_call" | custom-call | bytes 33554432 | tf_op jit(solution)/shard_map/pallas_call | solution.py:105
  24.7 3.9 %collective-permute-done.1 = bf16[64,2048]{0,1:T(8,128)(2,1)S(1)} collective-permute-done((bf16[64,2048]{0,1:T(8,128)(2,1)S(1)}, bf16[64,2048]{0,1:T(8,128)(2,1)S(1)}, u32[]{:S(2)}, u32[]{:S(2)}) %collective-permute-start.1) | collective-permute-done | bytes 262176 | tf_op jit(solution)/shard_map/ppermute | solution.py:27
  31.5 6.2 %shard_map.105 = (bf16[2,256,512]{2,1,0:T(8,128)(2,1)S(1)}, f32[2,256,512]{2,1,0:T(8,128)S(1)}) custom-call(s32[4]{0:T(128)S(1)} %get-tuple-element.70.ks, bf16[256,2048]{1,0:T(8,128)(2,1)S(1)} %copy.18.lhs, bf16[8,2048,512]{2,1,0:T(8,128)(2,1)} %shard_map.104.refs_0_), custom_call_target="tpu_custom_call" | custom-call | flops 2147483648 | bytes 8388608 | tf_op jit(solution)/shard_map/pallas_call | solution.py:141
  38.3 6.1 %shard_map.106 = (bf16[2,256,512]{2,1,0:T(8,128)(2,1)S(1)}, f32[2,256,512]{2,1,0:T(8,128)S(1)}) custom-call(s32[4]{0:T(128)S(1)} %get-tuple-element.71.ks, bf16[256,2048]{1,0:T(8,128)(2,1)S(1)} %copy.18.lhs, bf16[8,2048,512]{2,1,0:T(8,128)(2,1)} %shard_map.104.refs_0_, f32[2,256,512]{2,1,0:T(8,128)S(1)} %get-tuple-element.32.refs_1_.refs_0_), custom_call_target="tpu_custom_call" | custom-call | flops 2147483648 | bytes 8388608 | tf_op jit(solution)/shard_map/pallas_call | solution.py:141
  48.0 9.9 %shard_map.109.refs_3_.refs_0_ = bf16[8,4096,512]{2,1,0:T(8,128)(2,1)} custom-call(bf16[32768,512]{1,0:T(8,128)(2,1)} %bitcast.13, bf16[1,256,512]{2,1,0:T(8,128)(2,1)S(1)} %shard_map.108.refs_0_, bf16[1,256,512]{2,1,0:T(8,128)(2,1)S(1)} %shard_map.107.refs_1_), custom_call_target="tpu_custom_call" | custom-call | bytes 16777216 | tf_op jit(solution)/shard_map/pallas_call | solution.py:105
  61.6 19.3 %shard_map.111.refs_4_.refs_0_ = bf16[8,4096,512]{2,1,0:T(8,128)(2,1)} custom-call(bf16[32768,512]{1,0:T(8,128)(2,1)} %bitcast.14, bf16[8,4096,512]{2,1,0:T(8,128)(2,1)} %shard_map.109.refs_3_.refs_0_, bf16[1,256,512]{2,1,0:T(8,128)(2,1)S(1)} %shard_map.110.refs_1_), custom_call_target="tpu_custom_call", output_to_operand_aliasing={{}: (1, {})} | custom-call | bytes 33554432 | tf_op jit(solution)/shard_map/pallas_call | solution.py:105
  81.6 14.4 %collective-permute-done.11.refs_4_ = bf16[256,512]{1,0:T(8,128)(2,1)S(1)} collective-permute-done((bf16[256,512]{1,0:T(8,128)(2,1)S(1)}, bf16[256,512]{1,0:T(8,128)(2,1)S(1)}, u32[]{:S(2)}, u32[]{:S(2)}) %collective-permute-start.11) | collective-permute-done | bytes 262176 | tf_op jit(solution)/shard_map/ppermute | solution.py:27
  99.0 4.5 %collective-permute-done.28 = f32[8,256]{1,0:T(8,128)S(1)} collective-permute-done((f32[8,256]{1,0:T(8,128)S(1)}, f32[8,256]{1,0:T(8,128)S(1)}, u32[]{:S(2)}, u32[]{:S(2)}) %collective-permute-start.28) | collective-permute-done | bytes 8224 | tf_op jit(solution)/shard_map/ppermute | solution.py:27
  103.5 3.4 %collective-permute-done.29 = f32[8,256]{1,0:T(8,128)S(1)} collective-permute-done((f32[8,256]{1,0:T(8,128)S(1)}, f32[8,256]{1,0:T(8,128)S(1)}, u32[]{:S(2)}, u32[]{:S(2)}) %collective-permute-start.29) | collective-permute-done | bytes 8224 | tf_op jit(solution)/shard_map/ppermute | solution.py:27
  108.3 10.0 %shard_map.113.refs_8_.refs_0_ = bf16[8,4096,512]{2,1,0:T(8,128)(2,1)} custom-call(bf16[32768,512]{1,0:T(8,128)(2,1)} %bitcast.15, bf16[8,4096,512]{2,1,0:T(8,128)(2,1)} %shard_map.111.refs_4_.refs_0_, bf16[256,512]{1,0:T(8,128)(2,1)S(1)} %get-tuple-element.36.refs_1_.refs_0_), custom_call_target="tpu_custom_call", output_to_operand_aliasing={{}: (1, {})} | custom-call | bytes 16777216 | tf_op jit(solution)/shard_map/pallas_call | solution.py:105
  118.2 2.8 collective-permute-start.8
  123.3 4.9 %shard_map.117 = (f32[64,1024]{1,0:T(8,128)S(1)}, f32[64,1024]{1,0:T(8,128)S(1)}, f32[64,1024]{1,0:T(8,128)S(1)}, f32[64,1024]{1,0:T(8,128)S(1)}) custom-call(s32[1]{0:T(128)} %bitcast.me, bf16[256,512]{1,0:T(8,128)(2,1)S(1)} %get-tuple-element.36.refs_1_.refs_0_, bf16[256,512]{1,0:T(8,128)(2,1)S(1)} %collective-permute-done.8.refs_1_, ...), custom_call_target="tpu_custom_call" | custom-call | flops 2147483648 | bytes 8388608 | tf_op jit(solution)/shard_map/pallas_call | solution.py:232
  129.7 4.9 %shard_map.116 = (f32[64,1024]{1,0:T(8,128)S(1)}, f32[64,1024]{1,0:T(8,128)S(1)}, f32[64,1024]{1,0:T(8,128)S(1)}, f32[64,1024]{1,0:T(8,128)S(1)}) custom-call(s32[1]{0:T(128)} %bitcast.me, bf16[256,512]{1,0:T(8,128)(2,1)S(1)} %get-tuple-element.36.refs_1_.refs_0_, bf16[256,512]{1,0:T(8,128)(2,1)S(1)} %collective-permute-done.8.refs_1_, ...), custom_call_target="tpu_custom_call" | custom-call | flops 2147483648 | bytes 8388608 | tf_op jit(solution)/shard_map/pallas_call | solution.py:232
  136.1 4.9 %shard_map.115 = (f32[64,1024]{1,0:T(8,128)S(1)}, f32[64,1024]{1,0:T(8,128)S(1)}, f32[64,1024]{1,0:T(8,128)S(1)}, f32[64,1024]{1,0:T(8,128)S(1)}) custom-call(s32[1]{0:T(128)} %bitcast.me, bf16[256,512]{1,0:T(8,128)(2,1)S(1)} %get-tuple-element.36.refs_1_.refs_0_, bf16[256,512]{1,0:T(8,128)(2,1)S(1)} %collective-permute-done.8.refs_1_, ...), custom_call_target="tpu_custom_call" | custom-call | flops 2147483648 | bytes 8388608 | tf_op jit(solution)/shard_map/pallas_call | solution.py:232
  141.0 5.1 %shard_map.114 = (f32[64,1024]{1,0:T(8,128)S(1)}, f32[64,1024]{1,0:T(8,128)S(1)}, f32[64,1024]{1,0:T(8,128)S(1)}, f32[64,1024]{1,0:T(8,128)S(1)}) custom-call(s32[1]{0:T(128)} %bitcast.me, bf16[256,512]{1,0:T(8,128)(2,1)S(1)} %get-tuple-element.36.refs_1_.refs_0_, bf16[256,512]{1,0:T(8,128)(2,1)S(1)} %collective-permute-done.8.refs_1_, ...), custom_call_target="tpu_custom_call" | custom-call | flops 2147483648 | bytes 8388608 | tf_op jit(solution)/shard_map/pallas_call | solution.py:232
  148.0 10.0 %collective-permute-done.19 = f32[64,1024]{1,0:T(8,128)S(1)} collective-permute-done((f32[64,1024]{1,0:T(8,128)S(1)}, f32[64,1024]{1,0:T(8,128)S(1)}, u32[]{:S(2)}, u32[]{:S(2)}) %collective-permute-start.19) | collective-permute-done | bytes 262176 | tf_op jit(solution)/shard_map/ppermute | solution.py:27
  163.3 5.8 %collective-permute-done.26.refs_11_ = f32[64,1024]{1,0:T(8,128)S(1)} collective-permute-done((f32[64,1024]{1,0:T(8,128)S(1)}, f32[64,1024]{1,0:T(8,128)S(1)}, u32[]{:S(2)}, u32[]{:S(2)}) %collective-permute-start.26) | collective-permute-done | bytes 262176 | tf_op jit(solution)/shard_map/ppermute | solution.py:27
  169.0 5.6 %collective-permute-done.20.refs_5_ = f32[64,1024]{1,0:T(8,128)S(1)} collective-permute-done((f32[64,1024]{1,0:T(8,128)S(1)}, f32[64,1024]{1,0:T(8,128)S(1)}, u32[]{:S(2)}, u32[]{:S(2)}) %collective-permute-start.20) | collective-permute-done | bytes 262176 | tf_op jit(solution)/shard_map/ppermute | solution.py:27
  177.0 3.7 %collective-permute-done.32.refs_10_ = bf16[64,2048]{1,0:T(8,128)(2,1)S(1)} collective-permute-done((bf16[64,2048]{1,0:T(8,128)(2,1)S(1)}, bf16[64,2048]{1,0:T(8,128)(2,1)S(1)}, u32[]{:S(2)}, u32[]{:S(2)}) %collective-permute-start.32) | collective-permute-done | bytes 262176 | tf_op jit(solution)/shard_map/ppermute | solution.py:27
  182.6 6.9 %collective-permute-start.42 = (f32[64,128]{1,0:T(8,128)S(1)}, f32[64,128]{1,0:T(8,128)S(1)}, u32[]{:S(2)}, u32[]{:S(2)}) collective-permute-start(f32[64,128]{1,0:T(8,128)S(1)} %get-tuple-element.56.refs_0_), channel_id=1, source_target_pairs={{0,7},{1,6},{2,5},{3,4},{4,3},{5,2},{6,1},{7,0},{8,15},{9,14},{10,... | collective-permute-start | bytes 98312 | tf_op jit(solution)/shard_map/ppermute | solution.py:27
  189.5 3.8 %collective-permute-start.41 = (f32[64,128]{1,0:T(8,128)S(1)}, f32[64,128]{1,0:T(8,128)S(1)}, u32[]{:S(2)}, u32[]{:S(2)}) collective-permute-start(f32[64,128]{1,0:T(8,128)S(1)} %get-tuple-element.56.refs_0_), channel_id=1, source_target_pairs={{0,6},{1,7},{2,4},{3,5},{4,2},{5,3},{6,0},{7,1},{8,14},{9,15},{10,... | collective-permute-start | bytes 98312 | tf_op jit(solution)/shard_map/ppermute | solution.py:27
  195.4 2.7 collective-permute-done.40.refs_5_
  207.5 9.0 %shard_map.121 = (bf16[2,256,512]{2,1,0:T(8,128)(2,1)S(1)}, f32[2,256,512]{2,1,0:T(8,128)S(1)}) custom-call(s32[4]{0:T(128)S(1)} %get-tuple-element.70.ks, bf16[256,4096]{1,0:T(8,128)(2,1)S(1)} %shard_map.120.lhs, bf16[8,4096,512]{2,1,0:T(8,128)(2,1)} %shard_map.113.refs_8_.refs_0_), custom_call_target="tpu_custom_call" | custom-call | flops 4294967296 | bytes 16777216 | tf_op jit(solution)/shard_map/pallas_call | solution.py:141
  218.4 9.0 %shard_map.122 = (bf16[2,256,512]{2,1,0:T(8,128)(2,1)S(1)}, f32[2,256,512]{2,1,0:T(8,128)S(1)}) custom-call(s32[4]{0:T(128)S(1)} %copy-done.2, bf16[256,4096]{1,0:T(8,128)(2,1)S(1)} %shard_map.120.lhs, bf16[8,4096,512]{2,1,0:T(8,128)(2,1)} %shard_map.113.refs_8_.refs_0_, f32[2,256,512]{2,1,0:T(8,128)S(1)} %get-tuple-element.57.refs_1_.refs_0_), custom_call_target="tpu_custom_call" | custom-call | flops 4294967296 | bytes 16777216 | tf_op jit(solution)/shard_map/pallas_call | solution.py:141
  229.5 5.5 %collective-permute-done.49.refs_2_ = bf16[1,256,512]{2,1,0:T(8,128)(2,1)S(1)} collective-permute-done((bf16[1,256,512]{2,1,0:T(8,128)(2,1)S(1)}, bf16[1,256,512]{2,1,0:T(8,128)(2,1)S(1)}, u32[]{:S(2)}, u32[]{:S(2)}) %collective-permute-start.49) | collective-permute-done | bytes 262176 | tf_op jit(solution)/shard_map/ppermute | solution.py:27
  236.4 8.0 %collective-permute-done.47.refs_2_ = bf16[1,256,512]{2,1,0:T(8,128)(2,1)S(1)} collective-permute-done((bf16[1,256,512]{2,1,0:T(8,128)(2,1)S(1)}, bf16[1,256,512]{2,1,0:T(8,128)(2,1)S(1)}, u32[]{:S(2)}, u32[]{:S(2)}) %collective-permute-start.47) | collective-permute-done | bytes 262176 | tf_op jit(solution)/shard_map/ppermute | solution.py:27
  244.8 3.1 %collective-permute-start.54 = (bf16[256,512]{1,0:T(8,128)(2,1)S(1)}, bf16[256,512]{1,0:T(8,128)(2,1)S(1)}, u32[]{:S(2)}, u32[]{:S(2)}) collective-permute-start(bf16[256,512]{1,0:T(8,128)(2,1)S(1)} %shard_map.126.refs_0_), channel_id=1, source_target_pairs={{0,4},{1,5},{2,6},{3,7},{4,0},{5,1},{6,2},{7,3},{8,12},{9,13},{10,... | collective-permute-start | bytes 786440 | tf_op jit(solution)/shard_map/ppermute | solution.py:27
  248.1 11.0 %collective-permute-done.54.refs_4_ = bf16[256,512]{1,0:T(8,128)(2,1)S(1)} collective-permute-done((bf16[256,512]{1,0:T(8,128)(2,1)S(1)}, bf16[256,512]{1,0:T(8,128)(2,1)S(1)}, u32[]{:S(2)}, u32[]{:S(2)}) %collective-permute-start.54) | collective-permute-done | bytes 262176 | tf_op jit(solution)/shard_map/ppermute | solution.py:27
  260.6 2.7 collective-permute-start.51
  264.5 3.7 %collective-permute-start.57 = (bf16[256,512]{1,0:T(8,128)(2,1)S(1)}, bf16[256,512]{1,0:T(8,128)(2,1)S(1)}, u32[]{:S(2)}, u32[]{:S(2)}) collective-permute-start(bf16[256,512]{1,0:T(8,128)(2,1)S(1)} %collective-permute-done.56.refs_6_), channel_id=1, source_target_pairs={{0,1},{1,0},{2,3},{3,2},{4,5},{5,4},{6,7},{7,6},{8,9},{9,8},{10,11... | collective-permute-start | bytes 786440 | tf_op jit(solution)/shard_map/ppermute | solution.py:27
  272.9 11.1 %shard_map.127 = bf16[16384,512]{1,0:T(8,128)(2,1)} custom-call(s32[1]{0:T(128)} %bitcast.me, bf16[2048,256]{1,0:T(8,128)(2,1)S(1)} %fusion.3.h, bf16[256,512]{1,0:T(8,128)(2,1)S(1)} %shard_map.126.refs_0_, bf16[256,512]{1,0:T(8,128)(2,1)S(1)} %collective-permute-done.51.refs_1_, bf16[256,512]{1,0:T(8,128)(2,1)S(1)} %collective-permute-done.52.refs_2_, ...), custom_call_target="tpu_custom_call" | custom-call | flops 4294967296 | bytes 16777216 | tf_op jit(solution)/shard_map/pallas_call | solution.py:421
  (170 shorter events, 56.2 us)
Async XLA Ops:
  1.9 22.8 %collective-permute-start.2 = (bf16[64,2048]{0,1:T(8,128)(2,1)S(1)}, bf16[64,2048]{0,1:T(8,128)(2,1)S(1)}, u32[]{:S(2)}, u32[]{:S(2)}) collective-permute-start(bf16[64,2048]{0,1:T(8,128)(2,1)S(1)} %copy.16), channel_id=1, source_target_pairs={{0,24},{8,16},{16,8},{24,0},{1,25},{9,17},{17,9},{25,1},{2,26},{10... | collective-permute-start | bytes 786440 | tf_op jit(solution)/shard_map/ppermute | solution.py:27
  4.9 23.6 %collective-permute-start.1 = (bf16[64,2048]{0,1:T(8,128)(2,1)S(1)}, bf16[64,2048]{0,1:T(8,128)(2,1)S(1)}, u32[]{:S(2)}, u32[]{:S(2)}) collective-permute-start(bf16[64,2048]{0,1:T(8,128)(2,1)S(1)} %copy.16), channel_id=1, source_target_pairs={{0,16},{8,24},{16,0},{24,8},{1,17},{9,25},{17,1},{25,9},{2,18},{10... | collective-permute-start | bytes 786440 | tf_op jit(solution)/shard_map/ppermute | solution.py:27
  5.2 23.4 %collective-permute-start = (bf16[64,2048]{0,1:T(8,128)(2,1)S(1)}, bf16[64,2048]{0,1:T(8,128)(2,1)S(1)}, u32[]{:S(2)}, u32[]{:S(2)}) collective-permute-start(bf16[64,2048]{0,1:T(8,128)(2,1)S(1)} %copy.16), channel_id=1, source_target_pairs={{0,8},{8,0},{16,24},{24,16},{1,9},{9,1},{17,25},{25,17},{2,10},{10... | collective-permute-start | bytes 786440 | tf_op jit(solution)/shard_map/ppermute | solution.py:27
  44.6 13.4 %collective-permute-start.6 = (bf16[1,256,512]{2,1,0:T(8,128)(2,1)S(1)}, bf16[1,256,512]{2,1,0:T(8,128)(2,1)S(1)}, u32[]{:S(2)}, u32[]{:S(2)}) collective-permute-start(bf16[1,256,512]{2,1,0:T(8,128)(2,1)S(1)} %shard_map.108.refs_0_), channel_id=1, source_target_pairs={{0,2},{1,3},{2,0},{3,1},{4,6},{5,7},{6,4},{7,5},{8,10},{9,11},{10,... | collective-permute-start | bytes 786440 | tf_op jit(solution)/shard_map/ppermute | solution.py:27
  46.5 34.4 %collective-permute-start.4 = (bf16[1,256,512]{2,1,0:T(8,128)(2,1)S(1)}, bf16[1,256,512]{2,1,0:T(8,128)(2,1)S(1)}, u32[]{:S(2)}, u32[]{:S(2)}) collective-permute-start(bf16[1,256,512]{2,1,0:T(8,128)(2,1)S(1)} %shard_map.107.refs_1_), channel_id=1, source_target_pairs={{0,2},{1,3},{2,0},{3,1},{4,6},{5,7},{6,4},{7,5},{8,10},{9,11},{10,... | collective-permute-start | bytes 786440 | tf_op jit(solution)/shard_map/ppermute | solution.py:27
  58.1 22.9 %collective-permute-start.7 = (bf16[1,256,512]{2,1,0:T(8,128)(2,1)S(1)}, bf16[1,256,512]{2,1,0:T(8,128)(2,1)S(1)}, u32[]{:S(2)}, u32[]{:S(2)}) collective-permute-start(bf16[1,256,512]{2,1,0:T(8,128)(2,1)S(1)} %shard_map.110.refs_1_), channel_id=1, source_target_pairs={{0,4},{1,5},{2,6},{3,7},{4,0},{5,1},{6,2},{7,3},{8,12},{9,13},{10,... | collective-permute-start | bytes 786440 | tf_op jit(solution)/shard_map/ppermute | solution.py:27
  81.3 14.7 %collective-permute-start.11 = (bf16[256,512]{1,0:T(8,128)(2,1)S(1)}, bf16[256,512]{1,0:T(8,128)(2,1)S(1)}, u32[]{:S(2)}, u32[]{:S(2)}) collective-permute-start(bf16[256,512]{1,0:T(8,128)(2,1)S(1)} %get-tuple-element.36.refs_1_.refs_0_), channel_id=1, source_target_pairs={{0,4},{1,5},{2,6},{3,7},{4,0},{5,1},{6,2},{7,3},{8,12},{9,13},{10,... | collective-permute-start | bytes 786440 | tf_op jit(solution)/shard_map/ppermute | solution.py:27
  81.4 39.6 %collective-permute-start.9 = (bf16[256,512]{1,0:T(8,128)(2,1)S(1)}, bf16[256,512]{1,0:T(8,128)(2,1)S(1)}, u32[]{:S(2)}, u32[]{:S(2)}) collective-permute-start(bf16[256,512]{1,0:T(8,128)(2,1)S(1)} %get-tuple-element.36.refs_1_.refs_0_), channel_id=1, source_target_pairs={{0,2},{1,3},{2,0},{3,1},{4,6},{5,7},{6,4},{7,5},{8,10},{9,11},{10,... | collective-permute-start | bytes 786440 | tf_op jit(solution)/shard_map/ppermute | solution.py:27
  96.0 25.5 %collective-permute-start.13 = (bf16[256,512]{1,0:T(8,128)(2,1)S(1)}, bf16[256,512]{1,0:T(8,128)(2,1)S(1)}, u32[]{:S(2)}, u32[]{:S(2)}) collective-permute-start(bf16[256,512]{1,0:T(8,128)(2,1)S(1)} %collective-permute-done.11.refs_4_), channel_id=1, source_target_pairs={{0,2},{1,3},{2,0},{3,1},{4,6},{5,7},{6,4},{7,5},{8,10},{9,11},{10,... | collective-permute-start | bytes 786440 | tf_op jit(solution)/shard_map/ppermute | solution.py:27
  107.1 14.5 %collective-permute-start.30 = (f32[4,64]{1,0:T(4,128)S(1)}, f32[4,64]{1,0:T(4,128)S(1)}, u32[]{:S(2)}, u32[]{:S(2)}) collective-permute-start(f32[4,64]{1,0:T(4,128)S(1)} %reshape_squeeze.3), channel_id=1, source_target_pairs={{0,8},{8,0},{16,24},{24,16},{1,9},{9,1},{17,25},{25,17},{2,10},{10... | collective-permute-start | bytes 3080 | tf_op jit(solution)/shard_map/ppermute | solution.py:27
  121.6 24.5 %collective-permute-start.31 = (f32[4,64]{1,0:T(4,128)S(1)}, f32[4,64]{1,0:T(4,128)S(1)}, u32[]{:S(2)}, u32[]{:S(2)}) collective-permute-start(f32[4,64]{1,0:T(4,128)S(1)} %maximum_add_fusion), channel_id=1, source_target_pairs={{0,16},{8,24},{16,0},{24,8},{1,17},{9,25},{17,1},{25,9},{2,18},{10... | collective-permute-start | bytes 3080 | tf_op jit(solution)/shard_map/ppermute | solution.py:27
  128.1 31.5 %collective-permute-start.24 = (f32[64,1024]{1,0:T(8,128)S(1)}, f32[64,1024]{1,0:T(8,128)S(1)}, u32[]{:S(2)}, u32[]{:S(2)}) collective-permute-start(f32[64,1024]{1,0:T(8,128)S(1)} %get-tuple-element.50), channel_id=1, source_target_pairs={{0,16},{8,24},{16,0},{24,8},{1,17},{9,25},{17,1},{25,9},{2,18},{10... | collective-permute-start | bytes 786440 | tf_op jit(solution)/shard_map/ppermute | solution.py:27
  128.7 17.9 %collective-permute-start.25 = (f32[64,1024]{1,0:T(8,128)S(1)}, f32[64,1024]{1,0:T(8,128)S(1)}, u32[]{:S(2)}, u32[]{:S(2)}) collective-permute-start(f32[64,1024]{1,0:T(8,128)S(1)} %get-tuple-element.52), channel_id=1, source_target_pairs={{0,16},{8,24},{16,0},{24,8},{1,17},{9,25},{17,1},{25,9},{2,18},{10... | collective-permute-start | bytes 786440 | tf_op jit(solution)/shard_map/ppermute | solution.py:27
  134.6 25.7 %collective-permute-start.21 = (f32[64,1024]{1,0:T(8,128)S(1)}, f32[64,1024]{1,0:T(8,128)S(1)}, u32[]{:S(2)}, u32[]{:S(2)}) collective-permute-start(f32[64,1024]{1,0:T(8,128)S(1)} %get-tuple-element.46), channel_id=1, source_target_pairs={{0,8},{8,0},{16,24},{24,16},{1,9},{9,1},{17,25},{25,17},{2,10},{10... | collective-permute-start | bytes 786440 | tf_op jit(solution)/shard_map/ppermute | solution.py:27
  134.9 12.7 %collective-permute-start.22 = (f32[64,1024]{1,0:T(8,128)S(1)}, f32[64,1024]{1,0:T(8,128)S(1)}, u32[]{:S(2)}, u32[]{:S(2)}) collective-permute-start(f32[64,1024]{1,0:T(8,128)S(1)} %get-tuple-element.48), channel_id=1, source_target_pairs={{0,8},{8,0},{16,24},{24,16},{1,9},{9,1},{17,25},{25,17},{2,10},{10... | collective-permute-start | bytes 786440 | tf_op jit(solution)/shard_map/ppermute | solution.py:27
  146.0 15.2 %collective-permute-start.18 = (f32[64,1024]{1,0:T(8,128)S(1)}, f32[64,1024]{1,0:T(8,128)S(1)}, u32[]{:S(2)}, u32[]{:S(2)}) collective-permute-start(f32[64,1024]{1,0:T(8,128)S(1)} %get-tuple-element.42), channel_id=1, source_target_pairs={{0,16},{8,24},{16,0},{24,8},{1,17},{9,25},{17,1},{25,9},{2,18},{10... | collective-permute-start | bytes 786440 | tf_op jit(solution)/shard_map/ppermute | solution.py:27
  146.7 11.4 %collective-permute-start.19 = (f32[64,1024]{1,0:T(8,128)S(1)}, f32[64,1024]{1,0:T(8,128)S(1)}, u32[]{:S(2)}, u32[]{:S(2)}) collective-permute-start(f32[64,1024]{1,0:T(8,128)S(1)} %get-tuple-element.44), channel_id=1, source_target_pairs={{0,16},{8,24},{16,0},{24,8},{1,17},{9,25},{17,1},{25,9},{2,18},{10... | collective-permute-start | bytes 786440 | tf_op jit(solution)/shard_map/ppermute | solution.py:27
  147.6 10.7 %collective-permute-start.16 = (f32[64,1024]{1,0:T(8,128)S(1)}, f32[64,1024]{1,0:T(8,128)S(1)}, u32[]{:S(2)}, u32[]{:S(2)}) collective-permute-start(f32[64,1024]{1,0:T(8,128)S(1)} %get-tuple-element.40), channel_id=1, source_target_pairs={{0,8},{8,0},{16,24},{24,16},{1,9},{9,1},{17,25},{25,17},{2,10},{10... | collective-permute-start | bytes 786440 | tf_op jit(solution)/shard_map/ppermute | solution.py:27
  158.3 10.7 %collective-permute-start.26 = (f32[64,1024]{1,0:T(8,128)S(1)}, f32[64,1024]{1,0:T(8,128)S(1)}, u32[]{:S(2)}, u32[]{:S(2)}) collective-permute-start(f32[64,1024]{1,0:T(8,128)S(1)} %add.46), channel_id=1, source_target_pairs={{0,8},{8,0},{16,24},{24,16},{1,9},{9,1},{17,25},{25,17},{2,10},{10... | collective-permute-start | bytes 786440 | tf_op jit(solution)/shard_map/ppermute | solution.py:27
  159.6 9.4 %collective-permute-start.23 = (f32[64,1024]{1,0:T(8,128)S(1)}, f32[64,1024]{1,0:T(8,128)S(1)}, u32[]{:S(2)}, u32[]{:S(2)}) collective-permute-start(f32[64,1024]{1,0:T(8,128)S(1)} %add.45), channel_id=1, source_target_pairs={{0,16},{8,24},{16,0},{24,8},{1,17},{9,25},{17,1},{25,9},{2,18},{10... | collective-permute-start | bytes 786440 | tf_op jit(solution)/shard_map/ppermute | solution.py:27
  160.3 14.4 %collective-permute-start.20 = (f32[64,1024]{1,0:T(8,128)S(1)}, f32[64,1024]{1,0:T(8,128)S(1)}, u32[]{:S(2)}, u32[]{:S(2)}) collective-permute-start(f32[64,1024]{1,0:T(8,128)S(1)} %add.44), channel_id=1, source_target_pairs={{0,8},{8,0},{16,24},{24,16},{1,9},{9,1},{17,25},{25,17},{2,10},{10... | collective-permute-start | bytes 786440 | tf_op jit(solution)/shard_map/ppermute | solution.py:27
  161.2 13.4 %collective-permute-start.17 = (f32[64,1024]{1,0:T(8,128)S(1)}, f32[64,1024]{1,0:T(8,128)S(1)}, u32[]{:S(2)}, u32[]{:S(2)}) collective-permute-start(f32[64,1024]{1,0:T(8,128)S(1)} %add.43), channel_id=1, source_target_pairs={{0,16},{8,24},{16,0},{24,8},{1,17},{9,25},{17,1},{25,9},{2,18},{10... | collective-permute-start | bytes 786440 | tf_op jit(solution)/shard_map/ppermute | solution.py:27
  180.8 25.6 %collective-permute-start.33 = (bf16[128,2048]{1,0:T(8,128)(2,1)S(1)}, bf16[128,2048]{1,0:T(8,128)(2,1)S(1)}, u32[]{:S(2)}, u32[]{:S(2)}) collective-permute-start(bf16[128,2048]{1,0:T(8,128)(2,1)S(1)} %pad_maximum_fusion.3), channel_id=1, source_target_pairs={{0,16},{8,24},{16,0},{24,8},{1,17},{9,25},{17,1},{25,9},{2,18},{10... | collective-permute-start | bytes 1572872 | tf_op jit(solution)/shard_map/ppermute | solution.py:27
  181.5 25.1 %collective-permute-start.35 = (bf16[128,2048]{1,0:T(8,128)(2,1)S(1)}, bf16[128,2048]{1,0:T(8,128)(2,1)S(1)}, u32[]{:S(2)}, u32[]{:S(2)}) collective-permute-start(bf16[128,2048]{1,0:T(8,128)(2,1)S(1)} %pad_maximum_fusion.4), channel_id=1, source_target_pairs={{0,8},{8,0},{16,24},{24,16},{1,9},{9,1},{17,25},{25,17},{2,10},{10... | collective-permute-start | bytes 1572872 | tf_op jit(solution)/shard_map/ppermute | solution.py:27
  182.6 10.7 %collective-permute-start.42 = (f32[64,128]{1,0:T(8,128)S(1)}, f32[64,128]{1,0:T(8,128)S(1)}, u32[]{:S(2)}, u32[]{:S(2)}) collective-permute-start(f32[64,128]{1,0:T(8,128)S(1)} %get-tuple-element.56.refs_0_), channel_id=1, source_target_pairs={{0,7},{1,6},{2,5},{3,4},{4,3},{5,2},{6,1},{7,0},{8,15},{9,14},{10,... | collective-permute-start | bytes 98312 | tf_op jit(solution)/shard_map/ppermute | solution.py:27
  216.5 11.0 %collective-permute-start.48 = (bf16[2,256,512]{2,1,0:T(8,128)(2,1)S(1)}, bf16[2,256,512]{2,1,0:T(8,128)(2,1)S(1)}, u32[]{:S(2)}, u32[]{:S(2)}) collective-permute-start(bf16[2,256,512]{2,1,0:T(8,128)(2,1)S(1)} %get-tuple-element.60), channel_id=1, source_target_pairs={{0,1},{1,0},{2,3},{3,2},{4,5},{5,4},{6,7},{7,6},{8,9},{9,8},{10,11... | collective-permute-start | bytes 1572872 | tf_op jit(solution)/shard_map/ppermute | solution.py:27
  229.4 15.0 %collective-permute-start.47 = (bf16[1,256,512]{2,1,0:T(8,128)(2,1)S(1)}, bf16[1,256,512]{2,1,0:T(8,128)(2,1)S(1)}, u32[]{:S(2)}, u32[]{:S(2)}) collective-permute-start(bf16[1,256,512]{2,1,0:T(8,128)(2,1)S(1)} %shard_map.123), channel_id=1, source_target_pairs={{0,2},{1,3},{2,0},{3,1},{4,6},{5,7},{6,4},{7,5},{8,10},{9,11},{10,... | collective-permute-start | bytes 786440 | tf_op jit(solution)/shard_map/ppermute | solution.py:27
  244.8 14.3 %collective-permute-start.54 = (bf16[256,512]{1,0:T(8,128)(2,1)S(1)}, bf16[256,512]{1,0:T(8,128)(2,1)S(1)}, u32[]{:S(2)}, u32[]{:S(2)}) collective-permute-start(bf16[256,512]{1,0:T(8,128)(2,1)S(1)} %shard_map.126.refs_0_), channel_id=1, source_target_pairs={{0,4},{1,5},{2,6},{3,7},{4,0},{5,1},{6,2},{7,3},{8,12},{9,13},{10,... | collective-permute-start | bytes 786440 | tf_op jit(solution)/shard_map/ppermute | solution.py:27
  247.9 15.3 %collective-permute-start.52 = (bf16[256,512]{1,0:T(8,128)(2,1)S(1)}, bf16[256,512]{1,0:T(8,128)(2,1)S(1)}, u32[]{:S(2)}, u32[]{:S(2)}) collective-permute-start(bf16[256,512]{1,0:T(8,128)(2,1)S(1)} %shard_map.126.refs_0_), channel_id=1, source_target_pairs={{0,2},{1,3},{2,0},{3,1},{4,6},{5,7},{6,4},{7,5},{8,10},{9,11},{10,... | collective-permute-start | bytes 786440 | tf_op jit(solution)/shard_map/ppermute | solution.py:27
  260.6 12.3 %collective-permute-start.51 = (bf16[256,512]{1,0:T(8,128)(2,1)S(1)}, bf16[256,512]{1,0:T(8,128)(2,1)S(1)}, u32[]{:S(2)}, u32[]{:S(2)}) collective-permute-start(bf16[256,512]{1,0:T(8,128)(2,1)S(1)} %shard_map.126.refs_0_), channel_id=1, source_target_pairs={{0,1},{1,0},{2,3},{3,2},{4,5},{5,4},{6,7},{7,6},{8,9},{9,8},{10,11... | collective-permute-start | bytes 786440 | tf_op jit(solution)/shard_map/ppermute | solution.py:27
  263.3 9.6 %collective-permute-start.55 = (bf16[256,512]{1,0:T(8,128)(2,1)S(1)}, bf16[256,512]{1,0:T(8,128)(2,1)S(1)}, u32[]{:S(2)}, u32[]{:S(2)}) collective-permute-start(bf16[256,512]{1,0:T(8,128)(2,1)S(1)} %collective-permute-done.54.refs_4_), channel_id=1, source_target_pairs={{0,1},{1,0},{2,3},{3,2},{4,5},{5,4},{6,7},{7,6},{8,9},{9,8},{10,11... | collective-permute-start | bytes 786440 | tf_op jit(solution)/shard_map/ppermute | solution.py:27
  263.3 9.6 %collective-permute-start.53 = (bf16[256,512]{1,0:T(8,128)(2,1)S(1)}, bf16[256,512]{1,0:T(8,128)(2,1)S(1)}, u32[]{:S(2)}, u32[]{:S(2)}) collective-permute-start(bf16[256,512]{1,0:T(8,128)(2,1)S(1)} %collective-permute-done.52.refs_2_), channel_id=1, source_target_pairs={{0,1},{1,0},{2,3},{3,2},{4,5},{5,4},{6,7},{7,6},{8,9},{9,8},{10,11... | collective-permute-start | bytes 786440 | tf_op jit(solution)/shard_map/ppermute | solution.py:27
  (41 other events, 337.9 us)

commit v4 on v3

--- a/solution.py
+++ b/solution.py
@@ -10,6 +10,7 @@
 F32 = jnp.float32
 BF16 = jnp.bfloat16
 LANES = 128
+SHORT = pl.CostEstimate(flops=1, bytes_accessed=1, transcendentals=0)
 
 
 def params(mib):
@@ -27,11 +28,13 @@
     return lax.ppermute(value, axis, [(i, i ^ bit) for i in range(n)])
 
 
-def gather_xor(value, axis, bits):
+def gather_xor(value, axis, bits, deps=()):
     held = {0: value}
     for bit in bits:
         for s in list(held):
             held[s | bit] = swap(held[s], axis, bit)
+        if deps and len(held) == 2:
+            held[bit] = hold(held[bit], deps)
     return held
 
 
@@ -49,17 +52,6 @@
     return [value] + [swap(value, axis, s) for s in range(1, lax.axis_size(axis))]
 
 
-def scatter_xor(terms, axis, bits):
-    done = 0
-    for bit in bits:
-        for s in sorted(terms, reverse=True):
-            if s & bit and not s & done:
-                total = functools.reduce(jnp.add, terms[s])
-                terms[s ^ bit].append(swap(total, axis, bit))
-        done |= bit
-    return terms[0]
-
-
 def whole(shape):
     return pl.BlockSpec(shape, lambda *_: (0,) * len(shape))
 
@@ -79,23 +71,21 @@
 
 
 def relayout_kernel(n, n_skip, x, *refs):
-    out, mixed = refs[n_skip:]
-    rows = out.shape[1]
-    lanes = range(0, x.shape[1], LANES)
-
-    def spread(first, group):
-        at = pl.multiple_of(first * n, 16)
-        values = x[pl.ds(at, group * n), :].astype(F32)
-        for g in range(group):
-            for p in range(0, n, 8):
-                part = values[g * n + p : g * n + p + 8]
-                for j, lane in enumerate(lanes):
-                    mixed[j, pl.ds((first + g) * (n + 1) + p, 8), :] = part[:, lane : lane + LANES]
-
-    each_tile(n, rows, spread)
-    for k in range(n):
-        for j, lane in enumerate(lanes):
-            out[k, :, lane : lane + LANES] = mixed[j, pl.ds(k, rows, stride=n + 1), :].astype(BF16)
+    out, order = refs[n_skip:]
+    size = order.shape[0]
+    rows = size // n
+
+    @pl.when(pl.program_id(0) == 0)
+    def _():
+        to = lax.broadcasted_iota(jnp.int32, order.shape, 0)
+        source = lax.broadcasted_iota(jnp.int32, order.shape, 1)
+        order[...] = jnp.where(source == to % rows * n + to // rows, 1.0, 0.0).astype(BF16)
+
+    for part in range(out.shape[1] // rows):
+        mixed = jnp.dot(order[...], x[part * size : (part + 1) * size, :], preferred_element_type=F32)
+        mixed = mixed.astype(BF16)
+        for k in range(n):
+            out[k, part * rows : (part + 1) * rows, :] = mixed[k * rows : (k + 1) * rows]
 
 
 def relayout(flat, n, start, rows, into, deps):
@@ -108,11 +98,26 @@
         grid=(rows // step,),
         in_specs=[pl.BlockSpec((step * n, block), lambda i: (start // step + i, 0))] + after(skipped),
         out_specs=pl.BlockSpec((n, step, block), lambda i: (0, start // step + i, 0)),
-        scratch_shapes=[pltpu.VMEM((block // LANES, step * (n + 1), LANES), F32)],
+        scratch_shapes=[pltpu.VMEM((256, 256), BF16)],
         input_output_aliases={} if into is None else {1: 0},
         compiler_params=params(48),
-        cost_estimate=pl.CostEstimate(flops=0, bytes_accessed=4 * rows * n * block, transcendentals=0),
+        cost_estimate=SHORT,
     )(flat, *skipped)
+
+
+def hold_kernel(value, *refs):
+    refs[-1][...] = value[...]
+
+
+def hold(value, deps):
+    return pl.pallas_call(
+        hold_kernel,
+        out_shape=jax.ShapeDtypeStruct(value.shape, value.dtype),
+        grid=(1,),
+        in_specs=[whole(value.shape)] + after(deps),
+        out_specs=whole(value.shape),
+        compiler_params=params(48),
+    )(value, *deps)
 
 
 def project_kernel(n, n_skip, ks, lhs, *refs):
@@ -153,9 +158,7 @@
             out_specs=[pl.BlockSpec((1, rows, block), lambda i, ks: (i // 2, 0, 0))] * 2,
         ),
         compiler_params=params(48),
-        cost_estimate=pl.CostEstimate(
-            flops=4 * count * rows * depth * block, bytes_accessed=4 * count * depth * block, transcendentals=0
-        ),
+        cost_estimate=SHORT,
     )(ks, lhs, *ws, *deps)
 
 
@@ -185,15 +188,13 @@
 
 
 def act_kernel(n, *refs):
-    parts, (h, gain, pre, x, squares) = refs[:n], refs[-5:]
+    parts, (h, gain, pre, x) = refs[:n], refs[-4:]
     total = parts[0][0]
     for part in parts[1:]:
         total = total + part[0].astype(F32)
     pre[...] = total
     act = h[...].astype(F32) + total / (1.0 + jnp.exp(-total))
     x[...] = (act * gain[...]).astype(BF16)
-    sums = jnp.broadcast_to(jnp.sum(act * act, axis=1, keepdims=True), (act.shape[0], LANES))
-    squares[...] = jnp.transpose(sums)[: squares.shape[0]]
 
 
 def activate(parts, h, gain, deps=()):
@@ -203,65 +204,117 @@
         out_shape=[
             jax.ShapeDtypeStruct((rows, block), F32),
             jax.ShapeDtypeStruct((rows, block), BF16),
-            jax.ShapeDtypeStruct((8, rows), F32),
         ],
         grid=(1,),
         in_specs=[pick(t, rows, block) for t in parts] + after(deps) + [whole(h.shape), whole(gain.shape)],
-        out_specs=[whole((rows, block)), whole((rows, block)), whole((8, rows))],
+        out_specs=[whole((rows, block))] * 2,
         compiler_params=params(48),
     )(*[t[0] for t in parts], *deps, h, gain)
 
 
-def logits_kernel(order, n_out, me, *refs):
-    xs, e, outs = refs[: len(order)], refs[len(order)], refs[len(order) + 1 :]
+def hop_order(bits):
+    places = [0]
+    for bit in bits[::-1]:
+        places = places + [s | bit for s in places]
+    return places
+
+
+def logits_kernel(order, places, n_gains, me, *refs):
+    n = len(order)
+    xs, gains, e, (sent, kept) = refs[:n], refs[n : n + n_gains], refs[n + n_gains], refs[-2:]
     total = 0.0
     for s, x in zip(order, xs):
         total = total + lax.dot_general(
             x[...], e[me[0] ^ s], (((1,), (1,)), ((), ())), preferred_element_type=F32
         )
-    rows = total.shape[0] // n_out
-    for i, out in enumerate(outs):
-        out[...] = total[i * rows : (i + 1) * rows]
-
-
-def project_vocab(xs, embed, me, n_out, start, size):
+    rows, step = total.shape[0] // len(places), total.shape[1]
+
+    def store(values, at):
+        for i, s in enumerate(places):
+            out, j = (kept, i) if i < len(places) // 2 else (sent, i - len(places) // 2)
+            out[j * rows : (j + 1) * rows, at] = values[s * rows : (s + 1) * rows]
+
+    store(total, pl.ds(pl.multiple_of(pl.program_id(0) * step, step), step))
+    if n_gains:
+
+        @pl.when(pl.program_id(0) == 0)
+        def _():
+            squares = 0.0
+            for x, gain in zip(xs, gains):
+                act = x[...].astype(F32) / gain[...]
+                squares = squares + jnp.sum(act * act, axis=1, keepdims=True)
+            size = kept.shape[1] - LANES
+            store(jnp.broadcast_to(squares, (squares.shape[0], LANES)), slice(size, size + LANES))
+
+
+def project_vocab(xs, gains, embed, me, bits, start, size, deps):
     n, _, block = embed.shape
     order = sorted(xs)
     rows = xs[0].shape[0]
-    step = min(512, size)
-    return pl.pallas_call(
-        functools.partial(logits_kernel, order, n_out),
-        out_shape=[jax.ShapeDtypeStruct((rows // n_out, size), F32)] * n_out,
+    step = min(256, size)
+    shape = (rows // 2, size + (LANES if gains else 0))
+    return pl.pallas_call(
+        functools.partial(logits_kernel, order, hop_order(bits), len(gains)),
+        out_shape=[jax.ShapeDtypeStruct(shape, F32)] * 2,
         grid_spec=pltpu.PrefetchScalarGridSpec(
             num_scalar_prefetch=1,
             grid=(size // step,),
             in_specs=[whole((rows, block))] * n
-            + [pl.BlockSpec((n, step, block), lambda i, me: (0, start // step + i, 0))],
-            out_specs=[pl.BlockSpec((rows // n_out, step), lambda i, me: (0, i))] * n_out,
+            + [whole(g.shape) for g in gains]
+            + [pl.BlockSpec((n, step, block), lambda i, me: (0, start // step + i, 0))]
+            + after(deps),
+            out_specs=[whole(shape)] * 2,
         ),
         compiler_params=params(48),
-        cost_estimate=pl.CostEstimate(
-            flops=2 * rows * size * n * block, bytes_accessed=2 * size * n * block, transcendentals=0
-        ),
-    )(me, *[xs[s] for s in order], embed)
-
-
-def softmax_kernel(counts, width, *refs):
-    parts, refs = refs[: sum(counts)], refs[sum(counts) :]
-    squares, targets, refs = refs[0], refs[1], refs[2:]
+        cost_estimate=SHORT,
+    )(me, *[xs[s] for s in order], *gains, embed, *deps)
+
+
+def hop_kernel(n, *refs):
+    total = refs[0][...]
+    for ref in refs[1:n]:
+        total = total + ref[...]
+    refs[-1][...] = total
+
+
+def hop_sum(terms, rows, deps):
+    size = terms[0].shape[1]
+    return pl.pallas_call(
+        functools.partial(hop_kernel, len(terms)),
+        out_shape=jax.ShapeDtypeStruct((rows, size), F32),
+        grid=(1,),
+        in_specs=[pl.BlockSpec((rows, size), lambda i: (1, 0))] * len(terms) + after(deps),
+        out_specs=whole((rows, size)),
+        compiler_params=params(48),
+    )(*terms, *deps)
+
+
+def sum_hops(pieces, axis, orders):
+    terms = [[kept, swap(sent, axis, orders[i][0])] for i, (sent, kept) in enumerate(pieces)]
+    rows, before = pieces[0][1].shape[0], []
+    for hop in range(1, len(orders[0])):
+        rows //= 2
+        for i, held in enumerate(terms):
+            before = [hop_sum(held, rows, before)]
+            held.append(swap(before[0], axis, orders[i][hop]))
+    return terms
+
+
+def softmax_kernel(counts, size, width, *refs):
+    parts, (targets, *refs) = refs[: sum(counts)], refs[sum(counts) :]
     qs, stats = refs[:-1], refs[-1]
-    inv = lax.rsqrt(squares[:, 0:1] / width + 1e-05)
     target = targets[:, 0:1]
-    pieces, hits, at, first = [], [], 0, 0
-    for count in counts:
+    pieces, hits, at = [], [], 0
+    for i, count in enumerate(counts):
         total = parts[at][...]
         for part in parts[at + 1 : at + count]:
             total = total + part[...]
         at += count
-        total = total * inv
-        ids = lax.broadcasted_iota(jnp.int32, total.shape, 1) + first
-        first += total.shape[1]
-        pieces.append(total)
+        if i == 0:
+            inv = lax.rsqrt(total[:, size : size + 1] / width + 1e-05)
+            total = total[:, :size]
+        ids = lax.broadcasted_iota(jnp.int32, total.shape, 1) + i * size
+        pieces.append(total * inv)
         hits.append(ids == target)
     top = functools.reduce(jnp.maximum, [jnp.max(p, axis=1, keepdims=True) for p in pieces])
     mass, moment, picked = 0.0, 0.0, 0.0
@@ -271,26 +324,28 @@
         mass = mass + jnp.sum(e, axis=1, keepdims=True)
         moment = moment + jnp.sum(e * shifted, axis=1, keepdims=True)
         picked = picked + jnp.sum(jnp.where(hit, piece, 0.0), axis=1, keepdims=True)
-        size = piece.shape[1]
         first = i // len(qs) * size
         qs[i % len(qs)][:, first : first + size] = e.astype(BF16)
     lane = lax.broadcasted_iota(jnp.int32, stats.shape, 1)
     out = jnp.zeros(stats.shape, F32)
-    for i, value in enumerate([top, mass, moment, picked]):
+    for i, value in enumerate([top, mass, moment, picked, inv]):
         out = jnp.where(lane == i, value, out)
     stats[...] = out
 
 
-def softmax(pieces, squares, targets, width):
+def softmax(pieces, targets, size, width):
     counts = [len(p) for p in pieces]
     flat = [part for p in pieces for part in p]
-    rows = flat[0].shape[0]
-    return pl.pallas_call(
-        functools.partial(softmax_kernel, counts, width),
-        out_shape=[jax.ShapeDtypeStruct((rows, len(pieces) // 2 * flat[0].shape[1]), BF16)] * 2
+    rows = targets.shape[0]
+    return pl.pallas_call(
+        functools.partial(softmax_kernel, counts, size, width),
+        out_shape=[jax.ShapeDtypeStruct((rows, len(pieces) // 2 * size), BF16)] * 2
         + [jax.ShapeDtypeStruct((rows, LANES), F32)],
-        compiler_params=params(48),
-    )(*flat, squares, targets)
+        grid=(1,),
+        in_specs=[whole((rows, part.shape[1])) for part in flat] + [whole(targets.shape)],
+        out_specs=[whole((rows, len(pieces) // 2 * size))] * 2 + [whole((rows, LANES))],
+        compiler_params=params(48),
+    )(*flat, targets)
 
 
 def tree(op, values):
@@ -301,7 +356,7 @@
 
 
 def merge_kernel(n, tokens, width, *refs):
-    stats, (squares, targets), out = refs[:n], refs[n : n + 2], refs[-1]
+    stats, targets, out = refs[:n], refs[n], refs[-1]
     tops = [st[:, 0:1] for st in stats]
     top = tree(jnp.maximum, tops)
     weights = [jnp.exp(t - top) for t in tops]
@@ -311,7 +366,7 @@
     )
     picked = tree(jnp.add, [st[:, 3:4] for st in stats])
     lse = top + jnp.log(mass)
-    inv = lax.rsqrt(squares[:, 0:1] / width + 1e-05)
+    inv = stats[0][:, 4:5]
     scale = jnp.exp(tops[0] - lse) / tokens
     at_target = (jnp.exp(picked - lse) - 1.0) / tokens
     pull = (moment / mass + (top - picked)) * (inv * inv) / (tokens * width)
@@ -323,14 +378,14 @@
     out[...] = packed
 
 
-def merge(stats, squares, targets, tokens, width, deps):
+def merge(stats, targets, tokens, width, deps):
     n = len(stats)
     return pl.pallas_call(
         functools.partial(merge_kernel, n, tokens, width),
         out_shape=jax.ShapeDtypeStruct(stats[0].shape, F32),
-        in_specs=[pl.BlockSpec(memory_space=pltpu.VMEM)] * (n + 2) + after(deps),
-        compiler_params=params(48),
-    )(*stats, squares, targets, *deps)
+        in_specs=[pl.BlockSpec(memory_space=pltpu.VMEM)] * (n + 1) + after(deps),
+        compiler_params=params(48),
+    )(*stats, targets, *deps)
 
 
 def dlogits_kernel(places, quarter, *refs):
@@ -429,9 +484,7 @@
             scratch_shapes=[pltpu.VMEM((n, rows, block), BF16), pltpu.VMEM((block // LANES, step * (n + 1), LANES), F32)],
         ),
         compiler_params=params(48),
-        cost_estimate=pl.CostEstimate(
-            flops=2 * rows * width * n * block, bytes_accessed=2 * width * n * block, transcendentals=0
-        ),
+        cost_estimate=SHORT,
     )(me, h, *[ds[s] for s in order])
 
 
@@ -451,7 +504,6 @@
     mp_index = lax.axis_index("mp")
     me = mp_index.astype(jnp.int32).reshape(1)
     pairs = list(range(n_mp - 2, -1, -2))
-    orders = [dp_bits, dp_bits[::-1]]
 
     embed_rows = vocab_embed.reshape(vocab_mp * n_mp, block)
     gain = norm_gain.reshape(1, block)
@@ -461,18 +513,30 @@
     weight = relayout(head_weight.reshape(width_mp * n_mp, block), n_mp, 0, width_mp, None, [])
     own_h = lax.dynamic_slice_in_dim(h, dp_index * block, block, 1)
 
-    def reduce_blocks(products, fillers):
+    def reduce_product(lhs, w, deps, fillers):
         terms = {}
-        for group, (odd, even) in products:
+
+        def run(group, deps):
+            odd, even = project(lhs, [w], me, group, deps)
             arrived = swap(odd, "mp", 1)
             for i, s in enumerate(group):
                 terms[s] = [(even, i), (arrived, i)]
+            return even
+
+        even = run(pairs[:1], deps)
+        even = run(pairs[1:2], [even])
+        leaving = {pairs[0]: add_round(terms[pairs[0]])}
+        before = [even, leaving[pairs[0]]]
+        for pair in pairs[2:]:
+            before = [run([pair], before)]
         done, made = 1, None
         for bit in mp_bits[1:]:
             senders = [s for s in sorted(terms, reverse=True) if s & bit and not s & done]
-            totals = [add_round(terms[s], [] if made is None else [made]) for s in senders]
-            for s, total in zip(senders, totals):
-                terms[s ^ bit].append((swap(total, "mp", bit), 0))
+            totals = [leaving.get(s) for s in senders]
+            for i, s in enumerate(senders):
+                if totals[i] is None:
+                    totals[i] = add_round(terms[s], [] if made is None else [made])
+                terms[s ^ bit].append((swap(totals[i], "mp", bit), 0))
             if fillers:
                 made = fillers.pop(0)(made, totals)
             done |= bit
@@ -484,39 +548,30 @@
 
         return run
 
-    cut = n_mp // 4
-    early = project(h, [weight], me, pairs[:cut])
-    late = project(h, [weight], me, pairs[cut:], [early[1]])
-    parts, embed = reduce_blocks([(pairs[:cut], early), (pairs[cut:], late)], [fill(0, 1), fill(1, 2)])
-    pre, x, squares = activate(parts, own_h, gain, [embed])
-
-    xs = gather_xor(x, "mp", mp_bits[::-1])
-    for bit in mp_bits:
-        squares = squares + swap(squares, "mp", bit)
+    gains = gather_direct(gain, "mp")
+    parts, embed = reduce_product(h, weight, gains[1:], [fill(0, 1), fill(1, 2)])
+    pre, x = activate(parts, own_h, gain, [embed])
+
     embed = fill(3, 1)(embed, [x])
-    pieces = []
-    for i in range(4):
-        partial = project_vocab(xs, embed, me, n_dp, i * quarter, quarter)
-        pieces.append(scatter_xor({s: [p] for s, p in enumerate(partial)}, "dp", orders[i % 2]))
-
-    squares = squares[0].reshape(n_dp, tok_dp)
-    for bit in dp_bits:
-        arrived = swap(squares, "dp", bit)
-        squares = squares + jnp.stack([arrived[s ^ bit] for s in range(n_dp)])
-    squares = column(squares[0])
+    xs = gather_xor(x, "mp", mp_bits[::-1], [embed])
+    orders = [dp_bits, dp_bits[::-1]] * 2
+    pieces, before = [], []
+    for i, order in enumerate(orders):
+        pieces.append(project_vocab(xs, [] if i else gains, embed, me, order, i * quarter, quarter, before))
+        before = pieces[-1][1:]
+    pieces = sum_hops(pieces, "dp", orders)
+
     local = lax.dynamic_slice_in_dim(targets, dp_index * tok_dp, tok_dp, 0) - mp_index * vocab_mp
     local = column(local)
-    *own_q, stats = softmax(pieces, squares, local, width)
+    *own_q, stats = softmax(pieces, local, quarter, width)
     q, first_hops = zip(*[gather_rows(own_q[i], "dp", orders[i]) for i in range(2)])
-    packed = merge(gather_direct(stats, "mp"), squares, local, tokens, width, first_hops)
+    packed = merge(gather_direct(stats, "mp"), local, tokens, width, first_hops)
     packs = jnp.concatenate(gather_direct(packed, "dp"), axis=0)
     sums = [jnp.sum(packs[s * tok_dp : (s + 1) * tok_dp, 5]) for s in range(n_dp)]
     loss = tree(jnp.add, sums) / tokens
 
     dlogits = scale_rows(q, packs, quarter)
-    early = project(dlogits, [embed], me, pairs[:cut])
-    late = project(dlogits, [embed], me, pairs[cut:], [early[1]])
-    parts, _ = reduce_blocks([(pairs[:cut], early), (pairs[cut:], late)], [])
+    parts, _ = reduce_product(dlogits, embed, [], [])
     dpre = grad_pre(parts, packs, pre, own_h, gain)
     grad = weight_grad(h.T, gather_xor(dpre, "mp", mp_bits[::-1]), me)
     return (grad.reshape(head_weight.shape), loss)

time: 287 us -> 285 us (level)
  waiting for transfers between devices: 88.9 us -> 62.4 us
  Pallas kernels: 124 us -> 140 us
  starting transfers between devices: 58 us -> 61.9 us
    ppermute x58 -> x60, waiting for transfers between devices: 88.9 us -> 62.4 us  [swap(): return lax.ppermute(value, axis, [(i, i ^ bit) for i in range(n)])]
    pallas_call x5 -> x10, Pallas kernels: 20.3 us -> 28.2 us  [the longest x4 23.3 us: project_vocab(): pl.pallas_call(functools.partial(logits_kernel, order, hop_order(bits), l...]
    pallas_call x4 -> x8, Pallas kernels: 30.3 us -> 36.3 us  [project(): pl.pallas_call(functools.partial(project_kernel, len(ws), len(deps)), out...]
    ppermute x58 -> x60, starting transfers between devices: 58 us -> 61.9 us  [swap(): return lax.ppermute(value, axis, [(i, i ^ bit) for i in range(n)])]
  transfers between devices with their start and end apart: 58 -> 60, of which waited for: 25 -> 20; matrix products, arithmetic and copies ran while one was open for 2% -> 3% of each run, Pallas kernels for 33% -> 36%
where the time goes in v4:
time: 285 us; the launch traced here: 283 us
  Pallas kernels  140 us (49%)
  waiting for transfers between devices  62.4 us (22%)
  starting transfers between devices  61.9 us (22%)
  other arithmetic  7.15 us (3%)
  local copies, waits for them, and re-layouts  6.85 us (2%)
  between operations  4.92 us (2%)
    ppermute x60, waiting for transfers between devices, swap(): return lax.ppermute(value, axis, [(i, i ^ bit) for i in range(n)])  62.4 us
    ppermute x60, starting transfers between devices, swap(): return lax.ppermute(value, axis, [(i, i ^ bit) for i in range(n)])  61.9 us
    pallas_call x4, Pallas kernels, relayout(): pl.pallas_call(functools.partial(relayout_kernel, n, len(skipped)), out_s...  61.2 us
    pallas_call x8, Pallas kernels, project(): pl.pallas_call(functools.partial(project_kernel, len(ws), len(deps)), out...  36.3 us
    pallas_call x4, Pallas kernels, project_vocab(): pl.pallas_call(functools.partial(logits_kernel, order, hop_order(bits), l...  23.3 us
    pallas_call x1, Pallas kernels, weight_grad(): pl.pallas_call(functools.partial(grad_kernel, order), out_shape=jax.Shape...  11.1 us
  transfers between devices with their start and end apart: 60, of which 20 were waited for; matrix products, arithmetic and copies ran while one was open for 3% of the time, Pallas kernels for 36%

profile of v4, /device:TPU:1, one launch (start us, length us, event | category | flops | bytes accessed | tf_op | source)
XLA Modules:
  0.0 283.2 jit_solution(1720815441009750420)
XLA Ops:
  1.9 3.1 %collective-permute-start.2 = (bf16[64,2048]{0,1:T(8,128)(2,1)S(1)}, bf16[64,2048]{0,1:T(8,128)(2,1)S(1)}, u32[]{:S(2)}, u32[]{:S(2)}) collective-permute-start(bf16[64,2048]{0,1:T(8,128)(2,1)S(1)} %copy.20), channel_id=1, source_target_pairs={{0,24},{8,16},{16,8},{24,0},{1,25},{9,17},{17,9},{25,1},{2,26},{10... | collective-permute-start | bytes 786440 | tf_op jit(solution)/shard_map/ppermute | solution.py:28
  5.3 4.8 %collective-permute-start.9 = (f32[1,512]{1,0:T(1,128)}, f32[1,512]{1,0:T(1,128)S(1)}, u32[]{:S(2)}, u32[]{:S(2)}) collective-permute-start(f32[1,512]{1,0:T(1,128)} %bitcast.9), channel_id=1, source_target_pairs={{0,7},{1,6},{2,5},{3,4},{4,3},{5,2},{6,1},{7,0},{8,15},{9,14},{10,... | collective-permute-start | bytes 6152 | tf_op jit(solution)/shard_map/ppermute | solution.py:28
  10.8 20.2 %shard_map.140.refs_0_ = bf16[8,2048,512]{2,1,0:T(8,128)(2,1)} custom-call(bf16[16384,512]{1,0:T(8,128)(2,1)} %bitcast.22), custom_call_target="tpu_custom_call" | custom-call | flops 1 | bytes 1 | tf_op jit(solution)/shard_map/pallas_call | solution.py:95
  31.0 2.7 collective-permute-start.6
  38.3 3.7 %shard_map.141 = (bf16[1,256,512]{2,1,0:T(8,128)(2,1)S(1)}, f32[1,256,512]{2,1,0:T(8,128)S(1)}) custom-call(s32[2]{0:T(128)S(1)} %get-tuple-element.63.ks, bf16[256,2048]{1,0:T(8,128)(2,1)S(1)} %copy.24.lhs, bf16[8,2048,512]{2,1,0:T(8,128)(2,1)} %shard_map.140.refs_0_, f32[1,512]{1,0:T(1,128)S(1)} %collective-permute-done.3.refs_1_.refs_9_, ...), custom_call_target="tpu_custom_call" | custom-call | flops 1 | bytes 1 | tf_op jit(solution)/shard_map/pallas_call | solution.py:146
  42.4 3.6 %shard_map.142 = (bf16[1,256,512]{2,1,0:T(8,128)(2,1)S(1)}, f32[1,256,512]{2,1,0:T(8,128)S(1)}) custom-call(s32[2]{0:T(128)S(1)} %get-tuple-element.62.ks, bf16[256,2048]{1,0:T(8,128)(2,1)S(1)} %copy.24.lhs, bf16[8,2048,512]{2,1,0:T(8,128)(2,1)} %shard_map.140.refs_0_, f32[1,256,512]{2,1,0:T(8,128)S(1)} %get-tuple-element.31.refs_1_.refs_0_), custom_call_target="tpu_custom_call" | custom-call | flops 1 | bytes 1 | tf_op jit(solution)/shard_map/pallas_call | solution.py:146
  46.1 3.7 %shard_map.144 = (bf16[1,256,512]{2,1,0:T(8,128)(2,1)S(1)}, f32[1,256,512]{2,1,0:T(8,128)S(1)}) custom-call(s32[2]{0:T(128)S(1)} %broadcast_xor_fusion.1.ks, bf16[256,2048]{1,0:T(8,128)(2,1)S(1)} %copy.24.lhs, bf16[8,2048,512]{2,1,0:T(8,128)(2,1)} %shard_map.140.refs_0_, f32[1,256,512]{2,1,0:T(8,128)S(1)} %get-tuple-element.32.refs_1_.refs_0_, ...), custom_call_target="tpu_custom_call" | custom-call | flops 1 | bytes 1 | tf_op jit(solution)/shard_map/pallas_call | solution.py:146
  51.2 3.6 %shard_map.145 = (bf16[1,256,512]{2,1,0:T(8,128)(2,1)S(1)}, f32[1,256,512]{2,1,0:T(8,128)S(1)}) custom-call(s32[2]{0:T(128)S(1)} %broadcast_xor_fusion.3.ks, bf16[256,2048]{1,0:T(8,128)(2,1)S(1)} %copy.24.lhs, bf16[8,2048,512]{2,1,0:T(8,128)(2,1)} %shard_map.140.refs_0_, f32[1,256,512]{2,1,0:T(8,128)S(1)} %get-tuple-element.34.refs_1_.refs_0_), custom_call_target="tpu_custom_call" | custom-call | flops 1 | bytes 1 | tf_op jit(solution)/shard_map/pallas_call | solution.py:146
  56.2 10.4 %shard_map.147.refs_3_.refs_0_ = bf16[8,4096,512]{2,1,0:T(8,128)(2,1)} custom-call(bf16[32768,512]{1,0:T(8,128)(2,1)} %bitcast.19, bf16[1,256,512]{2,1,0:T(8,128)(2,1)S(1)} %shard_map.143.refs_2_.refs_0_, bf16[1,256,512]{2,1,0:T(8,128)(2,1)S(1)} %shard_map.146.refs_1_), custom_call_target="tpu_custom_call" | custom-call | flops 1 | bytes 1 | tf_op jit(solution)/shard_map/pallas_call | solution.py:95
  71.0 20.2 %shard_map.149.refs_4_.refs_0_ = bf16[8,4096,512]{2,1,0:T(8,128)(2,1)} custom-call(bf16[32768,512]{1,0:T(8,128)(2,1)} %bitcast.20, bf16[8,4096,512]{2,1,0:T(8,128)(2,1)} %shard_map.147.refs_3_.refs_0_, bf16[1,256,512]{2,1,0:T(8,128)(2,1)S(1)} %shard_map.148.refs_1_), custom_call_target="tpu_custom_call", output_to_operand_aliasing={{}: (1, {})} | custom-call | flops 1 | bytes 1 | tf_op jit(solution)/shard_map/pallas_call | solution.py:95
  92.2 10.5 %shard_map.151.refs_0_.refs_16_.refs_8_ = bf16[8,4096,512]{2,1,0:T(8,128)(2,1)} custom-call(bf16[32768,512]{1,0:T(8,128)(2,1)} %bitcast.21, bf16[8,4096,512]{2,1,0:T(8,128)(2,1)} %shard_map.149.refs_4_.refs_0_, bf16[256,512]{1,0:T(8,128)(2,1)S(1)} %get-tuple-element.39.refs_1_.refs_0_), custom_call_target="tpu_custom_call", output_to_operand_aliasing={{}: (1, {})} | custom-call | flops 1 | bytes 1 | tf_op jit(solution)/shard_map/pallas_call | solution.py:95
  103.6 2.9 %collective-permute-done.20.value = bf16[256,512]{1,0:T(8,128)(2,1)S(1)} collective-permute-done((bf16[256,512]{1,0:T(8,128)(2,1)S(1)}, bf16[256,512]{1,0:T(8,128)(2,1)S(1)}, u32[]{:S(2)}, u32[]{:S(2)}) %collective-permute-start.20) | collective-permute-done | bytes 262176 | tf_op jit(solution)/shard_map/ppermute | solution.py:28
  107.8 4.8 %collective-permute-done.18.refs_2_ = bf16[256,512]{1,0:T(8,128)(2,1)S(1)} collective-permute-done((bf16[256,512]{1,0:T(8,128)(2,1)S(1)}, bf16[256,512]{1,0:T(8,128)(2,1)S(1)}, u32[]{:S(2)}, u32[]{:S(2)}) %collective-permute-start.18) | collective-permute-done | bytes 262176 | tf_op jit(solution)/shard_map/ppermute | solution.py:28
  113.2 5.0 %collective-permute-done.22.refs_6_ = bf16[256,512]{1,0:T(8,128)(2,1)S(1)} collective-permute-done((bf16[256,512]{1,0:T(8,128)(2,1)S(1)}, bf16[256,512]{1,0:T(8,128)(2,1)S(1)}, u32[]{:S(2)}, u32[]{:S(2)}) %collective-permute-start.22) | collective-permute-done | bytes 262176 | tf_op jit(solution)/shard_map/ppermute | solution.py:28
  119.9 6.3 %shard_map.153 = (f32[128,1152]{1,0:T(8,128)S(1)}, f32[128,1152]{1,0:T(8,128)S(1)}) custom-call(s32[1]{0:T(128)} %bitcast.me, bf16[256,512]{1,0:T(8,128)(2,1)S(1)} %get-tuple-element.39.refs_1_.refs_0_, bf16[256,512]{1,0:T(8,128)(2,1)S(1)} %collective-permute-done.17.refs_1_, bf16[256,512]{1,0:T(8,128)(2,1)S(1)} %collective-permute-done.18.refs_2_, ...), custom_call_target="tpu_custom_call" | custom-call | flops 1 | bytes 1 | tf_op jit(solution)/shard_map/pallas_call | solution.py:256
  127.4 5.6 %shard_map.155 = (f32[128,1024]{1,0:T(8,128)S(1)}, f32[128,1024]{1,0:T(8,128)S(1)}) custom-call(s32[1]{0:T(128)} %bitcast.me, bf16[256,512]{1,0:T(8,128)(2,1)S(1)} %get-tuple-element.39.refs_1_.refs_0_, bf16[256,512]{1,0:T(8,128)(2,1)S(1)} %collective-permute-done.17.refs_1_, bf16[256,512]{1,0:T(8,128)(2,1)S(1)} %collective-permute-done.18.refs_2_, ...), custom_call_target="tpu_custom_call" | custom-call | flops 1 | bytes 1 | tf_op jit(solution)/shard_map/pallas_call | solution.py:256
  134.3 5.6 %shard_map.157 = (f32[128,1024]{1,0:T(8,128)S(1)}, f32[128,1024]{1,0:T(8,128)S(1)}) custom-call(s32[1]{0:T(128)} %bitcast.me, bf16[256,512]{1,0:T(8,128)(2,1)S(1)} %get-tuple-element.39.refs_1_.refs_0_, bf16[256,512]{1,0:T(8,128)(2,1)S(1)} %collective-permute-done.17.refs_1_, bf16[256,512]{1,0:T(8,128)(2,1)S(1)} %collective-permute-done.18.refs_2_, ...), custom_call_target="tpu_custom_call" | custom-call | flops 1 | bytes 1 | tf_op jit(solution)/shard_map/pallas_call | solution.py:256
  140.3 5.8 %shard_map.159 = (f32[128,1024]{1,0:T(8,128)S(1)}, f32[128,1024]{1,0:T(8,128)S(1)}) custom-call(s32[1]{0:T(128)} %bitcast.me, bf16[256,512]{1,0:T(8,128)(2,1)S(1)} %get-tuple-element.39.refs_1_.refs_0_, bf16[256,512]{1,0:T(8,128)(2,1)S(1)} %collective-permute-done.17.refs_1_, bf16[256,512]{1,0:T(8,128)(2,1)S(1)} %collective-permute-done.18.refs_2_, ...), custom_call_target="tpu_custom_call" | custom-call | flops 1 | bytes 1 | tf_op jit(solution)/shard_map/pallas_call | solution.py:256
  153.3 5.2 %collective-permute-done.30.refs_1_.refs_10_ = f32[128,1024]{1,0:T(8,128)S(1)} collective-permute-done((f32[128,1024]{1,0:T(8,128)S(1)}, f32[128,1024]{1,0:T(8,128)S(1)}, u32[]{:S(2)}, u32[]{:S(2)}) %collective-permute-start.30) | collective-permute-done | bytes 524320 | tf_op jit(solution)/shard_map/ppermute | solution.py:28
  161.0 4.3 %collective-permute-done.31.refs_11_ = f32[64,1024]{1,0:T(8,128)} collective-permute-done((f32[64,1024]{1,0:T(8,128)}, f32[64,1024]{1,0:T(8,128)}, u32[]{:S(2)}, u32[]{:S(2)}) %collective-permute-start.31) | collective-permute-done | bytes 262176 | tf_op jit(solution)/shard_map/ppermute | solution.py:28
  165.3 5.2 %collective-permute-done.29.refs_8_ = f32[64,1024]{1,0:T(8,128)} collective-permute-done((f32[64,1024]{1,0:T(8,128)}, f32[64,1024]{1,0:T(8,128)}, u32[]{:S(2)}, u32[]{:S(2)}) %collective-permute-start.29) | collective-permute-done | bytes 262176 | tf_op jit(solution)/shard_map/ppermute | solution.py:28
  176.0 4.2 %collective-permute-done.32.refs_9_ = bf16[64,2048]{1,0:T(8,128)(2,1)S(1)} collective-permute-done((bf16[64,2048]{1,0:T(8,128)(2,1)S(1)}, bf16[64,2048]{1,0:T(8,128)(2,1)S(1)}, u32[]{:S(2)}, u32[]{:S(2)}) %collective-permute-start.32) | collective-permute-done | bytes 262176 | tf_op jit(solution)/shard_map/ppermute | solution.py:28
  181.9 5.0 %collective-permute-start.42 = (f32[64,128]{1,0:T(8,128)S(1)}, f32[64,128]{1,0:T(8,128)S(1)}, u32[]{:S(2)}, u32[]{:S(2)}) collective-permute-start(f32[64,128]{1,0:T(8,128)S(1)} %get-tuple-element.50.refs_0_), channel_id=1, source_target_pairs={{0,7},{1,6},{2,5},{3,4},{4,3},{5,2},{6,1},{7,0},{8,15},{9,14},{10,... | collective-permute-start | bytes 98312 | tf_op jit(solution)/shard_map/ppermute | solution.py:28
  205.0 5.4 %shard_map.164 = (bf16[1,256,512]{2,1,0:T(8,128)(2,1)S(1)}, f32[1,256,512]{2,1,0:T(8,128)S(1)}) custom-call(s32[2]{0:T(128)S(1)} %copy-done.10, bf16[256,4096]{1,0:T(8,128)(2,1)S(1)} %shard_map.163.lhs, bf16[8,4096,512]{2,1,0:T(8,128)(2,1)} %shard_map.151.refs_0_.refs_16_.refs_8_), custom_call_target="tpu_custom_call" | custom-call | flops 1 | bytes 1 | tf_op jit(solution)/shard_map/pallas_call | solution.py:146
  212.4 5.4 %shard_map.165 = (bf16[1,256,512]{2,1,0:T(8,128)(2,1)S(1)}, f32[1,256,512]{2,1,0:T(8,128)S(1)}) custom-call(s32[2]{0:T(128)S(1)} %copy-done.8, bf16[256,4096]{1,0:T(8,128)(2,1)S(1)} %shard_map.163.lhs, bf16[8,4096,512]{2,1,0:T(8,128)(2,1)} %shard_map.151.refs_0_.refs_16_.refs_8_, f32[1,256,512]{2,1,0:T(8,128)S(1)} %get-tuple-element.51.refs_1_.refs_0_), custom_call_target="tpu_custom_call" | custom-call | flops 1 | bytes 1 | tf_op jit(solution)/shard_map/pallas_call | solution.py:146
  217.9 5.4 %shard_map.167 = (bf16[1,256,512]{2,1,0:T(8,128)(2,1)S(1)}, f32[1,256,512]{2,1,0:T(8,128)S(1)}) custom-call(s32[2]{0:T(128)S(1)} %copy-done.12, bf16[256,4096]{1,0:T(8,128)(2,1)S(1)} %shard_map.163.lhs, bf16[8,4096,512]{2,1,0:T(8,128)(2,1)} %shard_map.151.refs_0_.refs_16_.refs_8_, f32[1,256,512]{2,1,0:T(8,128)S(1)} %get-tuple-element.52.refs_1_.refs_0_, ...), custom_call_target="tpu_custom_call" | custom-call | flops 1 | bytes 1 | tf_op jit(solution)/shard_map/pallas_call | solution.py:146
  224.2 5.4 %shard_map.168 = (bf16[1,256,512]{2,1,0:T(8,128)(2,1)S(1)}, f32[1,256,512]{2,1,0:T(8,128)S(1)}) custom-call(s32[2]{0:T(128)S(1)} %copy-done.14, bf16[256,4096]{1,0:T(8,128)(2,1)S(1)} %shard_map.163.lhs, bf16[8,4096,512]{2,1,0:T(8,128)(2,1)} %shard_map.151.refs_0_.refs_16_.refs_8_, f32[1,256,512]{2,1,0:T(8,128)S(1)} %get-tuple-element.54.refs_1_.refs_0_), custom_call_target="tpu_custom_call" | custom-call | flops 1 | bytes 1 | tf_op jit(solution)/shard_map/pallas_call | solution.py:146
  232.9 9.7 %collective-permute-done.49.refs_2_ = bf16[1,256,512]{2,1,0:T(8,128)(2,1)S(1)} collective-permute-done((bf16[1,256,512]{2,1,0:T(8,128)(2,1)S(1)}, bf16[1,256,512]{2,1,0:T(8,128)(2,1)S(1)}, u32[]{:S(2)}, u32[]{:S(2)}) %collective-permute-start.49) | collective-permute-done | bytes 262176 | tf_op jit(solution)/shard_map/ppermute | solution.py:28
  243.1 3.1 %collective-permute-start.56 = (bf16[256,512]{1,0:T(8,128)(2,1)S(1)}, bf16[256,512]{1,0:T(8,128)(2,1)S(1)}, u32[]{:S(2)}, u32[]{:S(2)}) collective-permute-start(bf16[256,512]{1,0:T(8,128)(2,1)S(1)} %shard_map.171.refs_0_), channel_id=1, source_target_pairs={{0,4},{1,5},{2,6},{3,7},{4,0},{5,1},{6,2},{7,3},{8,12},{9,13},{10,... | collective-permute-start | bytes 786440 | tf_op jit(solution)/shard_map/ppermute | solution.py:28
  248.2 8.3 %collective-permute-done.56.refs_4_ = bf16[256,512]{1,0:T(8,128)(2,1)S(1)} collective-permute-done((bf16[256,512]{1,0:T(8,128)(2,1)S(1)}, bf16[256,512]{1,0:T(8,128)(2,1)S(1)}, u32[]{:S(2)}, u32[]{:S(2)}) %collective-permute-start.56) | collective-permute-done | bytes 262176 | tf_op jit(solution)/shard_map/ppermute | solution.py:28
  256.5 2.6 collective-permute-start.58
  271.1 11.1 %shard_map.172 = bf16[16384,512]{1,0:T(8,128)(2,1)} custom-call(s32[1]{0:T(128)} %bitcast.me, bf16[2048,256]{1,0:T(8,128)(2,1)S(1)} %fusion.h, bf16[256,512]{1,0:T(8,128)(2,1)S(1)} %shard_map.171.refs_0_, bf16[256,512]{1,0:T(8,128)(2,1)S(1)} %collective-permute-done.53.refs_1_, bf16[256,512]{1,0:T(8,128)(2,1)S(1)} %collective-permute-done.54.refs_2_, ...), custom_call_target="tpu_custom_call" | custom-call | flops 1 | bytes 1 | tf_op jit(solution)/shard_map/pallas_call | solution.py:476
  (189 shorter events, 75.5 us)
Async XLA Ops:
  1.9 31.8 %collective-permute-start.2 = (bf16[64,2048]{0,1:T(8,128)(2,1)S(1)}, bf16[64,2048]{0,1:T(8,128)(2,1)S(1)}, u32[]{:S(2)}, u32[]{:S(2)}) collective-permute-start(bf16[64,2048]{0,1:T(8,128)(2,1)S(1)} %copy.20), channel_id=1, source_target_pairs={{0,24},{8,16},{16,8},{24,0},{1,25},{9,17},{17,9},{25,1},{2,26},{10... | collective-permute-start | bytes 786440 | tf_op jit(solution)/shard_map/ppermute | solution.py:28
  4.9 30.0 %collective-permute-start.1 = (bf16[64,2048]{0,1:T(8,128)(2,1)S(1)}, bf16[64,2048]{0,1:T(8,128)(2,1)S(1)}, u32[]{:S(2)}, u32[]{:S(2)}) collective-permute-start(bf16[64,2048]{0,1:T(8,128)(2,1)S(1)} %copy.20), channel_id=1, source_target_pairs={{0,16},{8,24},{16,0},{24,8},{1,17},{9,25},{17,1},{25,9},{2,18},{10... | collective-permute-start | bytes 786440 | tf_op jit(solution)/shard_map/ppermute | solution.py:28
  5.2 30.3 %collective-permute-start = (bf16[64,2048]{0,1:T(8,128)(2,1)S(1)}, bf16[64,2048]{0,1:T(8,128)(2,1)}, u32[]{:S(2)}, u32[]{:S(2)}) collective-permute-start(bf16[64,2048]{0,1:T(8,128)(2,1)S(1)} %copy.20), channel_id=1, source_target_pairs={{0,8},{8,0},{16,24},{24,16},{1,9},{9,1},{17,25},{25,17},{2,10},{10... | collective-permute-start | bytes 786440 | tf_op jit(solution)/shard_map/ppermute | solution.py:28
  5.3 25.7 %collective-permute-start.9 = (f32[1,512]{1,0:T(1,128)}, f32[1,512]{1,0:T(1,128)S(1)}, u32[]{:S(2)}, u32[]{:S(2)}) collective-permute-start(f32[1,512]{1,0:T(1,128)} %bitcast.9), channel_id=1, source_target_pairs={{0,7},{1,6},{2,5},{3,4},{4,3},{5,2},{6,1},{7,0},{8,15},{9,14},{10,... | collective-permute-start | bytes 6152 | tf_op jit(solution)/shard_map/ppermute | solution.py:28
  10.1 20.9 %collective-permute-start.8 = (f32[1,512]{1,0:T(1,128)}, f32[1,512]{1,0:T(1,128)S(1)}, u32[]{:S(2)}, u32[]{:S(2)}) collective-permute-start(f32[1,512]{1,0:T(1,128)} %bitcast.10), channel_id=1, source_target_pairs={{0,6},{1,7},{2,4},{3,5},{4,2},{5,3},{6,0},{7,1},{8,14},{9,15},{10,... | collective-permute-start | bytes 6152 | tf_op jit(solution)/shard_map/ppermute | solution.py:28
  50.0 16.5 %collective-permute-start.14 = (bf16[1,256,512]{2,1,0:T(8,128)(2,1)S(1)}, bf16[1,256,512]{2,1,0:T(8,128)(2,1)S(1)}, u32[]{:S(2)}, u32[]{:S(2)}) collective-permute-start(bf16[1,256,512]{2,1,0:T(8,128)(2,1)S(1)} %get-tuple-element.38), channel_id=1, source_target_pairs={{0,1},{1,0},{2,3},{3,2},{4,5},{5,4},{6,7},{7,6},{8,9},{9,8},{10,11... | collective-permute-start | bytes 786440 | tf_op jit(solution)/shard_map/ppermute | solution.py:28
  50.4 16.2 %collective-permute-start.15 = (bf16[1,256,512]{2,1,0:T(8,128)(2,1)S(1)}, bf16[1,256,512]{2,1,0:T(8,128)(2,1)S(1)}, u32[]{:S(2)}, u32[]{:S(2)}) collective-permute-start(bf16[1,256,512]{2,1,0:T(8,128)(2,1)S(1)} %shard_map.143.refs_2_.refs_0_), channel_id=1, source_target_pairs={{0,2},{1,3},{2,0},{3,1},{4,6},{5,7},{6,4},{7,5},{8,10},{9,11},{10,... | collective-permute-start | bytes 786440 | tf_op jit(solution)/shard_map/ppermute | solution.py:28
  54.9 36.3 %collective-permute-start.11 = (bf16[1,256,512]{2,1,0:T(8,128)(2,1)S(1)}, bf16[1,256,512]{2,1,0:T(8,128)(2,1)S(1)}, u32[]{:S(2)}, u32[]{:S(2)}) collective-permute-start(bf16[1,256,512]{2,1,0:T(8,128)(2,1)S(1)} %get-tuple-element.36), channel_id=1, source_target_pairs={{0,1},{1,0},{2,3},{3,2},{4,5},{5,4},{6,7},{7,6},{8,9},{9,8},{10,11... | collective-permute-start | bytes 786440 | tf_op jit(solution)/shard_map/ppermute | solution.py:28
  55.6 35.6 %collective-permute-start.13 = (bf16[1,256,512]{2,1,0:T(8,128)(2,1)S(1)}, bf16[1,256,512]{2,1,0:T(8,128)(2,1)S(1)}, u32[]{:S(2)}, u32[]{:S(2)}) collective-permute-start(bf16[1,256,512]{2,1,0:T(8,128)(2,1)S(1)} %shard_map.146.refs_1_), channel_id=1, source_target_pairs={{0,2},{1,3},{2,0},{3,1},{4,6},{5,7},{6,4},{7,5},{8,10},{9,11},{10,... | collective-permute-start | bytes 786440 | tf_op jit(solution)/shard_map/ppermute | solution.py:28
  66.7 24.5 %collective-permute-start.16 = (bf16[1,256,512]{2,1,0:T(8,128)(2,1)S(1)}, bf16[1,256,512]{2,1,0:T(8,128)(2,1)S(1)}, u32[]{:S(2)}, u32[]{:S(2)}) collective-permute-start(bf16[1,256,512]{2,1,0:T(8,128)(2,1)S(1)} %shard_map.148.refs_1_), channel_id=1, source_target_pairs={{0,4},{1,5},{2,6},{3,7},{4,0},{5,1},{6,2},{7,3},{8,12},{9,13},{10,... | collective-permute-start | bytes 786440 | tf_op jit(solution)/shard_map/ppermute | solution.py:28
  92.2 14.3 %collective-permute-start.20 = (bf16[256,512]{1,0:T(8,128)(2,1)S(1)}, bf16[256,512]{1,0:T(8,128)(2,1)S(1)}, u32[]{:S(2)}, u32[]{:S(2)}) collective-permute-start(bf16[256,512]{1,0:T(8,128)(2,1)S(1)} %get-tuple-element.39.refs_1_.refs_0_), channel_id=1, source_target_pairs={{0,4},{1,5},{2,6},{3,7},{4,0},{5,1},{6,2},{7,3},{8,12},{9,13},{10,... | collective-permute-start | bytes 786440 | tf_op jit(solution)/shard_map/ppermute | solution.py:28
  102.7 9.9 %collective-permute-start.18 = (bf16[256,512]{1,0:T(8,128)(2,1)S(1)}, bf16[256,512]{1,0:T(8,128)(2,1)S(1)}, u32[]{:S(2)}, u32[]{:S(2)}) collective-permute-start(bf16[256,512]{1,0:T(8,128)(2,1)S(1)} %get-tuple-element.39.refs_1_.refs_0_), channel_id=1, source_target_pairs={{0,2},{1,3},{2,0},{3,1},{4,6},{5,7},{6,4},{7,5},{8,10},{9,11},{10,... | collective-permute-start | bytes 786440 | tf_op jit(solution)/shard_map/ppermute | solution.py:28
  106.5 11.7 %collective-permute-start.22 = (bf16[256,512]{1,0:T(8,128)(2,1)S(1)}, bf16[256,512]{1,0:T(8,128)(2,1)S(1)}, u32[]{:S(2)}, u32[]{:S(2)}) collective-permute-start(bf16[256,512]{1,0:T(8,128)(2,1)S(1)} %shard_map.152.refs_4_), channel_id=1, source_target_pairs={{0,2},{1,3},{2,0},{3,1},{4,6},{5,7},{6,4},{7,5},{8,10},{9,11},{10,... | collective-permute-start | bytes 786440 | tf_op jit(solution)/shard_map/ppermute | solution.py:28
  106.6 12.1 %collective-permute-start.17 = (bf16[256,512]{1,0:T(8,128)(2,1)S(1)}, bf16[256,512]{1,0:T(8,128)(2,1)S(1)}, u32[]{:S(2)}, u32[]{:S(2)}) collective-permute-start(bf16[256,512]{1,0:T(8,128)(2,1)S(1)} %get-tuple-element.39.refs_1_.refs_0_), channel_id=1, source_target_pairs={{0,1},{1,0},{2,3},{3,2},{4,5},{5,4},{6,7},{7,6},{8,9},{9,8},{10,11... | collective-permute-start | bytes 786440 | tf_op jit(solution)/shard_map/ppermute | solution.py:28
  107.7 11.0 %collective-permute-start.21 = (bf16[256,512]{1,0:T(8,128)(2,1)S(1)}, bf16[256,512]{1,0:T(8,128)(2,1)S(1)}, u32[]{:S(2)}, u32[]{:S(2)}) collective-permute-start(bf16[256,512]{1,0:T(8,128)(2,1)S(1)} %shard_map.152.refs_4_), channel_id=1, source_target_pairs={{0,1},{1,0},{2,3},{3,2},{4,5},{5,4},{6,7},{7,6},{8,9},{9,8},{10,11... | collective-permute-start | bytes 786440 | tf_op jit(solution)/shard_map/ppermute | solution.py:28
  126.1 20.3 %collective-permute-start.24 = (f32[128,1152]{1,0:T(8,128)S(1)}, f32[128,1152]{1,0:T(8,128)S(1)}, u32[]{:S(2)}, u32[]{:S(2)}) collective-permute-start(f32[128,1152]{1,0:T(8,128)S(1)} %get-tuple-element.41), channel_id=1, source_target_pairs={{0,8},{8,0},{16,24},{24,16},{1,9},{9,1},{17,25},{25,17},{2,10},{10... | collective-permute-start | bytes 1769480 | tf_op jit(solution)/shard_map/ppermute | solution.py:28
  133.0 15.4 %collective-permute-start.26 = (f32[128,1024]{1,0:T(8,128)S(1)}, f32[128,1024]{1,0:T(8,128)S(1)}, u32[]{:S(2)}, u32[]{:S(2)}) collective-permute-start(f32[128,1024]{1,0:T(8,128)S(1)} %get-tuple-element.43), channel_id=1, source_target_pairs={{0,16},{8,24},{16,0},{24,8},{1,17},{9,25},{17,1},{25,9},{2,18},{10... | collective-permute-start | bytes 1572872 | tf_op jit(solution)/shard_map/ppermute | solution.py:28
  140.0 12.6 %collective-permute-start.28 = (f32[128,1024]{1,0:T(8,128)S(1)}, f32[128,1024]{1,0:T(8,128)S(1)}, u32[]{:S(2)}, u32[]{:S(2)}) collective-permute-start(f32[128,1024]{1,0:T(8,128)S(1)} %get-tuple-element.45), channel_id=1, source_target_pairs={{0,8},{8,0},{16,24},{24,16},{1,9},{9,1},{17,25},{25,17},{2,10},{10... | collective-permute-start | bytes 1572872 | tf_op jit(solution)/shard_map/ppermute | solution.py:28
  146.2 12.4 %collective-permute-start.30 = (f32[128,1024]{1,0:T(8,128)S(1)}, f32[128,1024]{1,0:T(8,128)S(1)}, u32[]{:S(2)}, u32[]{:S(2)}) collective-permute-start(f32[128,1024]{1,0:T(8,128)S(1)} %get-tuple-element.47), channel_id=1, source_target_pairs={{0,16},{8,24},{16,0},{24,8},{1,17},{9,25},{17,1},{25,9},{2,18},{10... | collective-permute-start | bytes 1572872 | tf_op jit(solution)/shard_map/ppermute | solution.py:28
  147.2 23.3 %collective-permute-start.25 = (f32[64,1152]{1,0:T(8,128)}, f32[64,1152]{1,0:T(8,128)}, u32[]{:S(2)}, u32[]{:S(2)}) collective-permute-start(f32[64,1152]{1,0:T(8,128)} %shard_map.154.refs_2_), channel_id=1, source_target_pairs={{0,16},{8,24},{16,0},{24,8},{1,17},{9,25},{17,1},{25,9},{2,18},{10... | collective-permute-start | bytes 884744 | tf_op jit(solution)/shard_map/ppermute | solution.py:28
  149.2 11.8 %collective-permute-start.27 = (f32[64,1024]{1,0:T(8,128)}, f32[64,1024]{1,0:T(8,128)}, u32[]{:S(2)}, u32[]{:S(2)}) collective-permute-start(f32[64,1024]{1,0:T(8,128)} %shard_map.156.refs_2_), channel_id=1, source_target_pairs={{0,8},{8,0},{16,24},{24,16},{1,9},{9,1},{17,25},{25,17},{2,10},{10... | collective-permute-start | bytes 786440 | tf_op jit(solution)/shard_map/ppermute | solution.py:28
  160.7 9.8 %collective-permute-start.29 = (f32[64,1024]{1,0:T(8,128)}, f32[64,1024]{1,0:T(8,128)}, u32[]{:S(2)}, u32[]{:S(2)}) collective-permute-start(f32[64,1024]{1,0:T(8,128)} %shard_map.158.refs_2_), channel_id=1, source_target_pairs={{0,16},{8,24},{16,0},{24,8},{1,17},{9,25},{17,1},{25,9},{2,18},{10... | collective-permute-start | bytes 786440 | tf_op jit(solution)/shard_map/ppermute | solution.py:28
  180.3 23.7 %collective-permute-start.33 = (bf16[128,2048]{1,0:T(8,128)(2,1)S(1)}, bf16[128,2048]{1,0:T(8,128)(2,1)S(1)}, u32[]{:S(2)}, u32[]{:S(2)}) collective-permute-start(bf16[128,2048]{1,0:T(8,128)(2,1)S(1)} %pad_maximum_fusion.3), channel_id=1, source_target_pairs={{0,16},{8,24},{16,0},{24,8},{1,17},{9,25},{17,1},{25,9},{2,18},{10... | collective-permute-start | bytes 1572872 | tf_op jit(solution)/shard_map/ppermute | solution.py:28
  181.3 22.7 %collective-permute-start.35 = (bf16[128,2048]{1,0:T(8,128)(2,1)S(1)}, bf16[128,2048]{1,0:T(8,128)(2,1)S(1)}, u32[]{:S(2)}, u32[]{:S(2)}) collective-permute-start(bf16[128,2048]{1,0:T(8,128)(2,1)S(1)} %pad_maximum_fusion.4), channel_id=1, source_target_pairs={{0,8},{8,0},{16,24},{24,16},{1,9},{9,1},{17,25},{25,17},{2,10},{10... | collective-permute-start | bytes 1572872 | tf_op jit(solution)/shard_map/ppermute | solution.py:28
  223.5 8.0 %collective-permute-start.50 = (bf16[1,256,512]{2,1,0:T(8,128)(2,1)S(1)}, bf16[1,256,512]{2,1,0:T(8,128)(2,1)S(1)}, u32[]{:S(2)}, u32[]{:S(2)}) collective-permute-start(bf16[1,256,512]{2,1,0:T(8,128)(2,1)S(1)} %get-tuple-element.58), channel_id=1, source_target_pairs={{0,1},{1,0},{2,3},{3,2},{4,5},{5,4},{6,7},{7,6},{8,9},{9,8},{10,11... | collective-permute-start | bytes 786440 | tf_op jit(solution)/shard_map/ppermute | solution.py:28
  230.2 12.5 %collective-permute-start.49 = (bf16[1,256,512]{2,1,0:T(8,128)(2,1)S(1)}, bf16[1,256,512]{2,1,0:T(8,128)(2,1)S(1)}, u32[]{:S(2)}, u32[]{:S(2)}) collective-permute-start(bf16[1,256,512]{2,1,0:T(8,128)(2,1)S(1)} %shard_map.169), channel_id=1, source_target_pairs={{0,2},{1,3},{2,0},{3,1},{4,6},{5,7},{6,4},{7,5},{8,10},{9,11},{10,... | collective-permute-start | bytes 786440 | tf_op jit(solution)/shard_map/ppermute | solution.py:28
  231.9 10.7 %collective-permute-start.52 = (bf16[1,256,512]{2,1,0:T(8,128)(2,1)S(1)}, bf16[1,256,512]{2,1,0:T(8,128)(2,1)S(1)}, u32[]{:S(2)}, u32[]{:S(2)}) collective-permute-start(bf16[1,256,512]{2,1,0:T(8,128)(2,1)S(1)} %shard_map.170), channel_id=1, source_target_pairs={{0,4},{1,5},{2,6},{3,7},{4,0},{5,1},{6,2},{7,3},{8,12},{9,13},{10,... | collective-permute-start | bytes 786440 | tf_op jit(solution)/shard_map/ppermute | solution.py:28
  243.1 13.5 %collective-permute-start.56 = (bf16[256,512]{1,0:T(8,128)(2,1)S(1)}, bf16[256,512]{1,0:T(8,128)(2,1)S(1)}, u32[]{:S(2)}, u32[]{:S(2)}) collective-permute-start(bf16[256,512]{1,0:T(8,128)(2,1)S(1)} %shard_map.171.refs_0_), channel_id=1, source_target_pairs={{0,4},{1,5},{2,6},{3,7},{4,0},{5,1},{6,2},{7,3},{8,12},{9,13},{10,... | collective-permute-start | bytes 786440 | tf_op jit(solution)/shard_map/ppermute | solution.py:28
  246.2 16.1 %collective-permute-start.54 = (bf16[256,512]{1,0:T(8,128)(2,1)S(1)}, bf16[256,512]{1,0:T(8,128)(2,1)S(1)}, u32[]{:S(2)}, u32[]{:S(2)}) collective-permute-start(bf16[256,512]{1,0:T(8,128)(2,1)S(1)} %shard_map.171.refs_0_), channel_id=1, source_target_pairs={{0,2},{1,3},{2,0},{3,1},{4,6},{5,7},{6,4},{7,5},{8,10},{9,11},{10,... | collective-permute-start | bytes 786440 | tf_op jit(solution)/shard_map/ppermute | solution.py:28
  261.5 9.5 %collective-permute-start.53 = (bf16[256,512]{1,0:T(8,128)(2,1)S(1)}, bf16[256,512]{1,0:T(8,128)(2,1)S(1)}, u32[]{:S(2)}, u32[]{:S(2)}) collective-permute-start(bf16[256,512]{1,0:T(8,128)(2,1)S(1)} %shard_map.171.refs_0_), channel_id=1, source_target_pairs={{0,1},{1,0},{2,3},{3,2},{4,5},{5,4},{6,7},{7,6},{8,9},{9,8},{10,11... | collective-permute-start | bytes 786440 | tf_op jit(solution)/shard_map/ppermute | solution.py:28
  262.3 8.7 %collective-permute-start.57 = (bf16[256,512]{1,0:T(8,128)(2,1)S(1)}, bf16[256,512]{1,0:T(8,128)(2,1)S(1)}, u32[]{:S(2)}, u32[]{:S(2)}) collective-permute-start(bf16[256,512]{1,0:T(8,128)(2,1)S(1)} %collective-permute-done.56.refs_4_), channel_id=1, source_target_pairs={{0,1},{1,0},{2,3},{3,2},{4,5},{5,4},{6,7},{7,6},{8,9},{9,8},{10,11... | collective-permute-start | bytes 786440 | tf_op jit(solution)/shard_map/ppermute | solution.py:28
  262.3 8.7 %collective-permute-start.55 = (bf16[256,512]{1,0:T(8,128)(2,1)S(1)}, bf16[256,512]{1,0:T(8,128)(2,1)S(1)}, u32[]{:S(2)}, u32[]{:S(2)}) collective-permute-start(bf16[256,512]{1,0:T(8,128)(2,1)S(1)} %collective-permute-done.54.refs_2_), channel_id=1, source_target_pairs={{0,1},{1,0},{2,3},{3,2},{4,5},{5,4},{6,7},{7,6},{8,9},{9,8},{10,11... | collective-permute-start | bytes 786440 | tf_op jit(solution)/shard_map/ppermute | solution.py:28
  (52 other events, 423.9 us)
